TPU v7x, 512 devices: a whole 4x8x8 slice. The times are simulated.
512 devices in a mesh: gx: 32 (over y_lo, z), gy: 16 (over x, y_hi, core).
Axes of the slice: x: 4, y: 8 (y_hi: 2, y_lo: 4; y = y_hi * 4 + y_lo), z: 8, core: 2. Of those that a mesh axis runs over, the one named last changes fastest.
Arguments:
- plume_field: float32 [32, 256, 256, 128], P(None, 'gx', 'gy'), may hold values from -6 to 6
- spectral_weight: bfloat16 [2, 2304, 48, 1024], P(None, 'gx', 'gy'), may hold values from -4 to 4, as said below
- point_weight: float32 [32, 32], replicated, may hold values from -1 to 1
- point_bias: float32 [32], replicated, may hold values from -3 to 3
Outputs:
- activated: float32 [32, 256, 256, 128], P(None, 'gx', 'gy')
Inputs may be any that keep to these rules, and one draw needn't show every extreme that they name: `spectral_weight`: Real-valued entries.
All inputs are finite; a program needn't handle non-finite values.
Results may differ from a plain program's by a relative error of at most 0.0003.
Values sent between devices are 32-bit elements; how exact they have to be, the bound alone decides.
No kernel may reach another device: no remote copies, remote signals or barrier semaphores. Data moves between devices by JAX's collectives and lax.ppermute only.
A program may use at most 128 MiB of HBM per device.

v0:
```python
from functools import partial
import math

import jax
import jax.numpy as jnp
from jax import lax
from jax.sharding import PartitionSpec as P

MX = 48
MY = 48
MZ = 48


def kept_frequency(indices, kept):
    return jnp.where(indices < kept // 2, indices, indices - kept)


def phase_table(frequencies, positions, length):
    product = frequencies[:, None] * positions[None, :] % length
    angles = 2.0 * math.pi / length * product.astype(jnp.float32)
    return (jnp.cos(angles), jnp.sin(angles))


def on_device(plume_field, spectral_weight, point_weight, point_bias):
    precise = lax.Precision.HIGHEST
    contract = partial(jnp.einsum, precision=precise)
    channels, x_local, y_local, z_cells = plume_field.shape
    y_groups = lax.axis_size("gy")
    x_cells = x_local * lax.axis_size("gx")
    y_cells = y_local * y_groups
    mode_rows = spectral_weight.shape[1]
    z_modes = spectral_weight.shape[2]
    z_freq = jnp.arange(MZ, dtype=jnp.int32)
    z_cosine, z_sine = phase_table(z_freq, jnp.arange(z_cells, dtype=jnp.int32), z_cells)
    z_table = jnp.stack([z_cosine, -z_sine], axis=1).reshape(2 * MZ, z_cells).T
    z_spectra = contract(
        "cpz,zm->mcp", plume_field.reshape(channels, x_local * y_local, z_cells), z_table
    )
    z_spectra = z_spectra.reshape(2 * MZ, channels, 1, x_local * y_local)
    pencils = lax.all_to_all(z_spectra, "gy", split_axis=0, concat_axis=2, tiled=True)
    pencils = pencils.reshape(z_modes, 2, channels, y_groups, x_local, y_local)
    pencil_real = pencils[:, 0]
    pencil_imag = pencils[:, 1]
    y_cosine, y_sine = phase_table(
        kept_frequency(jnp.arange(MY, dtype=jnp.int32), MY),
        jnp.arange(y_cells, dtype=jnp.int32),
        y_cells,
    )
    y_cosine = y_cosine.reshape(MY, y_groups, y_local)
    y_sine = y_sine.reshape(MY, y_groups, y_local)
    along_real = contract("bsy,kcsxy->xbkc", y_cosine, pencil_real) + contract(
        "bsy,kcsxy->xbkc", y_sine, pencil_imag
    )
    along_imag = contract("bsy,kcsxy->xbkc", y_cosine, pencil_imag) - contract(
        "bsy,kcsxy->xbkc", y_sine, pencil_real
    )
    x_positions = lax.axis_index("gx") * x_local + jnp.arange(x_local, dtype=jnp.int32)
    extent = lax.axis_size("gx") * mode_rows // MY + 2
    kx_freq = kept_frequency(jnp.arange(extent, dtype=jnp.int32), MX)
    cosine_table, sine_table = phase_table(kx_freq, x_positions, x_cells)
    term_real = contract("ax,xbkc->abkc", cosine_table, along_real) + contract(
        "ax,xbkc->abkc", sine_table, along_imag
    )
    term_imag = contract("ax,xbkc->abkc", cosine_table, along_imag) - contract(
        "ax,xbkc->abkc", sine_table, along_real
    )
    whole_terms = jnp.stack([term_real, term_imag], axis=3).reshape(extent * MY, -1)
    summed = lax.psum_scatter(
        lax.slice_in_dim(whole_terms, 0, lax.axis_size("gx") * mode_rows, axis=0),
        "gx",
        scatter_dimension=0,
        tiled=True,
    )
    modes = summed.reshape(mode_rows, z_modes, 2, channels)
    weights = spectral_weight.astype(jnp.float32).reshape(2, mode_rows, z_modes, channels, channels)
    mode_real = modes[:, :, 0]
    mode_imag = modes[:, :, 1]
    mixed_real = contract("rkc,rkco->rko", mode_real, weights[0]) - contract(
        "rkc,rkco->rko", mode_imag, weights[1]
    )
    mixed_imag = contract("rkc,rkco->rko", mode_real, weights[1]) + contract(
        "rkc,rkco->rko", mode_imag, weights[0]
    )
    mixed = jnp.stack([mixed_real, mixed_imag], axis=2).reshape(mode_rows, -1)
    zeros_start = jnp.zeros((x_local, MY, z_modes, channels), jnp.float32)
    shard_rows = lax.all_gather(mixed, "gx", axis=0, tiled=True)
    row_count = shard_rows.shape[0]
    extent = row_count // MY + 2
    padded = jnp.zeros((extent * MY, shard_rows.shape[1]), jnp.float32)
    padded = lax.dynamic_update_slice_in_dim(padded, shard_rows, jnp.int32(0), 0)
    padded = padded.reshape(extent, MY, z_modes, 2, channels)
    kx_freq = kept_frequency(jnp.arange(extent, dtype=jnp.int32), MX)
    cosine_table, sine_table = phase_table(kx_freq, x_positions, x_cells)
    part_real = padded[:, :, :, 0]
    part_imag = padded[:, :, :, 1]
    new_real = (
        zeros_start
        + contract("ax,abkc->xbkc", cosine_table, part_real)
        - contract("ax,abkc->xbkc", sine_table, part_imag)
    )
    new_imag = (
        zeros_start
        + contract("ax,abkc->xbkc", cosine_table, part_imag)
        + contract("ax,abkc->xbkc", sine_table, part_real)
    )
    back_real = contract("bsy,xbkc->kcsxy", y_cosine, new_real) - contract(
        "bsy,xbkc->kcsxy", y_sine, new_imag
    )
    back_imag = contract("bsy,xbkc->kcsxy", y_cosine, new_imag) + contract(
        "bsy,xbkc->kcsxy", y_sine, new_real
    )
    lines_back = jnp.stack([back_real, back_imag], axis=1).reshape(
        2 * z_modes, channels, y_groups, x_local * y_local
    )
    slabs = lax.all_to_all(lines_back, "gy", split_axis=2, concat_axis=0, tiled=True)
    z_weights = jnp.where(z_freq == 0, 1.0, 2.0).astype(jnp.float32) / (x_cells * y_cells * z_cells)
    inverse_table = jnp.stack(
        [z_cosine * z_weights[:, None], -z_sine * z_weights[:, None]], axis=1
    ).reshape(2 * MZ, z_cells)
    spectral = contract(
        "mcp,mz->cpz", slabs.reshape(2 * MZ, channels, x_local * y_local), inverse_table
    ).reshape(plume_field.shape)
    linear = jnp.einsum("co,cxyz->oxyz", point_weight, plume_field, precision=precise)
    return jax.nn.gelu(spectral + linear + point_bias[:, None, None, None], approximate=False)


def solution(mesh):
    return jax.shard_map(
        on_device,
        mesh=mesh,
        in_specs=(P(None, "gx", "gy", None), P(None, "gx", "gy", None), P(), P()),
        out_specs=P(None, "gx", "gy", None),
        check_vma=False,
    )
```

profile of v0, /device:TPU:8, one launch (start us, length us, event | category | flops | bytes accessed | tf_op | source)
XLA Modules:
  0.0 612.2 jit_solution(15523869329635615278)
XLA Ops:
  12.4 8.8 %all-to-all-start = ((f32[96,32,1,128]{3,1,2,0:T(8,128)}), f32[96,32,1,128]{3,1,2,0:T(8,128)}, u32[]{:S(2)}, u32[]{:S(2)}) async-start(f32[96,32,1,128]{3,1,2,0:T(8,128)} %copy.90), calls=%async_computation | async-start | bytes 3145728 | tf_op jit(solution)/shard_map/all_to_all | solution.py:40
  21.3 42.8 %all-to-all-done = f32[96,32,1,128]{3,1,2,0:T(8,128)} async-done(((f32[96,32,1,128]{3,1,2,0:T(8,128)}), f32[96,32,1,128]{3,1,2,0:T(8,128)}, u32[]{:S(2)}, u32[]{:S(2)}) %all-to-all-start) | async-done | bytes 1572896 | tf_op jit(solution)/shard_map/all_to_all | solution.py:40
  64.1 5.5 copy.91
  73.2 5.5 fusion.40
  78.7 5.5 fusion.41
  84.2 5.6 fusion.47
  89.8 5.5 fusion.45
  113.9 13.2 %copy.161 = f32[48,48,3,2,32]{4,3,2,1,0:T(2,128)} copy(f32[48,48,3,2,32]{0,1,4,2,3:T(8,128)} %pad_maximum_fusion.1) | data formatting | bytes 3538944
  127.1 7.9 %reshape.270 = f32[2304,192]{1,0:T(8,128)} reshape(f32[48,48,3,2,32]{4,3,2,1,0:T(2,128)} %copy.161) | data formatting | bytes 3538944
  139.6 145.4 %reduce-scatter.4.cloned.1.call-done = f32[72,192]{1,0:T(8,128)} async-done(((f32[2304,192]{1,0:T(8,128)}), f32[72,192]{1,0:T(8,128)}) %reduce-scatter.4.cloned.1.call-update) | async-done | bytes 55312
  288.7 156.1 %all-gather.2.cloned.1.call-done = f32[2304,192]{1,0:T(8,128)} async-done(((f32[72,192]{1,0:T(8,128)}), f32[2304,192]{1,0:T(8,128)}) %all-gather.2.cloned.1.call-update) | async-done | bytes 1769488 | tf_op jit(solution)/shard_map/all_gather | solution.py:86
  448.1 8.0 %reshape.273 = f32[50,48,3,2,32]{4,3,2,1,0:T(2,128)} reshape(f32[2400,192]{1,0:T(8,128)} %dynamic_update_slice.3) | data formatting | bytes 3686400 | tf_op jit(solution)/shard_map/reshape | solution.py:91
  456.1 10.0 %fusion.175 = (f32[50,48,3,1,32]{4,3,2,1,0:T(1,128)}, f32[50,48,3,1,32]{4,3,2,1,0:T(1,128)}) fusion(f32[50,48,3,2,32]{4,3,2,1,0:T(2,128)} %reshape.273), kind=kLoop, calls=%fused_computation.202 | loop fusion | bytes 3686400 | tf_op jit(solution)/shard_map/slice | solution.py:94
  466.1 11.7 %copy.170 = f32[50,48,3,1,32]{0,1,4,2,3:T(8,128)} copy(f32[50,48,3,1,32]{4,3,2,1,0:T(1,128)} %get-tuple-element.12) | data formatting | bytes 1843200
  477.8 8.7 %fusion.6 = f32[8,48,3,32]{1,0,3,2:T(8,128)S(1)} fusion(f32[50,48,3,1,32]{0,1,4,2,3:T(8,128)} %copy.170, s32[8]{0:T(128)S(1)} %iota_add_fusion, s32[50]{0:T(128)S(1)} %compare_select_fusion.1), kind=kOutput, calls=%fused_computation.13 | convolution fusion | flops 22124000 | bytes 1069288 | tf_op jit(solution)/shard_map/ax,abkc->xbkc/dot_general | solution.py:99
  486.5 6.9 %fusion.4 = f32[8,48,3,32]{1,0,3,2:T(8,128)S(1)} fusion(f32[50,48,3,1,32]{0,1,4,2,3:T(8,128)S(1)} %copy-done.2, s32[8]{0:T(128)S(1)} %iota_add_fusion, s32[50]{0:T(128)S(1)} %compare_select_fusion.1), kind=kOutput, calls=%fused_computation.11 | convolution fusion | flops 22124000 | bytes 1069288 | tf_op jit(solution)/shard_map/ax,abkc->xbkc/dot_general | solution.py:103
  493.3 11.9 %copy.169 = f32[50,48,3,1,32]{0,1,4,2,3:T(8,128)} copy(f32[50,48,3,1,32]{4,3,2,1,0:T(1,128)} %get-tuple-element.11) | data formatting | bytes 1843200
  505.2 8.5 %fusion.31 = f32[8,48,3,32,1]{1,0,3,2,4:T(8,128)S(1)} fusion(f32[8,48,3,32]{1,0,3,2:T(8,128)S(1)} %fusion.6, f32[50,48,3,1,32]{0,1,4,2,3:T(8,128)} %copy.169, s32[8]{0:T(128)S(1)} %iota_add_fusion, s32[50]{0:T(128)S(1)} %compare_select_fusion.1), kind=kOutput, calls=%fused_computation.52 | convolution fusion | flops 22160864 | bytes 1216744 | tf_op jit(solution)/shard_map/ax,abkc->xbkc/dot_general | solution.py:98
  516.9 6.9 %fusion.37 = f32[8,48,3,32,1]{1,0,3,2,4:T(8,128)S(1)} fusion(f32[8,48,3,32]{1,0,3,2:T(8,128)S(1)} %fusion.4, f32[50,48,3,1,32]{0,1,4,2,3:T(8,128)S(1)} %copy-done.1, s32[8]{0:T(128)S(1)} %iota_add_fusion, s32[50]{0:T(128)S(1)} %compare_select_fusion.1), kind=kOutput, calls=%fused_computation.54 | convolution fusion | flops 22160864 | bytes 1216744 | tf_op jit(solution)/shard_map/ax,abkc->xbkc/dot_general | solution.py:104
  538.0 5.5 copy.110
  543.5 6.8 %all-to-all-start.1 = ((f32[6,32,16,128]{3,1,0,2:T(8,128)}), f32[6,32,16,128]{3,1,0,2:T(8,128)}, u32[]{:S(2)}, u32[]{:S(2)}) async-start(f32[6,32,16,128]{3,1,0,2:T(8,128)} %copy.110), calls=%async_computation.1 | async-start | bytes 3145728 | tf_op jit(solution)/shard_map/all_to_all | solution.py:115
  550.6 4.3 fusion.15
  554.9 38.4 %all-to-all-done.1 = f32[6,32,16,128]{3,1,0,2:T(8,128)} async-done(((f32[6,32,16,128]{3,1,0,2:T(8,128)}), f32[6,32,16,128]{3,1,0,2:T(8,128)}, u32[]{:S(2)}, u32[]{:S(2)}) %all-to-all-start.1) | async-done | bytes 1572896 | tf_op jit(solution)/shard_map/all_to_all | solution.py:115
  596.1 9.0 %fusion.13 = f32[32,8,16,128]{3,2,1,0:T(8,128)} fusion(f32[32,8,16,128]{3,0,2,1:T(8,128)} %fusion.15, f32[32,8,16,96]{3,2,1,0:T(8,128)} %bitcast.177, f32[96,128,1,1]{1,0,3,2:T(8,128)S(1)} %bitcast.181, f32[32]{0:T(128)S(1)} %copy-done.4), kind=kOutput, calls=%fused_computation.22 | convolution fusion | flops 638582784 | bytes 5816448 | tf_op jit(solution)/shard_map/mcp,mz->cpz/dot_general | solution.py:120
  (51 shorter events, 59.9 us)
Async XLA Ops:
  6.5 1.6 copy-start
  12.4 51.7 %all-to-all-start = ((f32[96,32,1,128]{3,1,2,0:T(8,128)}), f32[96,32,1,128]{3,1,2,0:T(8,128)}, u32[]{:S(2)}, u32[]{:S(2)}) async-start(f32[96,32,1,128]{3,1,2,0:T(8,128)} %copy.90), calls=%async_computation | async-start | bytes 3145728 | tf_op jit(solution)/shard_map/all_to_all | solution.py:40
  21.2 263.8 %reduce-scatter.4.cloned.1.call-start = ((), (), s32[]{:S(2)}) async-start(), calls=%async_computation.4 | async-start | bytes 2433024
  135.0 309.8 %all-gather.2.cloned.1.call-start = ((), (), s32[]{:S(2)}) async-start(), calls=%async_computation.3 | async-start | bytes 2433024 | tf_op jit(solution)/shard_map/all_gather | solution.py:86
  477.8 8.7 %copy-start.2 = (f32[50,48,3,1,32]{0,1,4,2,3:T(8,128)S(1)}, f32[50,48,3,1,32]{0,1,4,2,3:T(8,128)}, u32[]{:S(2)}) copy-start(f32[50,48,3,1,32]{0,1,4,2,3:T(8,128)} %copy.170) | copy-start | bytes 2764804
  513.7 3.1 copy-start.1
  543.5 7.0 %copy-start.3 = (f32[32,32]{1,0:T(8,128)S(1)}, f32[32,32]{1,0:T(8,128)}, u32[]{:S(2)}) copy-start(f32[32,32]{1,0:T(8,128)} %param.6) | copy-start | bytes 12292
  543.5 49.8 %all-to-all-start.1 = ((f32[6,32,16,128]{3,1,0,2:T(8,128)}), f32[6,32,16,128]{3,1,0,2:T(8,128)}, u32[]{:S(2)}, u32[]{:S(2)}) async-start(f32[6,32,16,128]{3,1,0,2:T(8,128)} %copy.110), calls=%async_computation.1 | async-start | bytes 3145728 | tf_op jit(solution)/shard_map/all_to_all | solution.py:115
  554.9 41.2 %copy-start.4 = (f32[32]{0:T(128)S(1)}, f32[32]{0:T(128)}, u32[]{:S(2)}) copy-start(f32[32]{0:T(128)} %param.7) | copy-start | bytes 388
Sparse Core Ops, SparseCore 0:
  135.1 149.8 reduce-scatter.3
  288.8 155.9 all-gather.1
where the time goes:
time: 617 us; the launch traced here: 612 us
  waiting for transfers between devices  383 us (62%)
  matrix products  97.2 us (16%)
  local copies, waits for them, and re-layouts  96.8 us (16%)
  starting transfers between devices  15.7 us (3%)
  between operations  13.9 us (2%)
    all_gather x1, waiting for transfers between devices, on_device(): shard_rows = lax.all_gather(mixed, 'gx', axis=0, tiled=True)  156 us
    unnamed x3, waiting for transfers between devices  145 us
    unnamed x17, local copies, waits for them, and re-layouts  49.6 us
    all_to_all x1, waiting for transfers between devices, on_device(): lax.all_to_all(z_spectra, 'gy', split_axis=0, concat_axis=2, tiled=True)  42.8 us
    all_to_all x1, waiting for transfers between devices, on_device(): lax.all_to_all(lines_back, 'gy', split_axis=2, concat_axis=0, tiled=True)  38.4 us
  transfers between devices with their start and end apart: 4, of which 4 were waited for; matrix products, arithmetic and copies ran while one was open for 1% of the time, Pallas kernels for 0%

commit v1 on v0

v1 whole, which is shorter than its diff:
```python
import numpy as np

import jax
import jax.numpy as jnp
import ml_dtypes
from jax import lax
from jax.experimental import pallas as pl
from jax.experimental.pallas import tpu as pltpu
from jax.sharding import Mesh, PartitionSpec as P

F32 = jnp.float32
BF16 = jnp.bfloat16
GX = ("yl", "zz")
GY = ("px", "ph", "core")
C = 32
NX, NY, NZ = 256, 256, 128
M = 48
B = 64


def freq(i, kept=M):
    return np.where(i < kept // 2, i, i - kept)


def two(table):
    t = np.asarray(table, np.float32)
    hi = t.astype(ml_dtypes.bfloat16)
    lo = (t - hi.astype(np.float32)).astype(ml_dtypes.bfloat16)
    return hi, lo


def angle(f, pos, n):
    return 2.0 * np.pi * ((f * pos) % n) / n


def z_modes():
    d = np.arange(8)[:, None, None]
    h = np.arange(2)[None, :, None]
    k = np.arange(3)[None, None, :]
    return 3 * (4 * (d // 2) + 2 * h + d % 2) + k


def z_tables():
    g = z_modes().reshape(-1)
    th = angle(g[:, None], np.arange(NZ)[None, :], NZ)
    fwd = np.stack([np.cos(th), -np.sin(th)], axis=1).reshape(96, NZ)
    w = (np.where(g == 0, 1.0, 2.0) / (NX * NY * NZ))[:, None]
    inv = np.stack([np.cos(th) * w, -np.sin(th) * w], axis=1).reshape(96, NZ)
    return fwd, inv


def y_tables():
    f = freq(np.arange(M))
    d = np.arange(8)
    fwds, invs = [], []
    for h in range(2):
        pos = (64 * (d // 2) + 32 * h + 16 * (d % 2))[:, None] + np.arange(16)[None, :]
        th = angle(f[:, None], pos.reshape(1, -1), NY)
        cos, sin = np.zeros((B, 128)), np.zeros((B, 128))
        cos[:M], sin[:M] = np.cos(th), np.sin(th)
        fwds.append(np.block([[cos, sin], [-sin, cos]]))
        invs.append(np.block([[cos, sin], [-sin, cos]]).T)
    return np.stack(fwds), np.stack(invs)


def x_rows():
    gx = np.arange(32)
    first = 3 * (gx // 2) + gx % 2
    return np.stack([first, first + 1])


def x_tables():
    f = freq(x_rows().reshape(-1))
    th = angle(f[:, None], np.arange(NX)[None, :], NX)
    fwd = np.concatenate([np.cos(th), np.sin(th)])
    inv = np.concatenate([np.cos(th), np.sin(th)]).T
    return fwd, inv


def split(v):
    hi = v.astype(BF16)
    return hi, (v - hi.astype(F32)).astype(BF16)


def dot(a, b, dims=((1,), (0,))):
    return lax.dot_general(a, b, (dims, ((), ())), preferred_element_type=F32)


def dot3(a, b, dims=((1,), (0,))):
    return dot(a[0], b[0], dims) + dot(a[0], b[1], dims) + dot(a[1], b[0], dims)


NT = ((1,), (1,))


def z_kernel(field, t_hi, t_lo, out):
    t = (t_hi[...], t_lo[...])
    for y in range(16):
        a = split(field[pl.ds(y, 256, stride=16), :])
        r = dot3(t, a, NT)
        for half in range(2):
            out[pl.ds(half * 16 + y, 96, stride=32), :] = r[:, half * 128 : half * 128 + 128]


def y_kernel(rows, t_hi, t_lo, out):
    t = (t_hi[...], t_lo[...])
    for j in range(6):
        b = jnp.concatenate(
            [
                jnp.concatenate([rows[:, j, ri, half].reshape(128, 128) for ri in range(2)], axis=0)
                for half in range(2)
            ],
            axis=1,
        )
        r = dot3(t, split(b))
        h, k = j // 3, j % 3
        out[h * 32 : h * 32 + 32, k] = r.T.reshape(32, 8, 128)


def turn(v):
    rolled = pltpu.roll(v, B, 1)
    lane = lax.broadcasted_iota(jnp.int32, v.shape, 1)
    return jnp.where(lane < B, rolled, -rolled)


def x_kernel(rows, t_hi, t_lo, out):
    t = (t_hi[...], t_lo[...])
    zero = jnp.zeros((32, 128), F32)
    for k in range(3):
        s = (rows[0:32, k] + rows[32:64, k]).reshape(256, 128)
        r = dot3(t, split(s))
        m = r[:64] + turn(r[64:])
        for a in range(2):
            out[pl.ds(2 * k + a, 32, stride=8), :] = m[32 * a : 32 * a + 32]
    for a in range(6, 8):
        out[pl.ds(a, 32, stride=8), :] = zero


def mix_kernel(par, modes, w, expand, out, in_re, in_im, mid_re, mid_im):
    zero96 = jnp.zeros((96, 32), F32)
    start = pl.multiple_of(par[0] * 24, 8)
    e = expand[...]
    for k in range(3):
        for a in range(2):
            v = modes[pl.ds(2 * k + a, 32, stride=8), :].T
            in_re[k, a * 48 : a * 48 + 48, :] = v[:48]
            in_im[k, a * 48 : a * 48 + 48, :] = v[B : B + 48]
        mid_re[k] = zero96
        mid_im[k] = zero96
    for k in range(3):
        v = jnp.concatenate([in_re[k, pl.ds(start, 72), :], in_im[k, pl.ds(start, 72), :]], axis=0)
        hi, lo = split(v)
        wide = dot(hi, e) + dot(lo, e)
        re, im = wide[:72], wide[72:]
        w_re, w_im = w[0, k].astype(F32), w[1, k].astype(F32)
        for part, ref in ((re * w_re - im * w_im, mid_re), (re * w_im + im * w_re, mid_im)):
            s = part[:, 0:128]
            for i in range(1, 8):
                s = s + part[:, 128 * i : 128 * i + 128]
            s = s + pltpu.roll(s, 64, 1)
            s = s + pltpu.roll(s, 32, 1)
            ref[k, pl.ds(start, 72), :] = s[:, :32]
    pad = jnp.zeros((B - M, 32), F32)
    for k in range(3):
        for a in range(2):
            rows = slice(a * 48, a * 48 + 48)
            v = jnp.concatenate([mid_re[k, rows, :], pad, mid_im[k, rows, :], pad], axis=0)
            out[pl.ds(2 * k + a, 32, stride=8), :] = v.T
    for a in range(6, 8):
        out[pl.ds(a, 32, stride=8), :] = jnp.zeros((32, 128), F32)


def x_back_kernel(modes, t_hi, t_lo, out):
    t = (t_hi[...], t_lo[...])
    for k in range(3):
        v = jnp.concatenate([modes[pl.ds(2 * k + a, 32, stride=8), :] for a in range(2)], axis=0)
        r = dot3(t, split(jnp.concatenate([v, -turn(v)], axis=0))).reshape(32, 8, 128)
        out[0:32, k] = r
        out[32:64, k] = r


def y_back_kernel(rows, t_hi, t_lo, out):
    t = (t_hi[...], t_lo[...])
    for j in range(6):
        h, k = j // 3, j % 3
        v = rows[h * 32 : h * 32 + 32, k].reshape(256, 128)
        r = dot3(t, split(v), NT)
        for ri in range(2):
            for half in range(2):
                part = r[ri * 128 : ri * 128 + 128, half * 128 : half * 128 + 128]
                out[:, j, ri, half] = part.reshape(8, 16, 128)


def erf(x):
    return lax.erf(x)


def z_back_kernel(rows, field, t_hi, t_lo, mixing, bias, out):
    t = (t_hi[...], t_lo[...])
    kron = split(mixing[...])
    b = bias[...]
    for y in range(16):
        v = jnp.concatenate(
            [rows[pl.ds(half * 16 + y, 96, stride=32), :] for half in range(2)], axis=1
        ).T
        a = split(field[pl.ds(y, 256, stride=16), :])
        s = dot3(split(v), t) + dot3(kron, a) + b
        out[pl.ds(y, 256, stride=16), :] = 0.5 * s * (1.0 + erf(s * np.float32(np.sqrt(0.5))))


PARAMS = pltpu.CompilerParams(vmem_limit_bytes=40 * 1024 * 1024)


def call(kernel, shape, *operands, scratch=(), smem=0):
    specs = [
        pl.BlockSpec(memory_space=pltpu.SMEM if i < smem else pltpu.VMEM) for i in range(len(operands))
    ]
    return pl.pallas_call(
        kernel,
        out_shape=jax.ShapeDtypeStruct(shape, F32),
        in_specs=specs,
        out_specs=pl.BlockSpec(memory_space=pltpu.VMEM),
        scratch_shapes=list(scratch),
        compiler_params=PARAMS,
    )(*operands)


def exchange(v, axes):
    return lax.all_to_all(v, axes, 0, 0, tiled=True)


def on_device(field, weight, point_weight, point_bias):
    z_fwd, z_inv = z_tables()
    y_fwd, y_inv = y_tables()
    x_fwd, x_inv = x_tables()
    half = lax.axis_index("ph")
    pick = lambda table: [lax.dynamic_index_in_dim(jnp.asarray(t), half, 0, False) for t in two(table)]
    lines = field.reshape(C * 8 * 16, NZ)

    v = call(z_kernel, (3072, 128), lines, *two(z_fwd))
    v = exchange(v.reshape(8, 12, 2, 16, 128), ("px", "core"))
    v = call(y_kernel, (64, 3, 8, 128), v.reshape(8, 6, 2, 2, 16, 128), *pick(y_fwd))
    v = exchange(v, ("ph",) + GX)
    v = call(x_kernel, (256, 128), v, *two(x_fwd))
    v = exchange(v.reshape(32, 8, 128), GX)

    par = (lax.axis_index("zz") % 2).astype(jnp.int32).reshape(1)
    expand = np.kron(np.eye(C), np.ones((1, C))).astype(ml_dtypes.bfloat16)
    v = call(
        mix_kernel,
        (256, 128),
        par,
        v.reshape(256, 128),
        weight.transpose(0, 2, 1, 3),
        expand,
        scratch=[pltpu.VMEM((3, 96, 32), F32) for _ in range(4)],
        smem=1,
    )

    v = exchange(v.reshape(32, 8, 128), GX)
    v = call(x_back_kernel, (64, 3, 8, 128), v.reshape(256, 128), *two(x_inv))
    v = exchange(v, ("ph",) + GX)
    v = call(y_back_kernel, (8, 6, 2, 2, 16, 128), v, *pick(y_inv))
    v = exchange(v.reshape(8, 12, 2, 16, 128), ("px", "core"))
    kron = jnp.kron(point_weight.T, jnp.eye(8, dtype=F32))
    bias = jnp.broadcast_to(point_bias[:, None, None], (C, 8, 128)).reshape(256, 128)
    out = call(z_back_kernel, (4096, 128), v.reshape(3072, 128), lines, *two(z_inv), kron, bias)
    return out.reshape(C, 8, 16, NZ)


def solution(mesh):
    shape = (4, 8, 4, 2, 2)
    fine = Mesh(mesh.devices.reshape(shape), GX + GY)
    spec = P(None, GX, GY, None)
    return jax.shard_map(
        on_device,
        mesh=fine,
        in_specs=(spec, spec, P(), P()),
        out_specs=spec,
        check_vma=False,
    )
```

time: 617 us -> 169 us (0.27)
  the two profiles are of different devices: /device:TPU:8 before, /device:TPU:1 now
where the time goes in v1:
time: 169 us
  waiting for transfers between devices  63 us (37%)
  blocking collectives  44.8 us (27%)
  starting transfers between devices  34.5 us (20%)
  Pallas kernels  15.9 us (9%)
  local copies, waits for them, and re-layouts  7.67 us (5%)
  other arithmetic  2.56 us (2%)
    all_to_all x4, waiting for transfers between devices, exchange(): return lax.all_to_all(v, axes, 0, 0, tiled=True)  63 us
    all_to_all x2, blocking collectives, exchange(): return lax.all_to_all(v, axes, 0, 0, tiled=True)  44.8 us
    all_to_all x4, starting transfers between devices, exchange(): return lax.all_to_all(v, axes, 0, 0, tiled=True)  34.5 us
    pallas_call x7, Pallas kernels, call(): pl.pallas_call(kernel, out_shape=jax.ShapeDtypeStruct(shape, F32), in_spe...  15.9 us
    mul x1, local copies, waits for them, and re-layouts, on_device(): kron = jnp.kron(point_weight.T, jnp.eye(8, dtype=F32))  4.18 us
  transfers between devices with their start and end apart: 4, of which 4 were waited for; matrix products, arithmetic and copies ran while one was open for 4% of the time, Pallas kernels for 0%

profile of v1, /device:TPU:1, one launch (start us, length us, event | category | flops | bytes accessed | tf_op | source)
XLA Modules:
  0.0 168.6 jit_solution(1365883074644191468)
XLA Ops:
  0.0 1.6 copy-done
  1.6 0.7 copy-done.10
  2.3 0.7 copy-done.11
  3.1 3.0 %shard_map.163 = f32[3072,128]{1,0:T(8,128)} custom-call(f32[4096,128]{1,0:T(8,128)S(1)} %bitcast.23, bf16[96,128]{1,0:T(8,128)(2,1)S(1)} %copy-done.10, bf16[96,128]{1,0:T(8,128)(2,1)S(1)} %copy-done.11), custom_call_target="tpu_custom_call" | custom-call | tf_op jit(solution)/shard_map/pallas_call | solution.py:218
  6.1 10.5 %all-to-all-start = ((f32[8,12,2,16,128]{4,3,2,1,0:T(8,128)}), f32[8,12,2,16,128]{4,3,2,1,0:T(8,128)S(1)}, u32[]{:S(2)}, u32[]{:S(2)}) async-start(f32[8,12,2,16,128]{4,3,2,1,0:T(8,128)} %bitcast.2), calls=%async_computation | async-start | bytes 3145728 | tf_op jit(solution)/shard_map/all_to_all | solution.py:229
  16.6 20.7 %all-to-all-done = f32[8,12,2,16,128]{4,3,2,1,0:T(8,128)S(1)} async-done(((f32[8,12,2,16,128]{4,3,2,1,0:T(8,128)}), f32[8,12,2,16,128]{4,3,2,1,0:T(8,128)S(1)}, u32[]{:S(2)}, u32[]{:S(2)}) %all-to-all-start) | async-done | bytes 1572896 | tf_op jit(solution)/shard_map/all_to_all | solution.py:229
  37.3 0.6 shard_map.164
  37.9 32.4 %all_to_all.30.rows = f32[64,3,8,128]{3,2,1,0:T(8,128)S(1)} all-to-all(f32[64,3,8,128]{3,2,1,0:T(8,128)S(1)} %shard_map.164), channel_id=1, replica_groups=mesh['yl'=4,'zz'=8,'px'=4,'ph'=2,'core'=2] {'ph','yl','zz'}, dimensions={0} | all-to-all | bytes 1572864 | tf_op jit(solution)/shard_map/all_to_all | solution.py:229
  70.3 1.0 shard_map.165
  71.4 7.8 %all-to-all-start.2 = ((f32[32,8,128]{2,1,0:T(8,128)}), f32[32,8,128]{2,1,0:T(8,128)S(1)}, u32[]{:S(2)}, u32[]{:S(2)}) async-start(f32[32,8,128]{2,1,0:T(8,128)} %bitcast.6), calls=%async_computation.2 | async-start | bytes 262144 | tf_op jit(solution)/shard_map/all_to_all | solution.py:229
  79.2 9.3 %all-to-all-done.2 = f32[32,8,128]{2,1,0:T(8,128)S(1)} async-done(((f32[32,8,128]{2,1,0:T(8,128)}), f32[32,8,128]{2,1,0:T(8,128)S(1)}, u32[]{:S(2)}, u32[]{:S(2)}) %all-to-all-start.2) | async-done | bytes 131104 | tf_op jit(solution)/shard_map/all_to_all | solution.py:229
  88.5 1.2 shard_map.166
  89.7 12.4 %all_to_all.31 = f32[32,8,128]{2,1,0:T(8,128)S(1)} all-to-all(f32[32,8,128]{2,1,0:T(8,128)S(1)} %bitcast.28), channel_id=1, replica_groups=mesh['yl'=4,'zz'=8,'px'=4,'ph'=2,'core'=2] {'yl','zz'}, dimensions={0} | all-to-all | bytes 262144 | tf_op jit(solution)/shard_map/all_to_all | solution.py:229
  102.1 1.3 shard_map.167
  103.4 5.9 %all-to-all-start.4 = ((f32[64,3,8,128]{3,2,1,0:T(8,128)}), f32[64,3,8,128]{3,2,1,0:T(8,128)S(1)}, u32[]{:S(2)}, u32[]{:S(2)}) async-start(f32[64,3,8,128]{3,2,1,0:T(8,128)} %shard_map.167), calls=%async_computation.4 | async-start | bytes 1572864 | tf_op jit(solution)/shard_map/all_to_all | solution.py:229
  109.3 19.1 %all-to-all-done.4.rows = f32[64,3,8,128]{3,2,1,0:T(8,128)S(1)} async-done(((f32[64,3,8,128]{3,2,1,0:T(8,128)}), f32[64,3,8,128]{3,2,1,0:T(8,128)S(1)}, u32[]{:S(2)}, u32[]{:S(2)}) %all-to-all-start.4) | async-done | bytes 786464 | tf_op jit(solution)/shard_map/all_to_all | solution.py:229
  128.4 1.9 %shard_map.168 = f32[8,6,2,2,16,128]{5,4,3,2,1,0:T(8,128)} custom-call(f32[64,3,8,128]{3,2,1,0:T(8,128)S(1)} %all-to-all-done.4.rows, bf16[256,128]{1,0:T(8,128)(2,1)S(1)} %get-tuple-element.6.t_hi, bf16[256,128]{1,0:T(8,128)(2,1)S(1)} %get-tuple-element.5.t_lo), custom_call_target="tpu_custom_call" | custom-call | tf_op jit(solution)/shard_map/pallas_call | solution.py:218
  130.4 10.4 %all-to-all-start.5 = ((f32[8,12,2,16,128]{4,3,2,1,0:T(8,128)}), f32[8,12,2,16,128]{4,3,2,1,0:T(8,128)}, u32[]{:S(2)}, u32[]{:S(2)}) async-start(f32[8,12,2,16,128]{4,3,2,1,0:T(8,128)} %bitcast.13), calls=%async_computation.5 | async-start | bytes 3145728 | tf_op jit(solution)/shard_map/all_to_all | solution.py:229
  140.9 2.6 %broadcast_multiply_fusion = f32[32,8,32,8]{3,2,1,0:T(8,128)} fusion(f32[8,8]{1,0:T(8,128)S(1)} %fusion, f32[32,32]{1,0:T(8,128)S(1)} %copy.19), kind=kLoop, calls=%fused_computation | loop fusion | flops 65536 | bytes 266496 | tf_op jit(solution)/shard_map/jit(kron)/mul | solution.py:265
  143.4 4.2 %mul.27.mixing = f32[256,256]{1,0:T(8,128)S(1)} reshape(f32[32,8,32,8]{3,2,1,0:T(8,128)} %broadcast_multiply_fusion) | data formatting | bytes 524288 | tf_op jit(solution)/shard_map/jit(kron)/mul | solution.py:265
  147.7 0.1 broadcast_in_dim.15
  147.8 13.8 %all-to-all-done.5 = f32[8,12,2,16,128]{4,3,2,1,0:T(8,128)} async-done(((f32[8,12,2,16,128]{4,3,2,1,0:T(8,128)}), f32[8,12,2,16,128]{4,3,2,1,0:T(8,128)}, u32[]{:S(2)}, u32[]{:S(2)}) %all-to-all-start.5) | async-done | bytes 1572896 | tf_op jit(solution)/shard_map/all_to_all | solution.py:229
  161.6 0.1 broadcast_in_dim.16.bias
  161.7 6.9 %shard_map.169 = f32[4096,128]{1,0:T(8,128)} custom-call(f32[3072,128]{1,0:T(8,128)} %bitcast.14.rows, f32[4096,128]{1,0:T(8,128)S(1)} %bitcast.24, bf16[96,128]{1,0:T(8,128)(2,1)S(1)} %copy-done.8, bf16[96,128]{1,0:T(8,128)(2,1)S(1)} %copy-done.9, f32[256,256]{1,0:T(8,128)S(1)} %mul.27.mixing, f32[256,128]{1,0:T(8,128)S(1)} %broadcast_in_dim.16.bias), custom_call_target="tpu_custom_call" | custom-call | tf_op jit(solution)/shard_map/pallas_call | solution.py:218
  (38 shorter events, 0.3 us)
Async XLA Ops:
  0.0 1.6 copy-start
  1.6 0.7 copy-start.10
  2.3 0.7 copy-start.11
  6.1 10.5 %copy-start.14 = (bf16[2,128,256]{2,1,0:T(8,128)(2,1)S(1)}, bf16[2,128,256]{2,1,0:T(8,128)(2,1)}, u32[]{:S(2)}) copy-start(bf16[2,128,256]{2,1,0:T(8,128)(2,1)} %constant.63.clone) | copy-start | bytes 393220
  6.1 10.5 %copy-start.15 = (bf16[2,128,256]{2,1,0:T(8,128)(2,1)S(1)}, bf16[2,128,256]{2,1,0:T(8,128)(2,1)}, u32[]{:S(2)}) copy-start(bf16[2,128,256]{2,1,0:T(8,128)(2,1)} %constant.64.clone) | copy-start | bytes 393220
  6.1 31.2 %all-to-all-start = ((f32[8,12,2,16,128]{4,3,2,1,0:T(8,128)}), f32[8,12,2,16,128]{4,3,2,1,0:T(8,128)S(1)}, u32[]{:S(2)}, u32[]{:S(2)}) async-start(f32[8,12,2,16,128]{4,3,2,1,0:T(8,128)} %bitcast.2), calls=%async_computation | async-start | bytes 3145728 | tf_op jit(solution)/shard_map/all_to_all | solution.py:229
  16.6 53.8 %copy-start.6 = (bf16[128,256]{1,0:T(8,128)(2,1)S(1)}, bf16[128,256]{1,0:T(8,128)(2,1)}, u32[]{:S(2)}) copy-start(bf16[128,256]{1,0:T(8,128)(2,1)} %constant.65.clone.t_hi) | copy-start | bytes 196612
  16.6 53.7 %copy-start.7 = (bf16[128,256]{1,0:T(8,128)(2,1)S(1)}, bf16[128,256]{1,0:T(8,128)(2,1)}, u32[]{:S(2)}) copy-start(bf16[128,256]{1,0:T(8,128)(2,1)} %constant.66.clone.t_lo) | copy-start | bytes 196612
  37.3 51.2 %copy-start.2 = (bf16[2,72,3,1024]{3,1,2,0:T(8,128)(2,1)S(1)}, bf16[2,72,3,1024]{3,1,2,0:T(8,128)(2,1)}, u32[]{:S(2)}) copy-start(bf16[2,72,3,1024]{3,1,2,0:T(8,128)(2,1)} %param.18) | copy-start | bytes 2654212
  37.3 51.2 %copy-start.5 = (bf16[32,1024]{1,0:T(8,128)(2,1)S(1)}, bf16[32,1024]{1,0:T(8,128)(2,1)}, u32[]{:S(2)}) copy-start(bf16[32,1024]{1,0:T(8,128)(2,1)} %constant.67.clone.expand) | copy-start | bytes 196612
  37.9 64.2 %copy-start.3 = (bf16[256,128]{1,0:T(8,128)(2,1)S(1)}, bf16[256,128]{1,0:T(8,128)(2,1)}, u32[]{:S(2)}) copy-start(bf16[256,128]{1,0:T(8,128)(2,1)} %constant.68.clone.t_hi) | copy-start | bytes 196612
  37.9 64.2 %copy-start.4 = (bf16[256,128]{1,0:T(8,128)(2,1)S(1)}, bf16[256,128]{1,0:T(8,128)(2,1)}, u32[]{:S(2)}) copy-start(bf16[256,128]{1,0:T(8,128)(2,1)} %constant.69.clone.t_lo) | copy-start | bytes 196612
  71.4 17.1 %all-to-all-start.2 = ((f32[32,8,128]{2,1,0:T(8,128)}), f32[32,8,128]{2,1,0:T(8,128)S(1)}, u32[]{:S(2)}, u32[]{:S(2)}) async-start(f32[32,8,128]{2,1,0:T(8,128)} %bitcast.6), calls=%async_computation.2 | async-start | bytes 262144 | tf_op jit(solution)/shard_map/all_to_all | solution.py:229
  79.2 30.1 %copy-start.12 = (bf16[2,256,128]{2,1,0:T(8,128)(2,1)S(1)}, bf16[2,256,128]{2,1,0:T(8,128)(2,1)}, u32[]{:S(2)}) copy-start(bf16[2,256,128]{2,1,0:T(8,128)(2,1)} %constant.70.clone) | copy-start | bytes 393220
  79.2 30.1 %copy-start.13 = (bf16[2,256,128]{2,1,0:T(8,128)(2,1)S(1)}, bf16[2,256,128]{2,1,0:T(8,128)(2,1)}, u32[]{:S(2)}) copy-start(bf16[2,256,128]{2,1,0:T(8,128)(2,1)} %constant.71.clone) | copy-start | bytes 393220
  103.4 25.0 %all-to-all-start.4 = ((f32[64,3,8,128]{3,2,1,0:T(8,128)}), f32[64,3,8,128]{3,2,1,0:T(8,128)S(1)}, u32[]{:S(2)}, u32[]{:S(2)}) async-start(f32[64,3,8,128]{3,2,1,0:T(8,128)} %shard_map.167), calls=%async_computation.4 | async-start | bytes 1572864 | tf_op jit(solution)/shard_map/all_to_all | solution.py:229
  130.4 10.4 %copy-start.16 = (f32[32,32]{1,0:T(8,128)S(1)}, f32[32,32]{1,0:T(8,128)}, u32[]{:S(2)}) copy-start(f32[32,32]{1,0:T(8,128)} %param.19) | copy-start | bytes 12292
  130.4 31.2 %all-to-all-start.5 = ((f32[8,12,2,16,128]{4,3,2,1,0:T(8,128)}), f32[8,12,2,16,128]{4,3,2,1,0:T(8,128)}, u32[]{:S(2)}, u32[]{:S(2)}) async-start(f32[8,12,2,16,128]{4,3,2,1,0:T(8,128)} %bitcast.13), calls=%async_computation.5 | async-start | bytes 3145728 | tf_op jit(solution)/shard_map/all_to_all | solution.py:229
  143.4 4.2 %copy-start.17 = (f32[32]{0:T(128)S(1)}, f32[32]{0:T(128)}, u32[]{:S(2)}) copy-start(f32[32]{0:T(128)} %param.20) | copy-start | bytes 388
  143.4 18.3 %copy-start.1 = (f32[32,8,16,128]{3,2,1,0:T(8,128)S(1)}, f32[32,8,16,128]{3,2,1,0:T(8,128)}, u32[]{:S(2)}) copy-start(f32[32,8,16,128]{3,2,1,0:T(8,128)} %param.17) | copy-start | bytes 6291460
  143.4 18.3 %copy-start.8 = (bf16[96,128]{1,0:T(8,128)(2,1)S(1)}, bf16[96,128]{1,0:T(8,128)(2,1)}, u32[]{:S(2)}) copy-start(bf16[96,128]{1,0:T(8,128)(2,1)} %constant.72.clone.t_hi) | copy-start | bytes 73732
  143.4 18.3 %copy-start.9 = (bf16[96,128]{1,0:T(8,128)(2,1)S(1)}, bf16[96,128]{1,0:T(8,128)(2,1)}, u32[]{:S(2)}) copy-start(bf16[96,128]{1,0:T(8,128)(2,1)} %constant.73.clone.t_lo) | copy-start | bytes 73732

commit v2 on v1

v2 whole, which is shorter than its diff:
```python
import numpy as np

import jax
import jax.numpy as jnp
import ml_dtypes
from jax import lax
from jax.experimental import pallas as pl
from jax.experimental.pallas import tpu as pltpu
from jax.sharding import Mesh, PartitionSpec as P

F32 = jnp.float32
BF16 = jnp.bfloat16
GX = ("yl", "zz")
GY = ("px", "ph", "core")
C = 32
NX, NY, NZ = 256, 256, 128
M = 48
B = 64


def freq(i, kept=M):
    return np.where(i < kept // 2, i, i - kept)


def two(table):
    t = np.asarray(table, np.float32)
    hi = t.astype(ml_dtypes.bfloat16)
    lo = (t - hi.astype(np.float32)).astype(ml_dtypes.bfloat16)
    return np.stack([hi, lo])


def angle(f, pos, n):
    return 2.0 * np.pi * ((f * pos) % n) / n


def z_modes():
    d = np.arange(8)[:, None, None]
    h = np.arange(2)[None, :, None]
    k = np.arange(3)[None, None, :]
    return 3 * (4 * (d // 2) + 2 * h + d % 2) + k


def z_tables():
    g = z_modes().reshape(-1)
    th = angle(g[:, None], np.arange(NZ)[None, :], NZ)
    fwd = np.stack([np.cos(th), -np.sin(th)], axis=1).reshape(96, NZ)
    w = (np.where(g == 0, 1.0, 2.0) / (NX * NY * NZ))[:, None]
    inv = np.stack([np.cos(th) * w, -np.sin(th) * w], axis=1).reshape(96, NZ)
    return fwd, inv


def y_tables():
    f = freq(np.arange(M))
    d = np.arange(8)
    fwds, invs = [], []
    for h in range(2):
        pos = (64 * (d // 2) + 32 * h + 16 * (d % 2))[:, None] + np.arange(16)[None, :]
        th = angle(f[:, None], pos.reshape(1, -1), NY)
        cos, sin = np.zeros((B, 128)), np.zeros((B, 128))
        cos[:M], sin[:M] = np.cos(th), np.sin(th)
        fwds.append(np.block([[cos, sin], [-sin, cos]]))
        invs.append(np.block([[cos, sin], [-sin, cos]]).T)
    return np.stack(fwds), np.stack(invs)


def x_rows():
    gx = np.arange(32)
    first = 3 * (gx // 2) + gx % 2
    return np.stack([first, first + 1])


def x_tables():
    f = freq(x_rows().reshape(-1))
    pos = (8 * np.arange(32)[None, :] + np.arange(8)[:, None]).reshape(-1)
    th = angle(f[:, None], pos[None, :], NX)
    fwd = np.concatenate([np.cos(th), np.sin(th)])
    inv = np.concatenate([np.cos(th), np.sin(th)]).T
    return fwd, inv


def split(v):
    hi = v.astype(BF16)
    return hi, (v - hi.astype(F32)).astype(BF16)


def dot(a, b, dims=((1,), (0,))):
    return lax.dot_general(a, b, (dims, ((), ())), preferred_element_type=F32)


def dot3(a, b, dims=((1,), (0,))):
    return dot(a[0], b[0], dims) + dot(a[0], b[1], dims) + dot(a[1], b[0], dims)


NT = ((1,), (1,))


def lines_at(ref, y):
    return jnp.concatenate([ref[pl.ds(x * 16 + y, 32, stride=128), :] for x in range(8)], axis=0)


def z_kernel(field, table, out):
    t = (table[0], table[1])
    for y in range(16):
        r = dot3(t, split(lines_at(field, y)), NT)
        for half in range(2):
            out[pl.ds(half * 16 + y, 96, stride=32), :] = r[:, half * 128 : half * 128 + 128]


def y_kernel(rows, table, out):
    t = (table[0], table[1])
    for h in range(2):
        r = []
        for k in range(3):
            j = 3 * h + k
            b = jnp.concatenate(
                [
                    jnp.concatenate([rows[:, j, ri, half].reshape(128, 128) for ri in range(2)], axis=0)
                    for half in range(2)
                ],
                axis=1,
            )
            r.append(dot3(t, split(b)))
        for k in range(2):
            v = jnp.concatenate([r[k][:48], r[2][16 * k : 16 * k + 16], r[k][64:112], r[2][64 + 16 * k : 80 + 16 * k]], axis=0)
            v = v.T
            for x in range(8):
                out[pl.ds(h * 576 + k * 8 + x, 32, stride=18), :] = v[32 * x : 32 * x + 32]
        for xh in range(2):
            v = jnp.concatenate(
                [
                    r[2][64 * ri + 32 : 64 * ri + 48, 32 * x : 32 * x + 32]
                    for ri in range(2)
                    for x in range(4 * xh, 4 * xh + 4)
                ],
                axis=0,
            )
            out[pl.ds(h * 576 + 16 + xh, 32, stride=18), :] = v.T


def turn(v):
    rolled = pltpu.roll(v, B, 1)
    lane = lax.broadcasted_iota(jnp.int32, v.shape, 1)
    return jnp.where(lane < B, rolled, -rolled)


def x_kernel(rows, table, out):
    t = (table[0], table[1])
    at = lambda r: rows[pl.ds(r, 32, stride=18), :] + rows[pl.ds(576 + r, 32, stride=18), :]
    last = [at(16), at(17)]
    for k in range(3):
        if k < 2:
            s = [at(8 * k + x) for x in range(8)]
        else:
            s = [pltpu.roll(last[x // 4], (128 - 16 * (x % 4)) % 128, 1) for x in range(8)]
        r = dot3(t, split(jnp.concatenate(s, axis=0)))
        m = r[:64] + turn(r[64:])
        for a in range(2):
            out[pl.ds(2 * k + a, 32, stride=8), :] = m[32 * a : 32 * a + 32]
    for a in range(6, 8):
        out[pl.ds(a, 32, stride=8), :] = jnp.zeros((32, 128), F32)


def mix_kernel(par, modes, w, expand, out, in_re, in_im, mid_re, mid_im):
    start = pl.multiple_of(par[0] * 24, 8)
    e = expand[...]
    for a in range(2):
        v = [modes[pl.ds(2 * k + a, 32, stride=8), :].T for k in range(3)]
        for ref, o in ((in_re, 0), (in_im, B)):
            for k in range(2):
                ref[k, a * 48 : a * 48 + 48, :] = v[k][o : o + 48]
                ref[2, a * 48 + 16 * k : a * 48 + 16 * k + 16, :] = v[k][o + 48 : o + 64]
            ref[2, a * 48 + 32 : a * 48 + 48, :] = v[2][o : o + 16]
    for k in range(3):
        mid_re[k] = jnp.zeros((96, 32), F32)
        mid_im[k] = jnp.zeros((96, 32), F32)
    for k in range(3):
        v = jnp.concatenate([in_re[k, pl.ds(start, 72), :], in_im[k, pl.ds(start, 72), :]], axis=0)
        hi, lo = split(v)
        wide = dot(hi, e) + dot(lo, e)
        re, im = wide[:72], wide[72:]
        w_re, w_im = w[0, k].astype(F32), w[1, k].astype(F32)
        for part, ref in ((re * w_re - im * w_im, mid_re), (re * w_im + im * w_re, mid_im)):
            s = part[:, 0:128]
            for i in range(1, 8):
                s = s + part[:, 128 * i : 128 * i + 128]
            s = s + pltpu.roll(s, 64, 1)
            s = s + pltpu.roll(s, 32, 1)
            ref[k, pl.ds(start, 72), :] = s[:, :32]
    pad = jnp.zeros((B - 16, 32), F32)
    for a in range(2):
        for k in range(3):
            v = []
            for ref in (mid_re, mid_im):
                if k < 2:
                    v += [ref[k, a * 48 : a * 48 + 48, :], ref[2, a * 48 + 16 * k : a * 48 + 16 * k + 16, :]]
                else:
                    v += [ref[2, a * 48 + 32 : a * 48 + 48, :], pad]
            out[pl.ds(2 * k + a, 32, stride=8), :] = jnp.concatenate(v, axis=0).T
    for a in range(6, 8):
        out[pl.ds(a, 32, stride=8), :] = jnp.zeros((32, 128), F32)


def x_back_kernel(modes, table, out):
    t = (table[0], table[1])
    lane = lax.broadcasted_iota(jnp.int32, (32, 128), 1) % B
    for k in range(3):
        v = jnp.concatenate([modes[pl.ds(2 * k + a, 32, stride=8), :] for a in range(2)], axis=0)
        r = dot3(t, split(jnp.concatenate([v, -turn(v)], axis=0)))
        s = [r[32 * x : 32 * x + 32] for x in range(8)]
        if k == 2:
            packed = []
            for xh in range(2):
                v = s[4 * xh]
                for i in range(1, 4):
                    v = jnp.where(lane < 16 * i, v, pltpu.roll(s[4 * xh + i], 16 * i, 1))
                packed.append(v)
            s = packed
        for x in range(len(s)):
            for h in range(2):
                out[pl.ds(h * 576 + k * 8 + x, 32, stride=18), :] = s[x]


def y_back_kernel(rows, table, out):
    t = (table[0], table[1])
    lane = lax.broadcasted_iota(jnp.int32, (256, 128), 1) % B
    for h in range(2):
        at = lambda r: rows[pl.ds(h * 576 + r, 32, stride=18), :]
        v = [jnp.concatenate([at(8 * k + x) for x in range(8)], axis=0) for k in range(2)]
        last = [at(16), at(17)]
        v.append(
            jnp.concatenate([pltpu.roll(last[x // 4], (160 - 16 * (x % 4)) % 128, 1) for x in range(8)], axis=0)
        )
        v[2] = jnp.where(lane < 16, pltpu.roll(v[0], 80, 1), jnp.where(lane < 32, pltpu.roll(v[1], 96, 1), v[2]))
        for k in range(3):
            r = dot3(t, split(v[k]), NT)
            for ri in range(2):
                for half in range(2):
                    part = r[ri * 128 : ri * 128 + 128, half * 128 : half * 128 + 128]
                    out[:, 3 * h + k, ri, half] = part.reshape(8, 16, 128)


def point_kernel(field, weight, bias, out):
    w = jnp.concatenate([jnp.concatenate([weight[...]] * 8, axis=1)] * 8, axis=0)
    row = lax.broadcasted_iota(jnp.int32, (256, 256), 0) // 32
    col = lax.broadcasted_iota(jnp.int32, (256, 256), 1) // 32
    w = split(jnp.where(row == col, w, 0.0))
    b = jnp.concatenate([bias[...]] * 8, axis=0)
    for y in range(16):
        out[256 * y : 256 * y + 256, :] = dot3(w, split(lines_at(field, y))) + b


def z_back_kernel(rows, linear, table, out):
    t = (table[0], table[1])
    for y in range(16):
        v = jnp.concatenate(
            [rows[pl.ds(half * 16 + y, 96, stride=32), :] for half in range(2)], axis=1
        ).T
        s = dot3(split(v), t) + linear[256 * y : 256 * y + 256, :]
        s = 0.5 * s * (1.0 + lax.erf(s * np.float32(np.sqrt(0.5))))
        for x in range(8):
            out[pl.ds(x * 16 + y, 32, stride=128), :] = s[32 * x : 32 * x + 32]


PARAMS = pltpu.CompilerParams(vmem_limit_bytes=40 * 1024 * 1024)


def call(kernel, shape, *operands, scratch=(), smem=0, cost=None):
    specs = [
        pl.BlockSpec(memory_space=pltpu.SMEM if i < smem else pltpu.VMEM) for i in range(len(operands))
    ]
    return pl.pallas_call(
        kernel,
        out_shape=jax.ShapeDtypeStruct(shape, F32),
        in_specs=specs,
        out_specs=pl.BlockSpec(memory_space=pltpu.VMEM),
        scratch_shapes=list(scratch),
        compiler_params=PARAMS,
        cost_estimate=cost,
    )(*operands)


def exchange(v, axes):
    return lax.all_to_all(v, axes, 0, 0, tiled=True)


def on_device(field, weight, point_weight, point_bias):
    z_fwd, z_inv = z_tables()
    y_fwd, y_inv = y_tables()
    x_fwd, x_inv = x_tables()
    half = lax.axis_index("ph")
    pick = lambda table: lax.dynamic_index_in_dim(jnp.asarray(two(table)), half, 1, False)
    lines = field.reshape(C * 8 * 16, NZ)

    v = call(z_kernel, (3072, 128), lines, two(z_fwd))
    v = exchange(v.reshape(8, 12, 2, 16, 128), ("px", "core"))
    v = call(y_kernel, (1152, 128), v.reshape(8, 6, 2, 2, 16, 128), pick(y_fwd))
    v = exchange(v.reshape(64, 9, 2, 128), ("ph",) + GX)
    v = call(x_kernel, (256, 128), v.reshape(1152, 128), two(x_fwd))
    v = exchange(v.reshape(32, 8, 128), GX)

    par = (lax.axis_index("zz") % 2).astype(jnp.int32).reshape(1)
    expand = np.kron(np.eye(C), np.ones((1, C))).astype(ml_dtypes.bfloat16)
    v = call(
        mix_kernel,
        (256, 128),
        par,
        v.reshape(256, 128),
        weight.transpose(0, 2, 1, 3),
        expand,
        scratch=[pltpu.VMEM((3, 96, 32), F32) for _ in range(4)],
        smem=1,
    )

    v = exchange(v.reshape(32, 8, 128), GX)
    v = call(x_back_kernel, (1152, 128), v.reshape(256, 128), two(x_inv))
    v = exchange(v.reshape(64, 9, 2, 128), ("ph",) + GX)
    v = call(y_back_kernel, (8, 6, 2, 2, 16, 128), v.reshape(1152, 128), pick(y_inv))
    v = exchange(v.reshape(8, 12, 2, 16, 128), ("px", "core"))
    bias = jnp.broadcast_to(point_bias[:, None], (C, NZ))
    cost = pl.CostEstimate(flops=800_000_000, bytes_accessed=4 << 20, transcendentals=0)
    linear = call(point_kernel, (4096, 128), lines, point_weight.T, bias, cost=cost)
    out = call(z_back_kernel, (4096, 128), v.reshape(3072, 128), linear, two(z_inv))
    return out.reshape(C, 8, 16, NZ)


def solution(mesh):
    shape = (4, 8, 4, 2, 2)
    fine = Mesh(mesh.devices.reshape(shape), GX + GY)
    spec = P(None, GX, GY, None)
    return jax.shard_map(
        on_device,
        mesh=fine,
        in_specs=(spec, spec, P(), P()),
        out_specs=spec,
        check_vma=False,
    )
```

time: 169 us -> 161 us (0.953)
  blocking collectives: 44.8 us -> 41.3 us
  other arithmetic: 2.56 us -> 0 us
    mul x1 -> x0, local copies, waits for them, and re-layouts: 4.18 us -> none  [on_device(): kron = jnp.kron(point_weight.T, jnp.eye(8, dtype=F32))]
    all_to_all x2, blocking collectives: 44.8 us -> 41.3 us  [exchange(): return lax.all_to_all(v, axes, 0, 0, tiled=True)]
    unnamed x36 -> x31, local copies, waits for them, and re-layouts: 3.14 us -> 6.54 us
    mul x1 -> x0, other arithmetic: 2.55 us -> none  [on_device(): kron = jnp.kron(point_weight.T, jnp.eye(8, dtype=F32))]
    pallas_call x7 -> x8, Pallas kernels: 15.9 us -> 16.6 us  [call(): pl.pallas_call(kernel, out_shape=jax.ShapeDtypeStruct(shape, F32), in_spe...]
  transfers between devices with their start and end apart: 4 -> 4, of which waited for: 4 -> 4; matrix products, arithmetic and copies ran while one was open for 4% -> 0% of each run, Pallas kernels for 0% -> 2%
where the time goes in v2:
time: 161 us
  waiting for transfers between devices  61.9 us (38%)
  blocking collectives  41.3 us (26%)
  starting transfers between devices  34.3 us (21%)
  Pallas kernels  16.6 us (10%)
  local copies, waits for them, and re-layouts  6.64 us (4%)
    all_to_all x4, waiting for transfers between devices, exchange(): return lax.all_to_all(v, axes, 0, 0, tiled=True)  61.9 us
    all_to_all x2, blocking collectives, exchange(): return lax.all_to_all(v, axes, 0, 0, tiled=True)  41.3 us
    all_to_all x4, starting transfers between devices, exchange(): return lax.all_to_all(v, axes, 0, 0, tiled=True)  34.3 us
    pallas_call x8, Pallas kernels, call(): pl.pallas_call(kernel, out_shape=jax.ShapeDtypeStruct(shape, F32), in_spe...  16.6 us
    unnamed x31, local copies, waits for them, and re-layouts  6.54 us
  transfers between devices with their start and end apart: 4, of which 4 were waited for; matrix products, arithmetic and copies ran while one was open for 0% of the time, Pallas kernels for 2%

profile of v2, /device:TPU:1, one launch (start us, length us, event | category | flops | bytes accessed | tf_op | source)
XLA Modules:
  0.0 160.8 jit_solution(15117851329857555723)
XLA Ops:
  0.0 1.6 copy-done
  1.6 0.8 copy-done.10
  2.4 3.5 %shard_map.109 = f32[3072,128]{1,0:T(8,128)} custom-call(f32[4096,128]{1,0:T(8,128)S(1)} %bitcast.21, bf16[2,96,128]{2,1,0:T(8,128)(2,1)S(1)} %copy-done.10), custom_call_target="tpu_custom_call" | custom-call | tf_op jit(solution)/shard_map/pallas_call | solution.py:271
  5.9 10.5 %all-to-all-start = ((f32[8,12,2,16,128]{4,3,2,1,0:T(8,128)}), f32[8,12,2,16,128]{4,3,2,1,0:T(8,128)S(1)}, u32[]{:S(2)}, u32[]{:S(2)}) async-start(f32[8,12,2,16,128]{4,3,2,1,0:T(8,128)} %bitcast.2), calls=%async_computation | async-start | bytes 3145728 | tf_op jit(solution)/shard_map/all_to_all | solution.py:283
  16.4 20.7 %all-to-all-done = f32[8,12,2,16,128]{4,3,2,1,0:T(8,128)S(1)} async-done(((f32[8,12,2,16,128]{4,3,2,1,0:T(8,128)}), f32[8,12,2,16,128]{4,3,2,1,0:T(8,128)S(1)}, u32[]{:S(2)}, u32[]{:S(2)}) %all-to-all-start) | async-done | bytes 1572896 | tf_op jit(solution)/shard_map/all_to_all | solution.py:283
  37.2 0.8 shard_map.110
  38.0 28.9 %all_to_all.30 = f32[64,9,2,128]{3,2,1,0:T(2,128)S(1)} all-to-all(f32[64,9,2,128]{3,2,1,0:T(2,128)S(1)} %bitcast.26), channel_id=1, replica_groups=mesh['yl'=4,'zz'=8,'px'=4,'ph'=2,'core'=2] {'ph','yl','zz'}, dimensions={0} | all-to-all | bytes 1179648 | tf_op jit(solution)/shard_map/all_to_all | solution.py:283
  66.9 1.1 shard_map.111
  67.9 7.1 %all-to-all-start.2 = ((f32[32,8,128]{2,1,0:T(8,128)}), f32[32,8,128]{2,1,0:T(8,128)S(1)}, u32[]{:S(2)}, u32[]{:S(2)}) async-start(f32[32,8,128]{2,1,0:T(8,128)} %bitcast.7), calls=%async_computation.2 | async-start | bytes 262144 | tf_op jit(solution)/shard_map/all_to_all | solution.py:283
  75.0 9.3 %all-to-all-done.2 = f32[32,8,128]{2,1,0:T(8,128)S(1)} async-done(((f32[32,8,128]{2,1,0:T(8,128)}), f32[32,8,128]{2,1,0:T(8,128)S(1)}, u32[]{:S(2)}, u32[]{:S(2)}) %all-to-all-start.2) | async-done | bytes 131104 | tf_op jit(solution)/shard_map/all_to_all | solution.py:283
  84.4 1.2 shard_map.112
  85.6 12.4 %all_to_all.31 = f32[32,8,128]{2,1,0:T(8,128)S(1)} all-to-all(f32[32,8,128]{2,1,0:T(8,128)S(1)} %bitcast.30), channel_id=1, replica_groups=mesh['yl'=4,'zz'=8,'px'=4,'ph'=2,'core'=2] {'yl','zz'}, dimensions={0} | all-to-all | bytes 262144 | tf_op jit(solution)/shard_map/all_to_all | solution.py:283
  98.0 1.3 shard_map.113
  99.2 5.7 %all-to-all-start.4 = ((f32[64,9,2,128]{3,2,1,0:T(2,128)}), f32[64,9,2,128]{3,2,1,0:T(2,128)S(1)}, u32[]{:S(2)}, u32[]{:S(2)}) async-start(f32[64,9,2,128]{3,2,1,0:T(2,128)} %bitcast.12), calls=%async_computation.4 | async-start | bytes 1179648 | tf_op jit(solution)/shard_map/all_to_all | solution.py:283
  105.0 15.0 %all-to-all-done.4 = f32[64,9,2,128]{3,2,1,0:T(2,128)S(1)} async-done(((f32[64,9,2,128]{3,2,1,0:T(2,128)}), f32[64,9,2,128]{3,2,1,0:T(2,128)S(1)}, u32[]{:S(2)}, u32[]{:S(2)}) %all-to-all-start.4) | async-done | bytes 589856 | tf_op jit(solution)/shard_map/all_to_all | solution.py:283
  120.0 0.8 shard_map.114
  120.9 1.1 copy-done.4
  122.0 10.9 %all-to-all-start.5 = ((f32[8,12,2,16,128]{4,3,2,1,0:T(8,128)}), f32[8,12,2,16,128]{4,3,2,1,0:T(8,128)}, u32[]{:S(2)}, u32[]{:S(2)}) async-start(f32[8,12,2,16,128]{4,3,2,1,0:T(8,128)} %bitcast.24), calls=%async_computation.5 | async-start | bytes 3145728 | tf_op jit(solution)/shard_map/all_to_all | solution.py:283
  132.9 0.1 copy.12
  133.1 2.5 %shard_map.115.linear = f32[4096,128]{1,0:T(8,128)S(1)} custom-call(f32[4096,128]{1,0:T(8,128)S(1)} %bitcast.22, f32[32,32]{1,0:T(8,128)S(1)} %bitcast.32, f32[32,128]{1,0:T(8,128)S(1)} %broadcast_in_dim.2.bias), custom_call_target="tpu_custom_call" | custom-call | flops 800000000 | bytes 4194304 | tf_op jit(solution)/shard_map/pallas_call | solution.py:271
  135.6 1.3 copy-done.2
  136.9 16.8 %all-to-all-done.5 = f32[8,12,2,16,128]{4,3,2,1,0:T(8,128)} async-done(((f32[8,12,2,16,128]{4,3,2,1,0:T(8,128)}), f32[8,12,2,16,128]{4,3,2,1,0:T(8,128)}, u32[]{:S(2)}, u32[]{:S(2)}) %all-to-all-start.5) | async-done | bytes 1572896 | tf_op jit(solution)/shard_map/all_to_all | solution.py:283
  153.7 1.6 copy-done.3
  155.3 5.5 %shard_map.116 = f32[4096,128]{1,0:T(8,128)} custom-call(f32[3072,128]{1,0:T(8,128)} %bitcast.16.rows, f32[4096,128]{1,0:T(8,128)S(1)} %copy-done.3, bf16[2,96,128]{2,1,0:T(8,128)(2,1)S(1)} %copy-done.9), custom_call_target="tpu_custom_call" | custom-call | tf_op jit(solution)/shard_map/pallas_call | solution.py:271
  (28 shorter events, 0.2 us)
Async XLA Ops:
  0.0 1.6 copy-start
  1.6 0.8 copy-start.10
  5.9 10.5 %copy-start.12 = (bf16[2,2,128,256]{3,2,0,1:T(8,128)(2,1)S(1)}, bf16[2,2,128,256]{3,2,0,1:T(8,128)(2,1)}, u32[]{:S(2)}) copy-start(bf16[2,2,128,256]{3,2,0,1:T(8,128)(2,1)} %constant.46.clone) | copy-start | bytes 786436
  5.9 31.2 %all-to-all-start = ((f32[8,12,2,16,128]{4,3,2,1,0:T(8,128)}), f32[8,12,2,16,128]{4,3,2,1,0:T(8,128)S(1)}, u32[]{:S(2)}, u32[]{:S(2)}) async-start(f32[8,12,2,16,128]{4,3,2,1,0:T(8,128)} %bitcast.2), calls=%async_computation | async-start | bytes 3145728 | tf_op jit(solution)/shard_map/all_to_all | solution.py:283
  37.2 29.7 %copy-start.7 = (bf16[2,128,256]{2,1,0:T(8,128)(2,1)S(1)}, bf16[2,128,256]{2,1,0:T(8,128)(2,1)}, u32[]{:S(2)}) copy-start(bf16[2,128,256]{2,1,0:T(8,128)(2,1)} %constant.47.clone.table) | copy-start | bytes 393220
  38.0 46.4 %copy-start.5 = (bf16[2,72,3,1024]{3,1,2,0:T(8,128)(2,1)S(1)}, bf16[2,72,3,1024]{3,1,2,0:T(8,128)(2,1)}, u32[]{:S(2)}) copy-start(bf16[2,72,3,1024]{3,1,2,0:T(8,128)(2,1)} %param.12) | copy-start | bytes 2654212
  38.0 46.4 %copy-start.8 = (bf16[32,1024]{1,0:T(8,128)(2,1)S(1)}, bf16[32,1024]{1,0:T(8,128)(2,1)}, u32[]{:S(2)}) copy-start(bf16[32,1024]{1,0:T(8,128)(2,1)} %constant.48.clone.expand) | copy-start | bytes 196612
  66.9 31.1 %copy-start.6 = (bf16[2,256,128]{2,1,0:T(8,128)(2,1)S(1)}, bf16[2,256,128]{2,1,0:T(8,128)(2,1)}, u32[]{:S(2)}) copy-start(bf16[2,256,128]{2,1,0:T(8,128)(2,1)} %constant.49.clone.table) | copy-start | bytes 393220
  67.9 16.5 %all-to-all-start.2 = ((f32[32,8,128]{2,1,0:T(8,128)}), f32[32,8,128]{2,1,0:T(8,128)S(1)}, u32[]{:S(2)}, u32[]{:S(2)}) async-start(f32[32,8,128]{2,1,0:T(8,128)} %bitcast.7), calls=%async_computation.2 | async-start | bytes 262144 | tf_op jit(solution)/shard_map/all_to_all | solution.py:283
  84.4 20.6 %copy-start.11 = (bf16[2,2,256,128]{3,2,0,1:T(8,128)(2,1)S(1)}, bf16[2,2,256,128]{3,2,0,1:T(8,128)(2,1)}, u32[]{:S(2)}) copy-start(bf16[2,2,256,128]{3,2,0,1:T(8,128)(2,1)} %constant.50.clone) | copy-start | bytes 786436
  99.2 20.8 %all-to-all-start.4 = ((f32[64,9,2,128]{3,2,1,0:T(2,128)}), f32[64,9,2,128]{3,2,1,0:T(2,128)S(1)}, u32[]{:S(2)}, u32[]{:S(2)}) async-start(f32[64,9,2,128]{3,2,1,0:T(2,128)} %bitcast.12), calls=%async_computation.4 | async-start | bytes 1179648 | tf_op jit(solution)/shard_map/all_to_all | solution.py:283
  120.8 1.1 copy-start.4
  122.0 10.9 %copy-start.13 = (f32[32,32]{1,0:T(8,128)S(1)}, f32[32,32]{1,0:T(8,128)}, u32[]{:S(2)}) copy-start(f32[32,32]{1,0:T(8,128)} %param.13) | copy-start | bytes 12292
  122.0 11.0 %copy-start.14 = (f32[32]{0:T(128)S(1)}, f32[32]{0:T(128)}, u32[]{:S(2)}) copy-start(f32[32]{0:T(128)} %param.14) | copy-start | bytes 388
  122.0 11.1 %copy-start.1 = (f32[32,8,16,128]{3,2,1,0:T(8,128)S(1)}, f32[32,8,16,128]{3,2,1,0:T(8,128)}, u32[]{:S(2)}) copy-start(f32[32,8,16,128]{3,2,1,0:T(8,128)} %param.11) | copy-start | bytes 6291460
  122.0 31.8 %all-to-all-start.5 = ((f32[8,12,2,16,128]{4,3,2,1,0:T(8,128)}), f32[8,12,2,16,128]{4,3,2,1,0:T(8,128)}, u32[]{:S(2)}, u32[]{:S(2)}) async-start(f32[8,12,2,16,128]{4,3,2,1,0:T(8,128)} %bitcast.24), calls=%async_computation.5 | async-start | bytes 3145728 | tf_op jit(solution)/shard_map/all_to_all | solution.py:283
  133.0 20.7 %copy-start.9 = (bf16[2,96,128]{2,1,0:T(8,128)(2,1)S(1)}, bf16[2,96,128]{2,1,0:T(8,128)(2,1)}, u32[]{:S(2)}) copy-start(bf16[2,96,128]{2,1,0:T(8,128)(2,1)} %constant.51.clone.table) | copy-start | bytes 147460
  135.6 1.3 copy-start.2
  153.7 1.6 copy-start.3

commit v3 on v2

--- a/solution.py
+++ b/solution.py
@@ -15,6 +15,7 @@
 C = 32
 NX, NY, NZ = 256, 256, 128
 M = 48
+GX_OF = 8 * (np.arange(32) % 4) + np.arange(32) // 4
 B = 64
 
 
@@ -37,7 +38,7 @@
     d = np.arange(8)[:, None, None]
     h = np.arange(2)[None, :, None]
     k = np.arange(3)[None, None, :]
-    return 3 * (4 * (d // 2) + 2 * h + d % 2) + k
+    return 3 * (4 * (d % 4) + 2 * h + d // 4) + k
 
 
 def z_tables():
@@ -54,7 +55,7 @@
     d = np.arange(8)
     fwds, invs = [], []
     for h in range(2):
-        pos = (64 * (d // 2) + 32 * h + 16 * (d % 2))[:, None] + np.arange(16)[None, :]
+        pos = (64 * (d % 4) + 32 * h + 16 * (d // 4))[:, None] + np.arange(16)[None, :]
         th = angle(f[:, None], pos.reshape(1, -1), NY)
         cos, sin = np.zeros((B, 128)), np.zeros((B, 128))
         cos[:M], sin[:M] = np.cos(th), np.sin(th)
@@ -64,7 +65,7 @@
 
 
 def x_rows():
-    gx = np.arange(32)
+    gx = GX_OF
     first = 3 * (gx // 2) + gx % 2
     return np.stack([first, first + 1])
 
@@ -94,16 +95,18 @@
 NT = ((1,), (1,))
 
 
-def lines_at(ref, y):
-    return jnp.concatenate([ref[pl.ds(x * 16 + y, 32, stride=128), :] for x in range(8)], axis=0)
+def lines_at(ref, y, ys=16):
+    return jnp.concatenate([ref[pl.ds(x * ys + y, 32, stride=8 * ys), :] for x in range(8)], axis=0)
 
 
 def z_kernel(field, table, out):
     t = (table[0], table[1])
-    for y in range(16):
-        r = dot3(t, split(lines_at(field, y)), NT)
+    field = field.reshape(2048, 128)
+    out = out.reshape(1536, 128)
+    for y in range(8):
+        r = dot3(t, split(lines_at(field, y, 8)), NT)
         for half in range(2):
-            out[pl.ds(half * 16 + y, 96, stride=32), :] = r[:, half * 128 : half * 128 + 128]
+            out[pl.ds(half * 8 + y, 96, stride=16), :] = r[:, half * 128 : half * 128 + 128]
 
 
 def y_kernel(rows, table, out):
@@ -124,7 +127,7 @@
             v = jnp.concatenate([r[k][:48], r[2][16 * k : 16 * k + 16], r[k][64:112], r[2][64 + 16 * k : 80 + 16 * k]], axis=0)
             v = v.T
             for x in range(8):
-                out[pl.ds(h * 576 + k * 8 + x, 32, stride=18), :] = v[32 * x : 32 * x + 32]
+                out[pl.ds(h * 18 + k * 8 + x, 32, stride=36), :] = v[32 * x : 32 * x + 32]
         for xh in range(2):
             v = jnp.concatenate(
                 [
@@ -134,7 +137,7 @@
                 ],
                 axis=0,
             )
-            out[pl.ds(h * 576 + 16 + xh, 32, stride=18), :] = v.T
+            out[pl.ds(h * 18 + 16 + xh, 32, stride=36), :] = v.T
 
 
 def turn(v):
@@ -145,7 +148,7 @@
 
 def x_kernel(rows, table, out):
     t = (table[0], table[1])
-    at = lambda r: rows[pl.ds(r, 32, stride=18), :] + rows[pl.ds(576 + r, 32, stride=18), :]
+    at = lambda r: rows[pl.ds(r, 32, stride=36), :] + rows[pl.ds(18 + r, 32, stride=36), :]
     last = [at(16), at(17)]
     for k in range(3):
         if k < 2:
@@ -195,7 +198,9 @@
                     v += [ref[k, a * 48 : a * 48 + 48, :], ref[2, a * 48 + 16 * k : a * 48 + 16 * k + 16, :]]
                 else:
                     v += [ref[2, a * 48 + 32 : a * 48 + 48, :], pad]
-            out[pl.ds(2 * k + a, 32, stride=8), :] = jnp.concatenate(v, axis=0).T
+            v = jnp.concatenate(v, axis=0).T
+            for yl in range(4):
+                out[pl.ds(8 * yl + 2 * k + a, 8, stride=32), :] = v[8 * yl : 8 * yl + 8]
     for a in range(6, 8):
         out[pl.ds(a, 32, stride=8), :] = jnp.zeros((32, 128), F32)
 
@@ -217,14 +222,14 @@
             s = packed
         for x in range(len(s)):
             for h in range(2):
-                out[pl.ds(h * 576 + k * 8 + x, 32, stride=18), :] = s[x]
+                out[pl.ds(h * 18 + k * 8 + x, 32, stride=36), :] = s[x]
 
 
 def y_back_kernel(rows, table, out):
     t = (table[0], table[1])
     lane = lax.broadcasted_iota(jnp.int32, (256, 128), 1) % B
     for h in range(2):
-        at = lambda r: rows[pl.ds(h * 576 + r, 32, stride=18), :]
+        at = lambda r: rows[pl.ds(h * 18 + r, 32, stride=36), :]
         v = [jnp.concatenate([at(8 * k + x) for x in range(8)], axis=0) for k in range(2)]
         last = [at(16), at(17)]
         v.append(
@@ -251,14 +256,16 @@
 
 def z_back_kernel(rows, linear, table, out):
     t = (table[0], table[1])
-    for y in range(16):
+    rows = rows.reshape(1536, 128)
+    out = out.reshape(2048, 128)
+    for y in range(8):
         v = jnp.concatenate(
-            [rows[pl.ds(half * 16 + y, 96, stride=32), :] for half in range(2)], axis=1
+            [rows[pl.ds(half * 8 + y, 96, stride=16), :] for half in range(2)], axis=1
         ).T
         s = dot3(split(v), t) + linear[256 * y : 256 * y + 256, :]
         s = 0.5 * s * (1.0 + lax.erf(s * np.float32(np.sqrt(0.5))))
         for x in range(8):
-            out[pl.ds(x * 16 + y, 32, stride=128), :] = s[32 * x : 32 * x + 32]
+            out[pl.ds(x * 8 + y, 32, stride=64), :] = s[32 * x : 32 * x + 32]
 
 
 PARAMS = pltpu.CompilerParams(vmem_limit_bytes=40 * 1024 * 1024)
@@ -279,6 +286,24 @@
     )(*operands)
 
 
+def halves(kernel, shape, *operands):
+    def spec(dims):
+        if len(dims) == 3 and dims[1] == 16:
+            return pl.BlockSpec((dims[0], 8, dims[2]), lambda i: (0, i, 0))
+        if dims == (4096, 128):
+            return pl.BlockSpec((2048, 128), lambda i: (i, 0))
+        return pl.BlockSpec(dims, lambda i: (0,) * len(dims))
+
+    return pl.pallas_call(
+        kernel,
+        grid=(2,),
+        out_shape=jax.ShapeDtypeStruct(shape, F32),
+        in_specs=[spec(v.shape) for v in operands],
+        out_specs=spec(shape),
+        compiler_params=pltpu.CompilerParams(vmem_limit_bytes=60 * 1024 * 1024),
+    )(*operands)
+
+
 def exchange(v, axes):
     return lax.all_to_all(v, axes, 0, 0, tiled=True)
 
@@ -291,15 +316,15 @@
     pick = lambda table: lax.dynamic_index_in_dim(jnp.asarray(two(table)), half, 1, False)
     lines = field.reshape(C * 8 * 16, NZ)
 
-    v = call(z_kernel, (3072, 128), lines, two(z_fwd))
-    v = exchange(v.reshape(8, 12, 2, 16, 128), ("px", "core"))
+    v = halves(z_kernel, (192, 16, 128), field.reshape(256, 16, 128), two(z_fwd))
+    v = exchange(v.reshape(8, 12, 2, 16, 128), ("core", "px"))
     v = call(y_kernel, (1152, 128), v.reshape(8, 6, 2, 2, 16, 128), pick(y_fwd))
-    v = exchange(v.reshape(64, 9, 2, 128), ("ph",) + GX)
+    v = exchange(v.reshape(64, 9, 2, 128), GX + ("ph",))
     v = call(x_kernel, (256, 128), v.reshape(1152, 128), two(x_fwd))
-    v = exchange(v.reshape(32, 8, 128), GX)
+    v = exchange(v.reshape(32, 8, 128), ("zz", "yl"))
 
     par = (lax.axis_index("zz") % 2).astype(jnp.int32).reshape(1)
-    expand = np.kron(np.eye(C), np.ones((1, C))).astype(ml_dtypes.bfloat16)
+    expand = np.kron(np.eye(C)[GX_OF], np.ones((1, C))).astype(ml_dtypes.bfloat16)
     v = call(
         mix_kernel,
         (256, 128),
@@ -311,15 +336,15 @@
         smem=1,
     )
 
-    v = exchange(v.reshape(32, 8, 128), GX)
+    v = exchange(v.reshape(32, 8, 128), ("zz", "yl"))
     v = call(x_back_kernel, (1152, 128), v.reshape(256, 128), two(x_inv))
-    v = exchange(v.reshape(64, 9, 2, 128), ("ph",) + GX)
+    v = exchange(v.reshape(64, 9, 2, 128), GX + ("ph",))
     v = call(y_back_kernel, (8, 6, 2, 2, 16, 128), v.reshape(1152, 128), pick(y_inv))
-    v = exchange(v.reshape(8, 12, 2, 16, 128), ("px", "core"))
+    v = exchange(v.reshape(8, 12, 2, 16, 128), ("core", "px"))
     bias = jnp.broadcast_to(point_bias[:, None], (C, NZ))
     cost = pl.CostEstimate(flops=800_000_000, bytes_accessed=4 << 20, transcendentals=0)
     linear = call(point_kernel, (4096, 128), lines, point_weight.T, bias, cost=cost)
-    out = call(z_back_kernel, (4096, 128), v.reshape(3072, 128), linear, two(z_inv))
+    out = halves(z_back_kernel, (256, 16, 128), v.reshape(192, 16, 128), linear, two(z_inv))
     return out.reshape(C, 8, 16, NZ)
 
 

time: 161 us -> 159 us (0.988)
  local copies, waits for them, and re-layouts: 6.64 us -> 2.68 us
  starting transfers between devices: 34.3 us -> 31.3 us
  blocking collectives: 41.3 us -> 43.7 us
    pallas_call x0 -> x2, Pallas kernels: none -> 9.3 us  [halves(): pl.pallas_call(kernel, grid=(2,), out_shape=jax.ShapeDtypeStruct(shape, F...]
    pallas_call x8 -> x6, Pallas kernels: 16.6 us -> 7.63 us  [call(): pl.pallas_call(kernel, out_shape=jax.ShapeDtypeStruct(shape, F32), in_spe...]
    unnamed x31 -> x23, local copies, waits for them, and re-layouts: 6.54 us -> 2.58 us
    all_to_all x4, starting transfers between devices: 34.3 us -> 31.3 us  [exchange(): return lax.all_to_all(v, axes, 0, 0, tiled=True)]
    all_to_all x2, blocking collectives: 41.3 us -> 43.7 us  [exchange(): return lax.all_to_all(v, axes, 0, 0, tiled=True)]
where the time goes in v3:
time: 159 us; the launch traced here: 158 us
  waiting for transfers between devices  63.4 us (40%)
  blocking collectives  43.7 us (27%)
  starting transfers between devices  31.3 us (20%)
  Pallas kernels  16.9 us (11%)
  local copies, waits for them, and re-layouts  2.68 us (2%)
    all_to_all x4, waiting for transfers between devices, exchange(): return lax.all_to_all(v, axes, 0, 0, tiled=True)  63.4 us
    all_to_all x2, blocking collectives, exchange(): return lax.all_to_all(v, axes, 0, 0, tiled=True)  43.7 us
    all_to_all x4, starting transfers between devices, exchange(): return lax.all_to_all(v, axes, 0, 0, tiled=True)  31.3 us
    pallas_call x2, Pallas kernels, halves(): pl.pallas_call(kernel, grid=(2,), out_shape=jax.ShapeDtypeStruct(shape, F...  9.3 us
    pallas_call x6, Pallas kernels, call(): pl.pallas_call(kernel, out_shape=jax.ShapeDtypeStruct(shape, F32), in_spe...  7.63 us
  transfers between devices with their start and end apart: 4, of which 4 were waited for; matrix products, arithmetic and copies ran while one was open for 0% of the time, Pallas kernels for 2%

profile of v3, /device:TPU:1, one launch (start us, length us, event | category | flops | bytes accessed | tf_op | source)
XLA Modules:
  0.0 158.0 jit_solution(17315154132612512323)
XLA Ops:
  0.0 4.3 %shard_map.109 = f32[192,16,128]{2,1,0:T(8,128)} custom-call(f32[256,16,128]{2,1,0:T(8,128)} %bitcast.22, bf16[2,96,128]{2,1,0:T(8,128)(2,1)} %constant.45.clone.table), custom_call_target="tpu_custom_call" | custom-call | tf_op jit(solution)/shard_map/pallas_call | solution.py:297
  4.3 10.5 %all-to-all-start = ((f32[8,12,2,16,128]{4,3,2,1,0:T(8,128)}), f32[8,12,2,16,128]{4,3,2,1,0:T(8,128)S(1)}, u32[]{:S(2)}, u32[]{:S(2)}) async-start(f32[8,12,2,16,128]{4,3,2,1,0:T(8,128)} %bitcast.34), calls=%async_computation | async-start | bytes 3145728 | tf_op jit(solution)/shard_map/all_to_all | solution.py:308
  14.8 20.6 %all-to-all-done = f32[8,12,2,16,128]{4,3,2,1,0:T(8,128)S(1)} async-done(((f32[8,12,2,16,128]{4,3,2,1,0:T(8,128)}), f32[8,12,2,16,128]{4,3,2,1,0:T(8,128)S(1)}, u32[]{:S(2)}, u32[]{:S(2)}) %all-to-all-start) | async-done | bytes 1572896 | tf_op jit(solution)/shard_map/all_to_all | solution.py:308
  35.4 0.8 shard_map.110
  36.2 0.0 copy-start.3
  36.2 0.0 copy-start.6
  36.2 30.8 %all_to_all.30 = f32[64,9,2,128]{3,2,1,0:T(2,128)S(1)} all-to-all(f32[64,9,2,128]{3,2,1,0:T(2,128)S(1)} %bitcast.27), channel_id=1, replica_groups=mesh['yl'=4,'zz'=8,'px'=4,'ph'=2,'core'=2] {'yl','zz','ph'}, dimensions={0} | all-to-all | bytes 1179648 | tf_op jit(solution)/shard_map/all_to_all | solution.py:308
  67.0 1.0 shard_map.111
  68.1 5.4 %all-to-all-start.2 = ((f32[32,8,128]{2,1,0:T(8,128)}), f32[32,8,128]{2,1,0:T(8,128)S(1)}, u32[]{:S(2)}, u32[]{:S(2)}) async-start(f32[32,8,128]{2,1,0:T(8,128)} %bitcast.7), calls=%async_computation.2 | async-start | bytes 262144 | tf_op jit(solution)/shard_map/all_to_all | solution.py:308
  73.5 9.9 %all-to-all-done.2 = f32[32,8,128]{2,1,0:T(8,128)S(1)} async-done(((f32[32,8,128]{2,1,0:T(8,128)}), f32[32,8,128]{2,1,0:T(8,128)S(1)}, u32[]{:S(2)}, u32[]{:S(2)}) %all-to-all-start.2) | async-done | bytes 131104 | tf_op jit(solution)/shard_map/all_to_all | solution.py:308
  83.3 1.2 shard_map.112
  84.6 12.9 %all_to_all.31 = f32[32,8,128]{2,1,0:T(8,128)S(1)} all-to-all(f32[32,8,128]{2,1,0:T(8,128)S(1)} %bitcast.31), channel_id=1, replica_groups=mesh['yl'=4,'zz'=8,'px'=4,'ph'=2,'core'=2] {'zz','yl'}, dimensions={0} | all-to-all | bytes 262144 | tf_op jit(solution)/shard_map/all_to_all | solution.py:308
  97.4 1.3 shard_map.113
  98.7 5.1 %all-to-all-start.4 = ((f32[64,9,2,128]{3,2,1,0:T(2,128)}), f32[64,9,2,128]{3,2,1,0:T(2,128)S(1)}, u32[]{:S(2)}, u32[]{:S(2)}) async-start(f32[64,9,2,128]{3,2,1,0:T(2,128)} %bitcast.12), calls=%async_computation.4 | async-start | bytes 1179648 | tf_op jit(solution)/shard_map/all_to_all | solution.py:308
  103.8 16.2 %all-to-all-done.4 = f32[64,9,2,128]{3,2,1,0:T(2,128)S(1)} async-done(((f32[64,9,2,128]{3,2,1,0:T(2,128)}), f32[64,9,2,128]{3,2,1,0:T(2,128)S(1)}, u32[]{:S(2)}, u32[]{:S(2)}) %all-to-all-start.4) | async-done | bytes 589856 | tf_op jit(solution)/shard_map/all_to_all | solution.py:308
  120.0 0.8 shard_map.114
  120.8 1.1 copy-done.2
  121.9 10.4 %all-to-all-start.5 = ((f32[8,12,2,16,128]{4,3,2,1,0:T(8,128)}), f32[8,12,2,16,128]{4,3,2,1,0:T(8,128)}, u32[]{:S(2)}, u32[]{:S(2)}) async-start(f32[8,12,2,16,128]{4,3,2,1,0:T(8,128)} %bitcast.25), calls=%async_computation.5 | async-start | bytes 3145728 | tf_op jit(solution)/shard_map/all_to_all | solution.py:308
  132.3 0.1 copy.12
  132.4 0.1 broadcast_in_dim.2.bias
  132.4 2.5 %shard_map.115.linear = f32[4096,128]{1,0:T(8,128)S(1)} custom-call(f32[4096,128]{1,0:T(8,128)S(1)} %bitcast.23, f32[32,32]{1,0:T(8,128)S(1)} %bitcast.33, f32[32,128]{1,0:T(8,128)S(1)} %broadcast_in_dim.2.bias), custom_call_target="tpu_custom_call" | custom-call | flops 800000000 | bytes 4194304 | tf_op jit(solution)/shard_map/pallas_call | solution.py:278
  135.0 1.3 copy-done.1
  136.3 16.7 %all-to-all-done.5 = f32[8,12,2,16,128]{4,3,2,1,0:T(8,128)} async-done(((f32[8,12,2,16,128]{4,3,2,1,0:T(8,128)}), f32[8,12,2,16,128]{4,3,2,1,0:T(8,128)}, u32[]{:S(2)}, u32[]{:S(2)}) %all-to-all-start.5) | async-done | bytes 1572896 | tf_op jit(solution)/shard_map/all_to_all | solution.py:308
  153.0 5.0 %shard_map.116 = f32[256,16,128]{2,1,0:T(8,128)} custom-call(f32[192,16,128]{2,1,0:T(8,128)} %bitcast.16.rows, f32[4096,128]{1,0:T(8,128)} %copy-done.1, bf16[2,96,128]{2,1,0:T(8,128)(2,1)} %constant.51.clone.table), custom_call_target="tpu_custom_call" | custom-call | tf_op jit(solution)/shard_map/pallas_call | solution.py:297
  (20 shorter events, 0.1 us)
Async XLA Ops:
  4.3 10.5 %copy-start.8 = (bf16[2,2,128,256]{3,2,0,1:T(8,128)(2,1)S(1)}, bf16[2,2,128,256]{3,2,0,1:T(8,128)(2,1)}, u32[]{:S(2)}) copy-start(bf16[2,2,128,256]{3,2,0,1:T(8,128)(2,1)} %constant.46.clone) | copy-start | bytes 786436
  4.3 31.1 %all-to-all-start = ((f32[8,12,2,16,128]{4,3,2,1,0:T(8,128)}), f32[8,12,2,16,128]{4,3,2,1,0:T(8,128)S(1)}, u32[]{:S(2)}, u32[]{:S(2)}) async-start(f32[8,12,2,16,128]{4,3,2,1,0:T(8,128)} %bitcast.34), calls=%async_computation | async-start | bytes 3145728 | tf_op jit(solution)/shard_map/all_to_all | solution.py:308
  35.4 31.6 %copy-start.5 = (bf16[2,128,256]{2,1,0:T(8,128)(2,1)S(1)}, bf16[2,128,256]{2,1,0:T(8,128)(2,1)}, u32[]{:S(2)}) copy-start(bf16[2,128,256]{2,1,0:T(8,128)(2,1)} %constant.47.clone.table) | copy-start | bytes 393220
  36.2 47.2 %copy-start.3 = (bf16[2,72,3,1024]{3,1,2,0:T(8,128)(2,1)S(1)}, bf16[2,72,3,1024]{3,1,2,0:T(8,128)(2,1)}, u32[]{:S(2)}) copy-start(bf16[2,72,3,1024]{3,1,2,0:T(8,128)(2,1)} %param.12) | copy-start | bytes 2654212
  36.2 47.1 %copy-start.6 = (bf16[32,1024]{1,0:T(8,128)(2,1)S(1)}, bf16[32,1024]{1,0:T(8,128)(2,1)}, u32[]{:S(2)}) copy-start(bf16[32,1024]{1,0:T(8,128)(2,1)} %constant.48.clone.expand) | copy-start | bytes 196612
  67.0 30.4 %copy-start.4 = (bf16[2,256,128]{2,1,0:T(8,128)(2,1)S(1)}, bf16[2,256,128]{2,1,0:T(8,128)(2,1)}, u32[]{:S(2)}) copy-start(bf16[2,256,128]{2,1,0:T(8,128)(2,1)} %constant.49.clone.table) | copy-start | bytes 393220
  68.1 15.3 %all-to-all-start.2 = ((f32[32,8,128]{2,1,0:T(8,128)}), f32[32,8,128]{2,1,0:T(8,128)S(1)}, u32[]{:S(2)}, u32[]{:S(2)}) async-start(f32[32,8,128]{2,1,0:T(8,128)} %bitcast.7), calls=%async_computation.2 | async-start | bytes 262144 | tf_op jit(solution)/shard_map/all_to_all | solution.py:308
  83.3 20.4 %copy-start.7 = (bf16[2,2,256,128]{3,2,0,1:T(8,128)(2,1)S(1)}, bf16[2,2,256,128]{3,2,0,1:T(8,128)(2,1)}, u32[]{:S(2)}) copy-start(bf16[2,2,256,128]{3,2,0,1:T(8,128)(2,1)} %constant.50.clone) | copy-start | bytes 786436
  98.7 21.3 %all-to-all-start.4 = ((f32[64,9,2,128]{3,2,1,0:T(2,128)}), f32[64,9,2,128]{3,2,1,0:T(2,128)S(1)}, u32[]{:S(2)}, u32[]{:S(2)}) async-start(f32[64,9,2,128]{3,2,1,0:T(2,128)} %bitcast.12), calls=%async_computation.4 | async-start | bytes 1179648 | tf_op jit(solution)/shard_map/all_to_all | solution.py:308
  120.8 1.1 copy-start.2
  121.9 10.4 %copy-start.9 = (f32[32,32]{1,0:T(8,128)S(1)}, f32[32,32]{1,0:T(8,128)}, u32[]{:S(2)}) copy-start(f32[32,32]{1,0:T(8,128)} %param.13) | copy-start | bytes 12292
  121.9 10.4 %copy-start.10 = (f32[32]{0:T(128)S(1)}, f32[32]{0:T(128)}, u32[]{:S(2)}) copy-start(f32[32]{0:T(128)} %param.14) | copy-start | bytes 388
  121.9 10.5 %copy-start = (f32[32,8,16,128]{3,2,1,0:T(8,128)S(1)}, f32[32,8,16,128]{3,2,1,0:T(8,128)}, u32[]{:S(2)}) copy-start(f32[32,8,16,128]{3,2,1,0:T(8,128)} %param.11) | copy-start | bytes 6291460
  121.9 31.1 %all-to-all-start.5 = ((f32[8,12,2,16,128]{4,3,2,1,0:T(8,128)}), f32[8,12,2,16,128]{4,3,2,1,0:T(8,128)}, u32[]{:S(2)}, u32[]{:S(2)}) async-start(f32[8,12,2,16,128]{4,3,2,1,0:T(8,128)} %bitcast.25), calls=%async_computation.5 | async-start | bytes 3145728 | tf_op jit(solution)/shard_map/all_to_all | solution.py:308
  135.0 1.3 copy-start.1

commit v4 on v3

--- a/solution.py
+++ b/solution.py
@@ -95,18 +95,18 @@
 NT = ((1,), (1,))
 
 
-def lines_at(ref, y, ys=16):
-    return jnp.concatenate([ref[pl.ds(x * ys + y, 32, stride=8 * ys), :] for x in range(8)], axis=0)
+def lines_at(ref, y, xs=8, ys=16):
+    return jnp.concatenate([ref[pl.ds(x * ys + y, 32, stride=xs * ys), :] for x in range(xs)], axis=0)
 
 
 def z_kernel(field, table, out):
-    t = (table[0], table[1])
-    field = field.reshape(2048, 128)
-    out = out.reshape(1536, 128)
+    t = table[...]
+    field = field.reshape(1024, 128)
+    out = out.reshape(768, 128)
     for y in range(8):
-        r = dot3(t, split(lines_at(field, y, 8)), NT)
-        for half in range(2):
-            out[pl.ds(half * 8 + y, 96, stride=16), :] = r[:, half * 128 : half * 128 + 128]
+        a = jnp.concatenate(split(lines_at(field, y, 4, 8)), axis=1)
+        r = dot(t, a, NT)
+        out[pl.ds(y, 96, stride=8), :] = r[:96] + r[96:]
 
 
 def y_kernel(rows, table, out):
@@ -225,9 +225,10 @@
                 out[pl.ds(h * 18 + k * 8 + x, 32, stride=36), :] = s[x]
 
 
-def y_back_kernel(rows, table, out):
+def y_back_kernel(rows, table, out, work, sems):
     t = (table[0], table[1])
     lane = lax.broadcasted_iota(jnp.int32, (256, 128), 1) % B
+    copies = []
     for h in range(2):
         at = lambda r: rows[pl.ds(h * 18 + r, 32, stride=36), :]
         v = [jnp.concatenate([at(8 * k + x) for x in range(8)], axis=0) for k in range(2)]
@@ -241,7 +242,11 @@
             for ri in range(2):
                 for half in range(2):
                     part = r[ri * 128 : ri * 128 + 128, half * 128 : half * 128 + 128]
-                    out[:, 3 * h + k, ri, half] = part.reshape(8, 16, 128)
+                    work[3 * h + k, :, ri, half] = part.reshape(8, 16, 128)
+            copies.append(pltpu.make_async_copy(work.at[3 * h + k], out.at[:, 3 * h + k], sems.at[3 * h + k]))
+            copies[-1].start()
+    for copy in copies:
+        copy.wait()
 
 
 def point_kernel(field, weight, bias, out):
@@ -251,27 +256,27 @@
     w = split(jnp.where(row == col, w, 0.0))
     b = jnp.concatenate([bias[...]] * 8, axis=0)
     for y in range(16):
-        out[256 * y : 256 * y + 256, :] = dot3(w, split(lines_at(field, y))) + b
+        out[y] = (dot3(w, split(lines_at(field, y))) + b).reshape(2, 128, 128)
 
 
 def z_back_kernel(rows, linear, table, out):
-    t = (table[0], table[1])
-    rows = rows.reshape(1536, 128)
-    out = out.reshape(2048, 128)
+    t = table[...]
+    rows = rows.reshape(768, 128)
+    linear = linear.reshape(1024, 128)
+    out = out.reshape(1024, 128)
     for y in range(8):
-        v = jnp.concatenate(
-            [rows[pl.ds(half * 8 + y, 96, stride=16), :] for half in range(2)], axis=1
-        ).T
-        s = dot3(split(v), t) + linear[256 * y : 256 * y + 256, :]
+        v = jnp.concatenate(split(rows[pl.ds(y, 96, stride=8), :]), axis=0)
+        r = dot(v.T, t)
+        s = r[:, :128] + r[:, 128:] + linear[128 * y : 128 * y + 128, :]
         s = 0.5 * s * (1.0 + lax.erf(s * np.float32(np.sqrt(0.5))))
-        for x in range(8):
-            out[pl.ds(x * 8 + y, 32, stride=64), :] = s[32 * x : 32 * x + 32]
+        for x in range(4):
+            out[pl.ds(x * 8 + y, 32, stride=32), :] = s[32 * x : 32 * x + 32]
 
 
 PARAMS = pltpu.CompilerParams(vmem_limit_bytes=40 * 1024 * 1024)
 
 
-def call(kernel, shape, *operands, scratch=(), smem=0, cost=None):
+def call(kernel, shape, *operands, scratch=(), smem=0, cost=None, place=pltpu.VMEM):
     specs = [
         pl.BlockSpec(memory_space=pltpu.SMEM if i < smem else pltpu.VMEM) for i in range(len(operands))
     ]
@@ -279,24 +284,23 @@
         kernel,
         out_shape=jax.ShapeDtypeStruct(shape, F32),
         in_specs=specs,
-        out_specs=pl.BlockSpec(memory_space=pltpu.VMEM),
+        out_specs=pl.BlockSpec(memory_space=place),
         scratch_shapes=list(scratch),
         compiler_params=PARAMS,
         cost_estimate=cost,
     )(*operands)
 
 
-def halves(kernel, shape, *operands):
-    def spec(dims):
-        if len(dims) == 3 and dims[1] == 16:
-            return pl.BlockSpec((dims[0], 8, dims[2]), lambda i: (0, i, 0))
-        if dims == (4096, 128):
-            return pl.BlockSpec((2048, 128), lambda i: (i, 0))
-        return pl.BlockSpec(dims, lambda i: (0,) * len(dims))
-
+def quarters(kernel, shape, *operands):
+    specs = {
+        (32, 2, 4, 16, 128): pl.BlockSpec((32, 1, 4, 8, 128), lambda i, j: (0, j, 0, i, 0)),
+        (96, 2, 16, 128): pl.BlockSpec((96, 1, 8, 128), lambda i, j: (0, j, i, 0)),
+        (16, 2, 128, 128): pl.BlockSpec((8, 1, 128, 128), lambda i, j: (i, j, 0, 0)),
+    }
+    spec = lambda dims: specs.get(dims) or pl.BlockSpec(dims, lambda i, j: (0, 0))
     return pl.pallas_call(
         kernel,
-        grid=(2,),
+        grid=(2, 2),
         out_shape=jax.ShapeDtypeStruct(shape, F32),
         in_specs=[spec(v.shape) for v in operands],
         out_specs=spec(shape),
@@ -316,7 +320,9 @@
     pick = lambda table: lax.dynamic_index_in_dim(jnp.asarray(two(table)), half, 1, False)
     lines = field.reshape(C * 8 * 16, NZ)
 
-    v = halves(z_kernel, (192, 16, 128), field.reshape(256, 16, 128), two(z_fwd))
+    hi, lo = two(z_fwd)
+    table = np.block([[hi, hi], [lo, np.zeros_like(lo)]])
+    v = quarters(z_kernel, (96, 2, 16, 128), field.reshape(C, 2, 4, 16, NZ), table)
     v = exchange(v.reshape(8, 12, 2, 16, 128), ("core", "px"))
     v = call(y_kernel, (1152, 128), v.reshape(8, 6, 2, 2, 16, 128), pick(y_fwd))
     v = exchange(v.reshape(64, 9, 2, 128), GX + ("ph",))
@@ -339,12 +345,21 @@
     v = exchange(v.reshape(32, 8, 128), ("zz", "yl"))
     v = call(x_back_kernel, (1152, 128), v.reshape(256, 128), two(x_inv))
     v = exchange(v.reshape(64, 9, 2, 128), GX + ("ph",))
-    v = call(y_back_kernel, (8, 6, 2, 2, 16, 128), v.reshape(1152, 128), pick(y_inv))
+    v = call(
+        y_back_kernel,
+        (8, 6, 2, 2, 16, 128),
+        v.reshape(1152, 128),
+        pick(y_inv),
+        scratch=[pltpu.VMEM((6, 8, 2, 2, 16, 128), F32), pltpu.SemaphoreType.DMA((6,))],
+        place=pltpu.HBM,
+    )
     v = exchange(v.reshape(8, 12, 2, 16, 128), ("core", "px"))
     bias = jnp.broadcast_to(point_bias[:, None], (C, NZ))
     cost = pl.CostEstimate(flops=800_000_000, bytes_accessed=4 << 20, transcendentals=0)
-    linear = call(point_kernel, (4096, 128), lines, point_weight.T, bias, cost=cost)
-    out = halves(z_back_kernel, (256, 16, 128), v.reshape(192, 16, 128), linear, two(z_inv))
+    linear = call(point_kernel, (16, 2, 128, 128), lines, point_weight.T, bias, cost=cost)
+    hi, lo = two(z_inv)
+    table = np.block([[hi, lo], [hi, np.zeros_like(lo)]])
+    out = quarters(z_back_kernel, (C, 2, 4, 16, NZ), v.reshape(96, 2, 16, 128), linear, table)
     return out.reshape(C, 8, 16, NZ)
 
 

time: 159 us -> 161 us (1.013)
  Pallas kernels: 16.9 us -> 19.2 us
where the time goes in v4:
time: 161 us; the launch traced here: 160 us
  waiting for transfers between devices  63.4 us (39%)
  blocking collectives  43.7 us (27%)
  starting transfers between devices  31.3 us (19%)
  Pallas kernels  19.2 us (12%)
  local copies, waits for them, and re-layouts  2.68 us (2%)
    all_to_all x4, waiting for transfers between devices, exchange(): return lax.all_to_all(v, axes, 0, 0, tiled=True)  63.4 us
    all_to_all x2, blocking collectives, exchange(): return lax.all_to_all(v, axes, 0, 0, tiled=True)  43.7 us
    all_to_all x4, starting transfers between devices, exchange(): return lax.all_to_all(v, axes, 0, 0, tiled=True)  31.3 us
    pallas_call x2, Pallas kernels, quarters(): pl.pallas_call(kernel, grid=(2, 2), out_shape=jax.ShapeDtypeStruct(shape,...  10 us
    pallas_call x6, Pallas kernels, call(): pl.pallas_call(kernel, out_shape=jax.ShapeDtypeStruct(shape, F32), in_spe...  9.16 us
  transfers between devices with their start and end apart: 4, of which 4 were waited for; matrix products, arithmetic and copies ran while one was open for 0% of the time, Pallas kernels for 2%

profile of v4, /device:TPU:1, one launch (start us, length us, event | category | flops | bytes accessed | tf_op | source)
XLA Modules:
  0.0 160.3 jit_solution(16551963004382757453)
XLA Ops:
  0.0 4.7 %shard_map.109 = f32[96,2,16,128]{3,2,1,0:T(8,128)} custom-call(f32[32,2,4,16,128]{4,3,2,1,0:T(8,128)} %bitcast.22, bf16[192,256]{1,0:T(8,128)(2,1)} %constant.45.clone.table), custom_call_target="tpu_custom_call" | custom-call | tf_op jit(solution)/shard_map/pallas_call | solution.py:301
  4.7 10.5 %all-to-all-start = ((f32[8,12,2,16,128]{4,3,2,1,0:T(8,128)}), f32[8,12,2,16,128]{4,3,2,1,0:T(8,128)S(1)}, u32[]{:S(2)}, u32[]{:S(2)}) async-start(f32[8,12,2,16,128]{4,3,2,1,0:T(8,128)} %bitcast.34), calls=%async_computation | async-start | bytes 3145728 | tf_op jit(solution)/shard_map/all_to_all | solution.py:312
  15.2 20.6 %all-to-all-done = f32[8,12,2,16,128]{4,3,2,1,0:T(8,128)S(1)} async-done(((f32[8,12,2,16,128]{4,3,2,1,0:T(8,128)}), f32[8,12,2,16,128]{4,3,2,1,0:T(8,128)S(1)}, u32[]{:S(2)}, u32[]{:S(2)}) %all-to-all-start) | async-done | bytes 1572896 | tf_op jit(solution)/shard_map/all_to_all | solution.py:312
  35.8 0.8 shard_map.110
  36.6 0.0 copy-start.3
  36.6 0.0 copy-start.6
  36.6 30.8 %all_to_all.30 = f32[64,9,2,128]{3,2,1,0:T(2,128)S(1)} all-to-all(f32[64,9,2,128]{3,2,1,0:T(2,128)S(1)} %bitcast.27), channel_id=1, replica_groups=mesh['yl'=4,'zz'=8,'px'=4,'ph'=2,'core'=2] {'yl','zz','ph'}, dimensions={0} | all-to-all | bytes 1179648 | tf_op jit(solution)/shard_map/all_to_all | solution.py:312
  67.5 1.0 shard_map.111
  68.5 5.4 %all-to-all-start.2 = ((f32[32,8,128]{2,1,0:T(8,128)}), f32[32,8,128]{2,1,0:T(8,128)S(1)}, u32[]{:S(2)}, u32[]{:S(2)}) async-start(f32[32,8,128]{2,1,0:T(8,128)} %bitcast.7), calls=%async_computation.2 | async-start | bytes 262144 | tf_op jit(solution)/shard_map/all_to_all | solution.py:312
  73.9 9.9 %all-to-all-done.2 = f32[32,8,128]{2,1,0:T(8,128)S(1)} async-done(((f32[32,8,128]{2,1,0:T(8,128)}), f32[32,8,128]{2,1,0:T(8,128)S(1)}, u32[]{:S(2)}, u32[]{:S(2)}) %all-to-all-start.2) | async-done | bytes 131104 | tf_op jit(solution)/shard_map/all_to_all | solution.py:312
  83.8 1.2 shard_map.112
  85.0 12.9 %all_to_all.31 = f32[32,8,128]{2,1,0:T(8,128)S(1)} all-to-all(f32[32,8,128]{2,1,0:T(8,128)S(1)} %bitcast.31), channel_id=1, replica_groups=mesh['yl'=4,'zz'=8,'px'=4,'ph'=2,'core'=2] {'zz','yl'}, dimensions={0} | all-to-all | bytes 262144 | tf_op jit(solution)/shard_map/all_to_all | solution.py:312
  97.9 1.3 shard_map.113
  99.1 5.1 %all-to-all-start.4 = ((f32[64,9,2,128]{3,2,1,0:T(2,128)}), f32[64,9,2,128]{3,2,1,0:T(2,128)S(1)}, u32[]{:S(2)}, u32[]{:S(2)}) async-start(f32[64,9,2,128]{3,2,1,0:T(2,128)} %bitcast.12), calls=%async_computation.4 | async-start | bytes 1179648 | tf_op jit(solution)/shard_map/all_to_all | solution.py:312
  104.2 16.2 %all-to-all-done.4 = f32[64,9,2,128]{3,2,1,0:T(2,128)S(1)} async-done(((f32[64,9,2,128]{3,2,1,0:T(2,128)}), f32[64,9,2,128]{3,2,1,0:T(2,128)S(1)}, u32[]{:S(2)}, u32[]{:S(2)}) %all-to-all-start.4) | async-done | bytes 589856 | tf_op jit(solution)/shard_map/all_to_all | solution.py:312
  120.4 2.3 %shard_map.114 = f32[8,6,2,2,16,128]{5,4,3,2,1,0:T(8,128)S(1)} custom-call(f32[1152,128]{1,0:T(8,128)S(1)} %bitcast.26, bf16[2,256,128]{2,1,0:T(8,128)(2,1)S(1)} %dynamic-slice_bitcast_fusion.table), custom_call_target="tpu_custom_call" | custom-call | tf_op jit(solution)/shard_map/pallas_call | solution.py:283
  122.8 1.1 copy-done.2
  123.9 10.4 %all-to-all-start.5 = ((f32[8,12,2,16,128]{4,3,2,1,0:T(8,128)}), f32[8,12,2,16,128]{4,3,2,1,0:T(8,128)}, u32[]{:S(2)}, u32[]{:S(2)}) async-start(f32[8,12,2,16,128]{4,3,2,1,0:T(8,128)} %bitcast.25), calls=%async_computation.5 | async-start | bytes 3145728 | tf_op jit(solution)/shard_map/all_to_all | solution.py:312
  134.3 0.1 copy.12
  134.3 0.1 broadcast_in_dim.2.bias
  134.4 2.5 %shard_map.115.linear = f32[16,2,128,128]{3,2,1,0:T(8,128)S(1)} custom-call(f32[4096,128]{1,0:T(8,128)S(1)} %bitcast.23, f32[32,32]{1,0:T(8,128)S(1)} %bitcast.33, f32[32,128]{1,0:T(8,128)S(1)} %broadcast_in_dim.2.bias), custom_call_target="tpu_custom_call" | custom-call | flops 800000000 | bytes 4194304 | tf_op jit(solution)/shard_map/pallas_call | solution.py:283
  137.0 1.3 copy-done.1
  138.3 16.7 %all-to-all-done.5 = f32[8,12,2,16,128]{4,3,2,1,0:T(8,128)} async-done(((f32[8,12,2,16,128]{4,3,2,1,0:T(8,128)}), f32[8,12,2,16,128]{4,3,2,1,0:T(8,128)}, u32[]{:S(2)}, u32[]{:S(2)}) %all-to-all-start.5) | async-done | bytes 1572896 | tf_op jit(solution)/shard_map/all_to_all | solution.py:312
  155.0 5.3 %shard_map.116 = f32[32,2,4,16,128]{4,3,2,1,0:T(8,128)} custom-call(f32[96,2,16,128]{3,2,1,0:T(8,128)} %bitcast.16.rows, f32[16,2,128,128]{3,2,1,0:T(8,128)} %copy-done.1, bf16[192,256]{1,0:T(8,128)(2,1)} %constant.51.clone.table), custom_call_target="tpu_custom_call" | custom-call | tf_op jit(solution)/shard_map/pallas_call | solution.py:301
  (20 shorter events, 0.1 us)
Async XLA Ops:
  4.7 10.5 %copy-start.8 = (bf16[2,2,128,256]{3,2,0,1:T(8,128)(2,1)S(1)}, bf16[2,2,128,256]{3,2,0,1:T(8,128)(2,1)}, u32[]{:S(2)}) copy-start(bf16[2,2,128,256]{3,2,0,1:T(8,128)(2,1)} %constant.46.clone) | copy-start | bytes 786436
  4.7 31.1 %all-to-all-start = ((f32[8,12,2,16,128]{4,3,2,1,0:T(8,128)}), f32[8,12,2,16,128]{4,3,2,1,0:T(8,128)S(1)}, u32[]{:S(2)}, u32[]{:S(2)}) async-start(f32[8,12,2,16,128]{4,3,2,1,0:T(8,128)} %bitcast.34), calls=%async_computation | async-start | bytes 3145728 | tf_op jit(solution)/shard_map/all_to_all | solution.py:312
  35.8 31.6 %copy-start.5 = (bf16[2,128,256]{2,1,0:T(8,128)(2,1)S(1)}, bf16[2,128,256]{2,1,0:T(8,128)(2,1)}, u32[]{:S(2)}) copy-start(bf16[2,128,256]{2,1,0:T(8,128)(2,1)} %constant.47.clone.table) | copy-start | bytes 393220
  36.6 47.2 %copy-start.3 = (bf16[2,72,3,1024]{3,1,2,0:T(8,128)(2,1)S(1)}, bf16[2,72,3,1024]{3,1,2,0:T(8,128)(2,1)}, u32[]{:S(2)}) copy-start(bf16[2,72,3,1024]{3,1,2,0:T(8,128)(2,1)} %param.12) | copy-start | bytes 2654212
  36.6 47.1 %copy-start.6 = (bf16[32,1024]{1,0:T(8,128)(2,1)S(1)}, bf16[32,1024]{1,0:T(8,128)(2,1)}, u32[]{:S(2)}) copy-start(bf16[32,1024]{1,0:T(8,128)(2,1)} %constant.48.clone.expand) | copy-start | bytes 196612
  67.5 30.4 %copy-start.4 = (bf16[2,256,128]{2,1,0:T(8,128)(2,1)S(1)}, bf16[2,256,128]{2,1,0:T(8,128)(2,1)}, u32[]{:S(2)}) copy-start(bf16[2,256,128]{2,1,0:T(8,128)(2,1)} %constant.49.clone.table) | copy-start | bytes 393220
  68.5 15.3 %all-to-all-start.2 = ((f32[32,8,128]{2,1,0:T(8,128)}), f32[32,8,128]{2,1,0:T(8,128)S(1)}, u32[]{:S(2)}, u32[]{:S(2)}) async-start(f32[32,8,128]{2,1,0:T(8,128)} %bitcast.7), calls=%async_computation.2 | async-start | bytes 262144 | tf_op jit(solution)/shard_map/all_to_all | solution.py:312
  83.8 20.4 %copy-start.7 = (bf16[2,2,256,128]{3,2,0,1:T(8,128)(2,1)S(1)}, bf16[2,2,256,128]{3,2,0,1:T(8,128)(2,1)}, u32[]{:S(2)}) copy-start(bf16[2,2,256,128]{3,2,0,1:T(8,128)(2,1)} %constant.50.clone) | copy-start | bytes 786436
  99.1 21.3 %all-to-all-start.4 = ((f32[64,9,2,128]{3,2,1,0:T(2,128)}), f32[64,9,2,128]{3,2,1,0:T(2,128)S(1)}, u32[]{:S(2)}, u32[]{:S(2)}) async-start(f32[64,9,2,128]{3,2,1,0:T(2,128)} %bitcast.12), calls=%async_computation.4 | async-start | bytes 1179648 | tf_op jit(solution)/shard_map/all_to_all | solution.py:312
  122.8 1.1 copy-start.2
  123.9 10.4 %copy-start.9 = (f32[32,32]{1,0:T(8,128)S(1)}, f32[32,32]{1,0:T(8,128)}, u32[]{:S(2)}) copy-start(f32[32,32]{1,0:T(8,128)} %param.13) | copy-start | bytes 12292
  123.9 10.4 %copy-start.10 = (f32[32]{0:T(128)S(1)}, f32[32]{0:T(128)}, u32[]{:S(2)}) copy-start(f32[32]{0:T(128)} %param.14) | copy-start | bytes 388
  123.9 10.5 %copy-start = (f32[32,8,16,128]{3,2,1,0:T(8,128)S(1)}, f32[32,8,16,128]{3,2,1,0:T(8,128)}, u32[]{:S(2)}) copy-start(f32[32,8,16,128]{3,2,1,0:T(8,128)} %param.11) | copy-start | bytes 6291460
  123.9 31.1 %all-to-all-start.5 = ((f32[8,12,2,16,128]{4,3,2,1,0:T(8,128)}), f32[8,12,2,16,128]{4,3,2,1,0:T(8,128)}, u32[]{:S(2)}, u32[]{:S(2)}) async-start(f32[8,12,2,16,128]{4,3,2,1,0:T(8,128)} %bitcast.25), calls=%async_computation.5 | async-start | bytes 3145728 | tf_op jit(solution)/shard_map/all_to_all | solution.py:312
  137.0 1.3 copy-start.1

commit v5 on v3

--- a/solution.py
+++ b/solution.py
@@ -95,22 +95,38 @@
 NT = ((1,), (1,))
 
 
-def lines_at(ref, y, ys=16):
-    return jnp.concatenate([ref[pl.ds(x * ys + y, 32, stride=8 * ys), :] for x in range(8)], axis=0)
-
-
-def z_kernel(field, table, out):
-    t = (table[0], table[1])
-    field = field.reshape(2048, 128)
-    out = out.reshape(1536, 128)
-    for y in range(8):
-        r = dot3(t, split(lines_at(field, y, 8)), NT)
-        for half in range(2):
-            out[pl.ds(half * 8 + y, 96, stride=16), :] = r[:, half * 128 : half * 128 + 128]
+def lines_at(ref, y):
+    return jnp.concatenate([ref[pl.ds(x * 16 + y, 32, stride=128), :] for x in range(8)], axis=0)
+
+
+CHUNKS = [(h, slice(4 * h, 4 * h + 4), slice(8 * i, 8 * i + 8)) for h in range(2) for i in range(2)]
+
+
+def z_kernel(field, table, out, work, t, done, sems):
+    copies = [pltpu.make_async_copy(table, t, sems.at[4])]
+    for i, (h, xs, ys) in enumerate(CHUNKS):
+        copies.append(pltpu.make_async_copy(field.at[:, xs, ys], work.at[:, xs, ys], sems.at[i]))
+    for copy in copies:
+        copy.start()
+    copies[0].wait()
+    for i, (h, xs, ys) in enumerate(CHUNKS):
+        copies[i + 1].wait()
+        by_y = [jnp.swapaxes(work[:, 4 * h + x, ys, :], 0, 1) for x in range(4)]
+        modes = []
+        for y in range(8):
+            a = jnp.concatenate([v[y] for v in by_y], axis=0)
+            r = dot(t[...], jnp.concatenate(split(a), axis=1), NT)
+            modes.append(r[:96] + r[96:])
+        done[:, h, ys, :] = jnp.swapaxes(jnp.stack(modes), 0, 1)
+        copies.append(pltpu.make_async_copy(done.at[:, h, ys], out.at[:, h, ys], sems.at[5 + i]))
+        copies[-1].start()
+    for copy in copies[5:]:
+        copy.wait()
 
 
 def y_kernel(rows, table, out):
-    t = (table[0], table[1])
+    half = lax.axis_index("ph")
+    t = (table[0, half], table[1, half])
     for h in range(2):
         r = []
         for k in range(3):
@@ -163,8 +179,8 @@
         out[pl.ds(a, 32, stride=8), :] = jnp.zeros((32, 128), F32)
 
 
-def mix_kernel(par, modes, w, expand, out, in_re, in_im, mid_re, mid_im):
-    start = pl.multiple_of(par[0] * 24, 8)
+def mix_kernel(modes, w, expand, out, in_re, in_im, mid_re, mid_im):
+    start = pl.multiple_of(lax.axis_index("zz") % 2 * 24, 8)
     e = expand[...]
     for a in range(2):
         v = [modes[pl.ds(2 * k + a, 32, stride=8), :].T for k in range(3)]
@@ -226,7 +242,8 @@
 
 
 def y_back_kernel(rows, table, out):
-    t = (table[0], table[1])
+    half = lax.axis_index("ph")
+    t = (table[0, half], table[1, half])
     lane = lax.broadcasted_iota(jnp.int32, (256, 128), 1) % B
     for h in range(2):
         at = lambda r: rows[pl.ds(h * 18 + r, 32, stride=36), :]
@@ -251,56 +268,41 @@
     w = split(jnp.where(row == col, w, 0.0))
     b = jnp.concatenate([bias[...]] * 8, axis=0)
     for y in range(16):
-        out[256 * y : 256 * y + 256, :] = dot3(w, split(lines_at(field, y))) + b
-
-
-def z_back_kernel(rows, linear, table, out):
-    t = (table[0], table[1])
-    rows = rows.reshape(1536, 128)
-    out = out.reshape(2048, 128)
-    for y in range(8):
-        v = jnp.concatenate(
-            [rows[pl.ds(half * 8 + y, 96, stride=16), :] for half in range(2)], axis=1
-        ).T
-        s = dot3(split(v), t) + linear[256 * y : 256 * y + 256, :]
-        s = 0.5 * s * (1.0 + lax.erf(s * np.float32(np.sqrt(0.5))))
-        for x in range(8):
-            out[pl.ds(x * 8 + y, 32, stride=64), :] = s[32 * x : 32 * x + 32]
-
-
-PARAMS = pltpu.CompilerParams(vmem_limit_bytes=40 * 1024 * 1024)
-
-
-def call(kernel, shape, *operands, scratch=(), smem=0, cost=None):
-    specs = [
-        pl.BlockSpec(memory_space=pltpu.SMEM if i < smem else pltpu.VMEM) for i in range(len(operands))
-    ]
+        out[y] = (dot3(w, split(lines_at(field, y))) + b).reshape(2, 128, 128)
+
+
+def z_back_kernel(rows, linear, table, out, work, sems):
+    t = table[...]
+    copies = []
+    for i, (h, xs, ys) in enumerate(CHUNKS):
+        by_y = jnp.swapaxes(rows[:, h, ys, :], 0, 1)
+        cells = []
+        for y in range(8):
+            r = dot(jnp.concatenate(split(by_y[y]), axis=0).T, t)
+            s = r[:, :128] + r[:, 128:] + linear[ys.start + y, h]
+            cells.append(0.5 * s * (1.0 + lax.erf(s * np.float32(np.sqrt(0.5)))))
+        cells = jnp.stack(cells)
+        for x in range(4):
+            work[:, 4 * h + x, ys, :] = jnp.swapaxes(cells[:, 32 * x : 32 * x + 32], 0, 1)
+        copies.append(pltpu.make_async_copy(work.at[:, xs, ys], out.at[:, xs, ys], sems.at[i]))
+        copies[-1].start()
+    for copy in copies:
+        copy.wait()
+
+
+VMEM = pl.BlockSpec(memory_space=pltpu.VMEM)
+ANY = pl.BlockSpec(memory_space=pl.ANY)
+
+
+def call(kernel, shape, *operands, ins=VMEM, outs=VMEM, scratch=(), limit=24, cost=None):
     return pl.pallas_call(
         kernel,
         out_shape=jax.ShapeDtypeStruct(shape, F32),
-        in_specs=specs,
-        out_specs=pl.BlockSpec(memory_space=pltpu.VMEM),
+        in_specs=[ins] * len(operands),
+        out_specs=outs,
         scratch_shapes=list(scratch),
-        compiler_params=PARAMS,
+        compiler_params=pltpu.CompilerParams(vmem_limit_bytes=limit * 1024 * 1024),
         cost_estimate=cost,
-    )(*operands)
-
-
-def halves(kernel, shape, *operands):
-    def spec(dims):
-        if len(dims) == 3 and dims[1] == 16:
-            return pl.BlockSpec((dims[0], 8, dims[2]), lambda i: (0, i, 0))
-        if dims == (4096, 128):
-            return pl.BlockSpec((2048, 128), lambda i: (i, 0))
-        return pl.BlockSpec(dims, lambda i: (0,) * len(dims))
-
-    return pl.pallas_call(
-        kernel,
-        grid=(2,),
-        out_shape=jax.ShapeDtypeStruct(shape, F32),
-        in_specs=[spec(v.shape) for v in operands],
-        out_specs=spec(shape),
-        compiler_params=pltpu.CompilerParams(vmem_limit_bytes=60 * 1024 * 1024),
     )(*operands)
 
 
@@ -312,40 +314,39 @@
     z_fwd, z_inv = z_tables()
     y_fwd, y_inv = y_tables()
     x_fwd, x_inv = x_tables()
-    half = lax.axis_index("ph")
-    pick = lambda table: lax.dynamic_index_in_dim(jnp.asarray(two(table)), half, 1, False)
-    lines = field.reshape(C * 8 * 16, NZ)
-
-    v = halves(z_kernel, (192, 16, 128), field.reshape(256, 16, 128), two(z_fwd))
+    block = pltpu.VMEM((C, 8, 16, NZ), F32)
+
+    hi, lo = two(z_fwd)
+    table = np.block([[hi, hi], [lo, np.zeros_like(lo)]])
+    scratch = [block, pltpu.VMEM(table.shape, BF16), pltpu.VMEM((96, 2, 16, 128), F32), pltpu.SemaphoreType.DMA((9,))]
+    v = call(z_kernel, (96, 2, 16, 128), field, table, ins=ANY, outs=ANY, scratch=scratch, limit=60)
     v = exchange(v.reshape(8, 12, 2, 16, 128), ("core", "px"))
-    v = call(y_kernel, (1152, 128), v.reshape(8, 6, 2, 2, 16, 128), pick(y_fwd))
+    v = call(y_kernel, (1152, 128), v.reshape(8, 6, 2, 2, 16, 128), two(y_fwd))
     v = exchange(v.reshape(64, 9, 2, 128), GX + ("ph",))
     v = call(x_kernel, (256, 128), v.reshape(1152, 128), two(x_fwd))
+
+    v, again = lax.optimization_barrier((v, field))
+    bias = jnp.broadcast_to(point_bias[:, None], (C, NZ))
+    cost = pl.CostEstimate(flops=800_000_000, bytes_accessed=4 << 20, transcendentals=0)
+    linear = call(point_kernel, (16, 2, 128, 128), again.reshape(C * 8 * 16, NZ), point_weight.T, bias, cost=cost)
     v = exchange(v.reshape(32, 8, 128), ("zz", "yl"))
-
-    par = (lax.axis_index("zz") % 2).astype(jnp.int32).reshape(1)
+    v, linear = lax.optimization_barrier((v, linear))
+
     expand = np.kron(np.eye(C)[GX_OF], np.ones((1, C))).astype(ml_dtypes.bfloat16)
-    v = call(
-        mix_kernel,
-        (256, 128),
-        par,
-        v.reshape(256, 128),
-        weight.transpose(0, 2, 1, 3),
-        expand,
-        scratch=[pltpu.VMEM((3, 96, 32), F32) for _ in range(4)],
-        smem=1,
-    )
+    scratch = [pltpu.VMEM((3, 96, 32), F32) for _ in range(4)]
+    v = call(mix_kernel, (256, 128), v.reshape(256, 128), weight.transpose(0, 2, 1, 3), expand, scratch=scratch)
 
     v = exchange(v.reshape(32, 8, 128), ("zz", "yl"))
     v = call(x_back_kernel, (1152, 128), v.reshape(256, 128), two(x_inv))
     v = exchange(v.reshape(64, 9, 2, 128), GX + ("ph",))
-    v = call(y_back_kernel, (8, 6, 2, 2, 16, 128), v.reshape(1152, 128), pick(y_inv))
+    v = call(y_back_kernel, (8, 6, 2, 2, 16, 128), v.reshape(1152, 128), two(y_inv))
     v = exchange(v.reshape(8, 12, 2, 16, 128), ("core", "px"))
-    bias = jnp.broadcast_to(point_bias[:, None], (C, NZ))
-    cost = pl.CostEstimate(flops=800_000_000, bytes_accessed=4 << 20, transcendentals=0)
-    linear = call(point_kernel, (4096, 128), lines, point_weight.T, bias, cost=cost)
-    out = halves(z_back_kernel, (256, 16, 128), v.reshape(192, 16, 128), linear, two(z_inv))
-    return out.reshape(C, 8, 16, NZ)
+    hi, lo = two(z_inv)
+    table = np.block([[hi, lo], [hi, np.zeros_like(lo)]])
+    scratch = [block, pltpu.SemaphoreType.DMA((4,))]
+    return call(
+        z_back_kernel, (C, 8, 16, NZ), v.reshape(96, 2, 16, 128), linear, table, outs=ANY, scratch=scratch
+    )
 
 
 def solution(mesh):

time: 159 us -> 152 us (0.956)
  blocking collectives: 43.7 us -> 126 us
  waiting for transfers between devices: 63.4 us -> 5.86 us
  starting transfers between devices: 31.3 us -> 5.38 us
  Pallas kernels: 16.9 us -> 13.3 us
    all_to_all x2 -> x5, blocking collectives: 43.7 us -> 126 us  [exchange(): return lax.all_to_all(v, axes, 0, 0, tiled=True)]
    all_to_all x4 -> x1, waiting for transfers between devices: 63.4 us -> 5.86 us  [exchange(): return lax.all_to_all(v, axes, 0, 0, tiled=True)]
    all_to_all x4 -> x1, starting transfers between devices: 31.3 us -> 5.38 us  [exchange(): return lax.all_to_all(v, axes, 0, 0, tiled=True)]
    pallas_call x2 -> x0, Pallas kernels: 9.3 us -> none  [halves(): pl.pallas_call(kernel, grid=(2,), out_shape=jax.ShapeDtypeStruct(shape, F...]
    pallas_call x6 -> x8, Pallas kernels: 7.63 us -> 13.3 us  [call(): pl.pallas_call(kernel, out_shape=jax.ShapeDtypeStruct(shape, F32), in_spe...]
  transfers between devices with their start and end apart: 4 -> 1, of which waited for: 4 -> 1; matrix products, arithmetic and copies ran while one was open for 0% -> 0% of each run, Pallas kernels for 2% -> 2%
where the time goes in v5:
time: 152 us
  blocking collectives  126 us (83%)
  Pallas kernels  13.3 us (9%)
  waiting for transfers between devices  5.86 us (4%)
  starting transfers between devices  5.38 us (4%)
  local copies, waits for them, and re-layouts  1.52 us (1%)
    all_to_all x5, blocking collectives, exchange(): return lax.all_to_all(v, axes, 0, 0, tiled=True)  126 us
    pallas_call x8, Pallas kernels, call(): pl.pallas_call(kernel, out_shape=jax.ShapeDtypeStruct(shape, F32), in_spe...  13.3 us
    all_to_all x1, waiting for transfers between devices, exchange(): return lax.all_to_all(v, axes, 0, 0, tiled=True)  5.86 us
    all_to_all x1, starting transfers between devices, exchange(): return lax.all_to_all(v, axes, 0, 0, tiled=True)  5.38 us
  transfers between devices with their start and end apart: 1, of which 1 were waited for; matrix products, arithmetic and copies ran while one was open for 0% of the time, Pallas kernels for 2%

profile of v5, /device:TPU:1, one launch (start us, length us, event | category | flops | bytes accessed | tf_op | source)
XLA Modules:
  0.0 151.8 jit_solution(15833178764552112838)
XLA Ops:
  0.0 3.8 %shard_map.109 = f32[96,2,16,128]{3,2,1,0:T(8,128)} custom-call(f32[32,8,16,128]{3,2,1,0:T(8,128)} %field.1, bf16[192,256]{1,0:T(8,128)(2,1)} %constant.14.clone.table), custom_call_target="tpu_custom_call" | custom-call | tf_op jit(solution)/shard_map/pallas_call | solution.py:298
  3.8 0.0 copy-start.5
  3.8 31.1 %all_to_all.30 = f32[8,12,2,16,128]{4,3,2,1,0:T(8,128)S(1)} all-to-all(f32[8,12,2,16,128]{4,3,2,1,0:T(8,128)} %bitcast.28), channel_id=1, replica_groups=mesh['yl'=4,'zz'=8,'px'=4,'ph'=2,'core'=2] {'core','px'}, dimensions={0} | all-to-all | bytes 3145728 | tf_op jit(solution)/shard_map/all_to_all | solution.py:310
  34.9 0.8 shard_map.110
  35.7 0.0 copy-start.10
  35.7 0.0 copy-start.11
  35.7 30.8 %all_to_all.31 = f32[64,9,2,128]{3,2,1,0:T(2,128)S(1)} all-to-all(f32[64,9,2,128]{3,2,1,0:T(2,128)S(1)} %bitcast.21), channel_id=1, replica_groups=mesh['yl'=4,'zz'=8,'px'=4,'ph'=2,'core'=2] {'yl','zz','ph'}, dimensions={0} | all-to-all | bytes 1179648 | tf_op jit(solution)/shard_map/all_to_all | solution.py:310
  66.6 1.0 shard_map.111
  67.6 5.4 %all-to-all-start.2 = ((f32[32,8,128]{2,1,0:T(8,128)}), f32[32,8,128]{2,1,0:T(8,128)S(1)}, u32[]{:S(2)}, u32[]{:S(2)}) async-start(f32[32,8,128]{2,1,0:T(8,128)} %bitcast.4), calls=%async_computation.2 | async-start | bytes 262144 | tf_op jit(solution)/shard_map/all_to_all | solution.py:310
  73.0 0.1 copy.12
  73.1 0.1 broadcast_in_dim.2.bias
  73.2 0.0 copy-start.6
  73.2 2.5 %shard_map.112.linear = f32[16,2,128,128]{3,2,1,0:T(8,128)S(1)} custom-call(f32[4096,128]{1,0:T(8,128)S(1)} %bitcast.15, f32[32,32]{1,0:T(8,128)S(1)} %bitcast.27, f32[32,128]{1,0:T(8,128)S(1)} %broadcast_in_dim.2.bias), custom_call_target="tpu_custom_call" | custom-call | flops 800000000 | bytes 4194304 | tf_op jit(solution)/shard_map/pallas_call | solution.py:298
  75.7 0.0 copy-start.1
  75.7 1.3 copy-done.1
  77.0 5.9 %all-to-all-done.2 = f32[32,8,128]{2,1,0:T(8,128)S(1)} async-done(((f32[32,8,128]{2,1,0:T(8,128)}), f32[32,8,128]{2,1,0:T(8,128)S(1)}, u32[]{:S(2)}, u32[]{:S(2)}) %all-to-all-start.2) | async-done | bytes 131104 | tf_op jit(solution)/shard_map/all_to_all | solution.py:310
  82.9 1.2 shard_map.113
  84.1 13.3 %all_to_all.32 = f32[32,8,128]{2,1,0:T(8,128)S(1)} all-to-all(f32[32,8,128]{2,1,0:T(8,128)S(1)} %bitcast.25), channel_id=1, replica_groups=mesh['yl'=4,'zz'=8,'px'=4,'ph'=2,'core'=2] {'zz','yl'}, dimensions={0} | all-to-all | bytes 262144 | tf_op jit(solution)/shard_map/all_to_all | solution.py:310
  97.4 0.4 shard_map.114
  97.8 21.4 %all_to_all.33 = f32[64,9,2,128]{3,2,1,0:T(2,128)S(1)} all-to-all(f32[64,9,2,128]{3,2,1,0:T(2,128)S(1)} %bitcast.20), channel_id=1, replica_groups=mesh['yl'=4,'zz'=8,'px'=4,'ph'=2,'core'=2] {'yl','zz','ph'}, dimensions={0} | all-to-all | bytes 1179648 | tf_op jit(solution)/shard_map/all_to_all | solution.py:310
  119.3 0.8 shard_map.115
  120.0 0.0 copy-start.8
  120.1 29.0 %all_to_all.34 = f32[8,12,2,16,128]{4,3,2,1,0:T(8,128)S(1)} all-to-all(f32[8,12,2,16,128]{4,3,2,1,0:T(8,128)S(1)} %bitcast.17), channel_id=1, replica_groups=mesh['yl'=4,'zz'=8,'px'=4,'ph'=2,'core'=2] {'core','px'}, dimensions={0} | all-to-all | bytes 3145728 | tf_op jit(solution)/shard_map/all_to_all | solution.py:310
  149.0 2.8 %shard_map.116 = f32[32,8,16,128]{3,2,1,0:T(8,128)} custom-call(f32[96,2,16,128]{3,2,1,0:T(8,128)S(1)} %bitcast.18, f32[16,2,128,128]{3,2,1,0:T(8,128)S(1)} %copy-done.2, bf16[192,256]{1,0:T(8,128)(2,1)S(1)} %copy-done.8), custom_call_target="tpu_custom_call" | custom-call | tf_op jit(solution)/shard_map/pallas_call | solution.py:298
  (17 shorter events, 0.0 us)
Async XLA Ops:
  3.8 31.1 %copy-start.5 = (bf16[2,2,128,256]{3,2,1,0:T(8,128)(2,1)S(1)}, bf16[2,2,128,256]{3,2,1,0:T(8,128)(2,1)}, u32[]{:S(2)}) copy-start(bf16[2,2,128,256]{3,2,1,0:T(8,128)(2,1)} %constant.15.clone.table) | copy-start | bytes 786436
  34.9 31.7 %copy-start.7 = (bf16[2,128,256]{2,1,0:T(8,128)(2,1)S(1)}, bf16[2,128,256]{2,1,0:T(8,128)(2,1)}, u32[]{:S(2)}) copy-start(bf16[2,128,256]{2,1,0:T(8,128)(2,1)} %constant.16.clone.table) | copy-start | bytes 393220
  35.7 37.3 %copy-start.10 = (f32[32,32]{1,0:T(8,128)S(1)}, f32[32,32]{1,0:T(8,128)}, u32[]{:S(2)}) copy-start(f32[32,32]{1,0:T(8,128)} %param.13) | copy-start | bytes 12292
  35.7 37.4 %copy-start.11 = (f32[32]{0:T(128)S(1)}, f32[32]{0:T(128)}, u32[]{:S(2)}) copy-start(f32[32]{0:T(128)} %param.14) | copy-start | bytes 388
  35.7 37.4 %copy-start = (f32[32,8,16,128]{3,2,1,0:T(8,128)S(1)}, f32[32,8,16,128]{3,2,1,0:T(8,128)}, u32[]{:S(2)}) copy-start(f32[32,8,16,128]{3,2,1,0:T(8,128)} %field.1) | copy-start | bytes 6291460
  67.6 15.3 %all-to-all-start.2 = ((f32[32,8,128]{2,1,0:T(8,128)}), f32[32,8,128]{2,1,0:T(8,128)S(1)}, u32[]{:S(2)}, u32[]{:S(2)}) async-start(f32[32,8,128]{2,1,0:T(8,128)} %bitcast.4), calls=%async_computation.2 | async-start | bytes 262144 | tf_op jit(solution)/shard_map/all_to_all | solution.py:310
  73.2 9.7 %copy-start.3 = (bf16[2,72,3,1024]{3,1,2,0:T(8,128)(2,1)S(1)}, bf16[2,72,3,1024]{3,1,2,0:T(8,128)(2,1)}, u32[]{:S(2)}) copy-start(bf16[2,72,3,1024]{3,1,2,0:T(8,128)(2,1)} %param.12) | copy-start | bytes 2654212
  73.2 9.7 %copy-start.9 = (bf16[32,1024]{1,0:T(8,128)(2,1)S(1)}, bf16[32,1024]{1,0:T(8,128)(2,1)}, u32[]{:S(2)}) copy-start(bf16[32,1024]{1,0:T(8,128)(2,1)} %constant.17.clone.expand) | copy-start | bytes 196612
  73.2 24.2 %copy-start.6 = (bf16[2,256,128]{2,1,0:T(8,128)(2,1)S(1)}, bf16[2,256,128]{2,1,0:T(8,128)(2,1)}, u32[]{:S(2)}) copy-start(bf16[2,256,128]{2,1,0:T(8,128)(2,1)} %constant.18.clone.table) | copy-start | bytes 393220
  75.7 1.3 copy-start.1
  82.9 36.4 %copy-start.4 = (bf16[2,2,256,128]{3,2,1,0:T(8,128)(2,1)S(1)}, bf16[2,2,256,128]{3,2,1,0:T(8,128)(2,1)}, u32[]{:S(2)}) copy-start(bf16[2,2,256,128]{3,2,1,0:T(8,128)(2,1)} %constant.19.clone.table) | copy-start | bytes 786436
  120.0 29.0 %copy-start.2 = (f32[16,2,128,128]{3,2,1,0:T(8,128)S(1)}, f32[16,2,128,128]{3,2,1,0:T(8,128)}, u32[]{:S(2)}) copy-start(f32[16,2,128,128]{3,2,1,0:T(8,128)} %copy-done.1) | copy-start | bytes 6291460
  120.0 29.0 %copy-start.8 = (bf16[192,256]{1,0:T(8,128)(2,1)S(1)}, bf16[192,256]{1,0:T(8,128)(2,1)}, u32[]{:S(2)}) copy-start(bf16[192,256]{1,0:T(8,128)(2,1)} %constant.20.clone.table) | copy-start | bytes 294916

commit v6 on v5

--- a/solution.py
+++ b/solution.py
@@ -41,13 +41,11 @@
     return 3 * (4 * (d % 4) + 2 * h + d // 4) + k
 
 
-def z_tables():
+def z_inverse():
     g = z_modes().reshape(-1)
     th = angle(g[:, None], np.arange(NZ)[None, :], NZ)
-    fwd = np.stack([np.cos(th), -np.sin(th)], axis=1).reshape(96, NZ)
     w = (np.where(g == 0, 1.0, 2.0) / (NX * NY * NZ))[:, None]
-    inv = np.stack([np.cos(th) * w, -np.sin(th) * w], axis=1).reshape(96, NZ)
-    return fwd, inv
+    return np.stack([np.cos(th) * w, -np.sin(th) * w], axis=1).reshape(96, NZ)
 
 
 def y_tables():
@@ -102,26 +100,40 @@
 CHUNKS = [(h, slice(4 * h, 4 * h + 4), slice(8 * i, 8 * i + 8)) for h in range(2) for i in range(2)]
 
 
-def z_kernel(field, table, out, work, t, done, sems):
-    copies = [pltpu.make_async_copy(table, t, sems.at[4])]
-    for i, (h, xs, ys) in enumerate(CHUNKS):
-        copies.append(pltpu.make_async_copy(field.at[:, xs, ys], work.at[:, xs, ys], sems.at[i]))
-    for copy in copies:
-        copy.start()
-    copies[0].wait()
-    for i, (h, xs, ys) in enumerate(CHUNKS):
-        copies[i + 1].wait()
+def z_table():
+    m = lax.broadcasted_iota(jnp.int32, (96, NZ), 0).astype(F32)
+    z = lax.broadcasted_iota(jnp.int32, (96, NZ), 1).astype(F32)
+    d = jnp.floor((m + 0.5) * np.float32(1 / 12))
+    j = jnp.floor((m - 12 * d + 0.5) * np.float32(1 / 2))
+    ri = m - 12 * d - 2 * j
+    q = jnp.floor(d * np.float32(1 / 4))
+    h = jnp.floor((j + 0.5) * np.float32(1 / 3))
+    g = 3 * (4 * (d - 4 * q) + 2 * h + q) + (j - 3 * h)
+    turns = g * z + 32 * ri
+    turns = turns - 128 * jnp.floor(turns * np.float32(1 / 128) + 0.5)
+    return jnp.cos(turns * np.float32(2 * np.pi / 128))
+
+
+def z_kernel(field, out, work, sems):
+    copies = []
+    for h in range(2):
+        xs = slice(4 * h, 4 * h + 4)
+        copies.append(pltpu.make_async_copy(field.at[:, xs], work.at[:, xs], sems.at[h]))
+        copies[h].start()
+    hi, lo = split(z_table())
+    t = jnp.concatenate(
+        [jnp.concatenate([hi, hi], axis=1), jnp.concatenate([lo, jnp.zeros_like(lo)], axis=1)], axis=0
+    )
+    for h, xs, ys in CHUNKS:
+        if ys.start == 0:
+            copies[h].wait()
         by_y = [jnp.swapaxes(work[:, 4 * h + x, ys, :], 0, 1) for x in range(4)]
         modes = []
         for y in range(8):
             a = jnp.concatenate([v[y] for v in by_y], axis=0)
-            r = dot(t[...], jnp.concatenate(split(a), axis=1), NT)
+            r = dot(t, jnp.concatenate(split(a), axis=1), NT)
             modes.append(r[:96] + r[96:])
-        done[:, h, ys, :] = jnp.swapaxes(jnp.stack(modes), 0, 1)
-        copies.append(pltpu.make_async_copy(done.at[:, h, ys], out.at[:, h, ys], sems.at[5 + i]))
-        copies[-1].start()
-    for copy in copies[5:]:
-        copy.wait()
+        out[:, h, ys, :] = jnp.swapaxes(jnp.stack(modes), 0, 1)
 
 
 def y_kernel(rows, table, out):
@@ -283,9 +295,10 @@
             cells.append(0.5 * s * (1.0 + lax.erf(s * np.float32(np.sqrt(0.5)))))
         cells = jnp.stack(cells)
         for x in range(4):
-            work[:, 4 * h + x, ys, :] = jnp.swapaxes(cells[:, 32 * x : 32 * x + 32], 0, 1)
-        copies.append(pltpu.make_async_copy(work.at[:, xs, ys], out.at[:, xs, ys], sems.at[i]))
-        copies[-1].start()
+            at = (slice(None), 4 * h + x, ys)
+            work[at] = jnp.swapaxes(cells[:, 32 * x : 32 * x + 32], 0, 1)
+            copies.append(pltpu.make_async_copy(work.at[at], out.at[at], sems.at[4 * i + x]))
+            copies[-1].start()
     for copy in copies:
         copy.wait()
 
@@ -311,15 +324,13 @@
 
 
 def on_device(field, weight, point_weight, point_bias):
-    z_fwd, z_inv = z_tables()
+    z_inv = z_inverse()
     y_fwd, y_inv = y_tables()
     x_fwd, x_inv = x_tables()
     block = pltpu.VMEM((C, 8, 16, NZ), F32)
 
-    hi, lo = two(z_fwd)
-    table = np.block([[hi, hi], [lo, np.zeros_like(lo)]])
-    scratch = [block, pltpu.VMEM(table.shape, BF16), pltpu.VMEM((96, 2, 16, 128), F32), pltpu.SemaphoreType.DMA((9,))]
-    v = call(z_kernel, (96, 2, 16, 128), field, table, ins=ANY, outs=ANY, scratch=scratch, limit=60)
+    scratch = [block, pltpu.SemaphoreType.DMA((2,))]
+    v = call(z_kernel, (96, 2, 16, 128), field, ins=ANY, scratch=scratch, limit=52)
     v = exchange(v.reshape(8, 12, 2, 16, 128), ("core", "px"))
     v = call(y_kernel, (1152, 128), v.reshape(8, 6, 2, 2, 16, 128), two(y_fwd))
     v = exchange(v.reshape(64, 9, 2, 128), GX + ("ph",))
@@ -343,7 +354,7 @@
     v = exchange(v.reshape(8, 12, 2, 16, 128), ("core", "px"))
     hi, lo = two(z_inv)
     table = np.block([[hi, lo], [hi, np.zeros_like(lo)]])
-    scratch = [block, pltpu.SemaphoreType.DMA((4,))]
+    scratch = [block, pltpu.SemaphoreType.DMA((16,))]
     return call(
         z_back_kernel, (C, 8, 16, NZ), v.reshape(96, 2, 16, 128), linear, table, outs=ANY, scratch=scratch
     )

time: 152 us -> 151 us (level)
  no operation moved by 1% of the time
where the time goes in v6:
time: 151 us; the launch traced here: 150 us
  blocking collectives  125 us (83%)
  Pallas kernels  11.9 us (8%)
  waiting for transfers between devices  5.88 us (4%)
  starting transfers between devices  5.38 us (4%)
  local copies, waits for them, and re-layouts  1.52 us (1%)
    all_to_all x5, blocking collectives, exchange(): return lax.all_to_all(v, axes, 0, 0, tiled=True)  125 us
    pallas_call x8, Pallas kernels, call(): pl.pallas_call(kernel, out_shape=jax.ShapeDtypeStruct(shape, F32), in_spe...  11.9 us
    all_to_all x1, waiting for transfers between devices, exchange(): return lax.all_to_all(v, axes, 0, 0, tiled=True)  5.88 us
    all_to_all x1, starting transfers between devices, exchange(): return lax.all_to_all(v, axes, 0, 0, tiled=True)  5.38 us
  transfers between devices with their start and end apart: 1, of which 1 were waited for; matrix products, arithmetic and copies ran while one was open for 0% of the time, Pallas kernels for 2%

profile of v6, /device:TPU:1, one launch (start us, length us, event | category | flops | bytes accessed | tf_op | source)
XLA Modules:
  0.0 150.2 jit_solution(17358542308512237066)
XLA Ops:
  0.0 2.7 %shard_map.100 = f32[96,2,16,128]{3,2,1,0:T(8,128)S(1)} custom-call(f32[32,8,16,128]{3,2,1,0:T(8,128)} %field.1), custom_call_target="tpu_custom_call" | custom-call | tf_op jit(solution)/shard_map/pallas_call | solution.py:311
  2.7 0.0 copy-start.5
  2.7 30.0 %all_to_all.30 = f32[8,12,2,16,128]{4,3,2,1,0:T(8,128)S(1)} all-to-all(f32[8,12,2,16,128]{4,3,2,1,0:T(8,128)S(1)} %bitcast.18), channel_id=1, replica_groups=mesh['yl'=4,'zz'=8,'px'=4,'ph'=2,'core'=2] {'core','px'}, dimensions={0} | all-to-all | bytes 3145728 | tf_op jit(solution)/shard_map/all_to_all | solution.py:323
  32.7 0.8 shard_map.101
  33.5 0.0 copy-start.10
  33.5 0.0 copy-start.11
  33.6 31.7 %all_to_all.31 = f32[64,9,2,128]{3,2,1,0:T(2,128)S(1)} all-to-all(f32[64,9,2,128]{3,2,1,0:T(2,128)S(1)} %bitcast.22), channel_id=1, replica_groups=mesh['yl'=4,'zz'=8,'px'=4,'ph'=2,'core'=2] {'yl','zz','ph'}, dimensions={0} | all-to-all | bytes 1179648 | tf_op jit(solution)/shard_map/all_to_all | solution.py:323
  65.2 1.0 shard_map.102
  66.3 5.4 %all-to-all-start.2 = ((f32[32,8,128]{2,1,0:T(8,128)}), f32[32,8,128]{2,1,0:T(8,128)S(1)}, u32[]{:S(2)}, u32[]{:S(2)}) async-start(f32[32,8,128]{2,1,0:T(8,128)} %bitcast.4), calls=%async_computation.2 | async-start | bytes 262144 | tf_op jit(solution)/shard_map/all_to_all | solution.py:323
  71.7 0.1 copy.11
  71.8 0.1 broadcast_in_dim.2.bias
  71.8 0.0 copy-start.6
  71.8 2.5 %shard_map.103.linear = f32[16,2,128,128]{3,2,1,0:T(8,128)S(1)} custom-call(f32[4096,128]{1,0:T(8,128)S(1)} %bitcast.15, f32[32,32]{1,0:T(8,128)S(1)} %bitcast.28, f32[32,128]{1,0:T(8,128)S(1)} %broadcast_in_dim.2.bias), custom_call_target="tpu_custom_call" | custom-call | flops 800000000 | bytes 4194304 | tf_op jit(solution)/shard_map/pallas_call | solution.py:311
  74.4 0.0 copy-start.1
  74.4 1.3 copy-done.1
  75.7 5.9 %all-to-all-done.2 = f32[32,8,128]{2,1,0:T(8,128)S(1)} async-done(((f32[32,8,128]{2,1,0:T(8,128)}), f32[32,8,128]{2,1,0:T(8,128)S(1)}, u32[]{:S(2)}, u32[]{:S(2)}) %all-to-all-start.2) | async-done | bytes 131104 | tf_op jit(solution)/shard_map/all_to_all | solution.py:323
  81.6 1.2 shard_map.104
  82.8 13.3 %all_to_all.32 = f32[32,8,128]{2,1,0:T(8,128)S(1)} all-to-all(f32[32,8,128]{2,1,0:T(8,128)S(1)} %bitcast.26), channel_id=1, replica_groups=mesh['yl'=4,'zz'=8,'px'=4,'ph'=2,'core'=2] {'zz','yl'}, dimensions={0} | all-to-all | bytes 262144 | tf_op jit(solution)/shard_map/all_to_all | solution.py:323
  96.0 0.4 shard_map.105
  96.5 21.4 %all_to_all.33 = f32[64,9,2,128]{3,2,1,0:T(2,128)S(1)} all-to-all(f32[64,9,2,128]{3,2,1,0:T(2,128)S(1)} %bitcast.21), channel_id=1, replica_groups=mesh['yl'=4,'zz'=8,'px'=4,'ph'=2,'core'=2] {'yl','zz','ph'}, dimensions={0} | all-to-all | bytes 1179648 | tf_op jit(solution)/shard_map/all_to_all | solution.py:323
  117.9 0.8 shard_map.106
  118.7 0.0 copy-start.8
  118.7 29.0 %all_to_all.34 = f32[8,12,2,16,128]{4,3,2,1,0:T(8,128)S(1)} all-to-all(f32[8,12,2,16,128]{4,3,2,1,0:T(8,128)S(1)} %bitcast.17), channel_id=1, replica_groups=mesh['yl'=4,'zz'=8,'px'=4,'ph'=2,'core'=2] {'core','px'}, dimensions={0} | all-to-all | bytes 3145728 | tf_op jit(solution)/shard_map/all_to_all | solution.py:323
  147.7 2.6 %shard_map.107 = f32[32,8,16,128]{3,2,1,0:T(8,128)} custom-call(f32[96,2,16,128]{3,2,1,0:T(8,128)S(1)} %bitcast.19, f32[16,2,128,128]{3,2,1,0:T(8,128)S(1)} %copy-done.2, bf16[192,256]{1,0:T(8,128)(2,1)S(1)} %copy-done.8), custom_call_target="tpu_custom_call" | custom-call | tf_op jit(solution)/shard_map/pallas_call | solution.py:311
  (17 shorter events, 0.0 us)
Async XLA Ops:
  2.7 30.1 %copy-start.5 = (bf16[2,2,128,256]{3,2,1,0:T(8,128)(2,1)S(1)}, bf16[2,2,128,256]{3,2,1,0:T(8,128)(2,1)}, u32[]{:S(2)}) copy-start(bf16[2,2,128,256]{3,2,1,0:T(8,128)(2,1)} %constant.12.clone.table) | copy-start | bytes 786436
  32.7 32.5 %copy-start.7 = (bf16[2,128,256]{2,1,0:T(8,128)(2,1)S(1)}, bf16[2,128,256]{2,1,0:T(8,128)(2,1)}, u32[]{:S(2)}) copy-start(bf16[2,128,256]{2,1,0:T(8,128)(2,1)} %constant.13.clone.table) | copy-start | bytes 393220
  33.5 38.1 %copy-start.10 = (f32[32,32]{1,0:T(8,128)S(1)}, f32[32,32]{1,0:T(8,128)}, u32[]{:S(2)}) copy-start(f32[32,32]{1,0:T(8,128)} %param.12) | copy-start | bytes 12292
  33.5 38.2 %copy-start.11 = (f32[32]{0:T(128)S(1)}, f32[32]{0:T(128)}, u32[]{:S(2)}) copy-start(f32[32]{0:T(128)} %param.13) | copy-start | bytes 388
  33.5 38.3 %copy-start = (f32[32,8,16,128]{3,2,1,0:T(8,128)S(1)}, f32[32,8,16,128]{3,2,1,0:T(8,128)}, u32[]{:S(2)}) copy-start(f32[32,8,16,128]{3,2,1,0:T(8,128)} %field.1) | copy-start | bytes 6291460
  66.3 15.3 %all-to-all-start.2 = ((f32[32,8,128]{2,1,0:T(8,128)}), f32[32,8,128]{2,1,0:T(8,128)S(1)}, u32[]{:S(2)}, u32[]{:S(2)}) async-start(f32[32,8,128]{2,1,0:T(8,128)} %bitcast.4), calls=%async_computation.2 | async-start | bytes 262144 | tf_op jit(solution)/shard_map/all_to_all | solution.py:323
  71.8 9.8 %copy-start.3 = (bf16[2,72,3,1024]{3,1,2,0:T(8,128)(2,1)S(1)}, bf16[2,72,3,1024]{3,1,2,0:T(8,128)(2,1)}, u32[]{:S(2)}) copy-start(bf16[2,72,3,1024]{3,1,2,0:T(8,128)(2,1)} %param.11) | copy-start | bytes 2654212
  71.8 9.8 %copy-start.9 = (bf16[32,1024]{1,0:T(8,128)(2,1)S(1)}, bf16[32,1024]{1,0:T(8,128)(2,1)}, u32[]{:S(2)}) copy-start(bf16[32,1024]{1,0:T(8,128)(2,1)} %constant.14.clone.expand) | copy-start | bytes 196612
  71.8 24.2 %copy-start.6 = (bf16[2,256,128]{2,1,0:T(8,128)(2,1)S(1)}, bf16[2,256,128]{2,1,0:T(8,128)(2,1)}, u32[]{:S(2)}) copy-start(bf16[2,256,128]{2,1,0:T(8,128)(2,1)} %constant.15.clone.table) | copy-start | bytes 393220
  74.4 1.3 copy-start.1
  81.6 36.3 %copy-start.4 = (bf16[2,2,256,128]{3,2,1,0:T(8,128)(2,1)S(1)}, bf16[2,2,256,128]{3,2,1,0:T(8,128)(2,1)}, u32[]{:S(2)}) copy-start(bf16[2,2,256,128]{3,2,1,0:T(8,128)(2,1)} %constant.16.clone.table) | copy-start | bytes 786436
  118.7 29.0 %copy-start.2 = (f32[16,2,128,128]{3,2,1,0:T(8,128)S(1)}, f32[16,2,128,128]{3,2,1,0:T(8,128)}, u32[]{:S(2)}) copy-start(f32[16,2,128,128]{3,2,1,0:T(8,128)} %copy-done.1) | copy-start | bytes 6291460
  118.7 29.0 %copy-start.8 = (bf16[192,256]{1,0:T(8,128)(2,1)S(1)}, bf16[192,256]{1,0:T(8,128)(2,1)}, u32[]{:S(2)}) copy-start(bf16[192,256]{1,0:T(8,128)(2,1)} %constant.17.clone.table) | copy-start | bytes 294916

commit v7 on v6

--- a/solution.py
+++ b/solution.py
@@ -136,7 +136,18 @@
         out[:, h, ys, :] = jnp.swapaxes(jnp.stack(modes), 0, 1)
 
 
-def y_kernel(rows, table, out):
+def point(field, weight, bias, linear):
+    w = jnp.concatenate([jnp.concatenate([weight[...]] * 8, axis=1)] * 8, axis=0)
+    row = lax.broadcasted_iota(jnp.int32, (256, 256), 0) // 32
+    col = lax.broadcasted_iota(jnp.int32, (256, 256), 1) // 32
+    w = split(jnp.where(row == col, w, 0.0).T)
+    b = jnp.broadcast_to(bias[...].reshape(1, 32), (NZ, 32)).T
+    b = jnp.concatenate([b] * 8, axis=0)
+    for y in range(16):
+        linear[y] = (dot3(w, split(lines_at(field, y))) + b).reshape(2, 128, 128)
+
+
+def y_kernel(rows, table, field, weight, bias, out, linear):
     half = lax.axis_index("ph")
     t = (table[0, half], table[1, half])
     for h in range(2):
@@ -166,6 +177,10 @@
                 axis=0,
             )
             out[pl.ds(h * 18 + 16 + xh, 32, stride=36), :] = v.T
+
+    @pl.when(lax.axis_index("core") == 0)
+    def _():
+        point(field, weight, bias, linear)
 
 
 def turn(v):
@@ -253,7 +268,7 @@
                 out[pl.ds(h * 18 + k * 8 + x, 32, stride=36), :] = s[x]
 
 
-def y_back_kernel(rows, table, out):
+def y_back_kernel(rows, table, field, weight, bias, out, linear):
     half = lax.axis_index("ph")
     t = (table[0, half], table[1, half])
     lane = lax.broadcasted_iota(jnp.int32, (256, 128), 1) % B
@@ -272,26 +287,22 @@
                     part = r[ri * 128 : ri * 128 + 128, half * 128 : half * 128 + 128]
                     out[:, 3 * h + k, ri, half] = part.reshape(8, 16, 128)
 
-
-def point_kernel(field, weight, bias, out):
-    w = jnp.concatenate([jnp.concatenate([weight[...]] * 8, axis=1)] * 8, axis=0)
-    row = lax.broadcasted_iota(jnp.int32, (256, 256), 0) // 32
-    col = lax.broadcasted_iota(jnp.int32, (256, 256), 1) // 32
-    w = split(jnp.where(row == col, w, 0.0))
-    b = jnp.concatenate([bias[...]] * 8, axis=0)
-    for y in range(16):
-        out[y] = (dot3(w, split(lines_at(field, y))) + b).reshape(2, 128, 128)
-
-
-def z_back_kernel(rows, linear, table, out, work, sems):
+    @pl.when(lax.axis_index("core") == 1)
+    def _():
+        point(field, weight, bias, linear)
+
+
+def z_back_kernel(rows, linear_0, linear_1, table, out, work, sems):
     t = table[...]
+    first = lax.axis_index("core") == 0
     copies = []
     for i, (h, xs, ys) in enumerate(CHUNKS):
         by_y = jnp.swapaxes(rows[:, h, ys, :], 0, 1)
         cells = []
         for y in range(8):
             r = dot(jnp.concatenate(split(by_y[y]), axis=0).T, t)
-            s = r[:, :128] + r[:, 128:] + linear[ys.start + y, h]
+            at = (ys.start + y, h)
+            s = r[:, :128] + r[:, 128:] + jnp.where(first, linear_0[at], linear_1[at])
             cells.append(0.5 * s * (1.0 + lax.erf(s * np.float32(np.sqrt(0.5)))))
         cells = jnp.stack(cells)
         for x in range(4):
@@ -307,16 +318,17 @@
 ANY = pl.BlockSpec(memory_space=pl.ANY)
 
 
-def call(kernel, shape, *operands, ins=VMEM, outs=VMEM, scratch=(), limit=24, cost=None):
-    return pl.pallas_call(
+def call(kernel, shape, *operands, ins=VMEM, outs=VMEM, scratch=(), limit=24):
+    shapes = shape if isinstance(shape, list) else [shape]
+    result = pl.pallas_call(
         kernel,
-        out_shape=jax.ShapeDtypeStruct(shape, F32),
+        out_shape=[jax.ShapeDtypeStruct(dims, F32) for dims in shapes],
         in_specs=[ins] * len(operands),
-        out_specs=outs,
+        out_specs=[outs] * len(shapes),
         scratch_shapes=list(scratch),
         compiler_params=pltpu.CompilerParams(vmem_limit_bytes=limit * 1024 * 1024),
-        cost_estimate=cost,
     )(*operands)
+    return result if isinstance(shape, list) else result[0]
 
 
 def exchange(v, axes):
@@ -332,16 +344,15 @@
     scratch = [block, pltpu.SemaphoreType.DMA((2,))]
     v = call(z_kernel, (96, 2, 16, 128), field, ins=ANY, scratch=scratch, limit=52)
     v = exchange(v.reshape(8, 12, 2, 16, 128), ("core", "px"))
-    v = call(y_kernel, (1152, 128), v.reshape(8, 6, 2, 2, 16, 128), two(y_fwd))
+    lines = field.reshape(C * 8 * 16, NZ)
+    mixing = (lines, point_weight, point_bias)
+    mixed = (16, 2, 128, 128)
+    v = v.reshape(8, 6, 2, 2, 16, 128)
+    v, linear_0 = call(y_kernel, [(1152, 128), mixed], v, two(y_fwd), *mixing)
     v = exchange(v.reshape(64, 9, 2, 128), GX + ("ph",))
     v = call(x_kernel, (256, 128), v.reshape(1152, 128), two(x_fwd))
 
-    v, again = lax.optimization_barrier((v, field))
-    bias = jnp.broadcast_to(point_bias[:, None], (C, NZ))
-    cost = pl.CostEstimate(flops=800_000_000, bytes_accessed=4 << 20, transcendentals=0)
-    linear = call(point_kernel, (16, 2, 128, 128), again.reshape(C * 8 * 16, NZ), point_weight.T, bias, cost=cost)
     v = exchange(v.reshape(32, 8, 128), ("zz", "yl"))
-    v, linear = lax.optimization_barrier((v, linear))
 
     expand = np.kron(np.eye(C)[GX_OF], np.ones((1, C))).astype(ml_dtypes.bfloat16)
     scratch = [pltpu.VMEM((3, 96, 32), F32) for _ in range(4)]
@@ -350,14 +361,14 @@
     v = exchange(v.reshape(32, 8, 128), ("zz", "yl"))
     v = call(x_back_kernel, (1152, 128), v.reshape(256, 128), two(x_inv))
     v = exchange(v.reshape(64, 9, 2, 128), GX + ("ph",))
-    v = call(y_back_kernel, (8, 6, 2, 2, 16, 128), v.reshape(1152, 128), two(y_inv))
+    v = v.reshape(1152, 128)
+    v, linear_1 = call(y_back_kernel, [(8, 6, 2, 2, 16, 128), mixed], v, two(y_inv), *mixing)
     v = exchange(v.reshape(8, 12, 2, 16, 128), ("core", "px"))
     hi, lo = two(z_inv)
     table = np.block([[hi, lo], [hi, np.zeros_like(lo)]])
     scratch = [block, pltpu.SemaphoreType.DMA((16,))]
-    return call(
-        z_back_kernel, (C, 8, 16, NZ), v.reshape(96, 2, 16, 128), linear, table, outs=ANY, scratch=scratch
-    )
+    v = v.reshape(96, 2, 16, 128)
+    return call(z_back_kernel, (C, 8, 16, NZ), v, linear_0, linear_1, table, outs=ANY, scratch=scratch)
 
 
 def solution(mesh):

time: 151 us -> 148 us (0.980)
  blocking collectives: 125 us -> 136 us
  waiting for transfers between devices: 5.88 us -> 0 us
  starting transfers between devices: 5.38 us -> 0 us
    all_to_all x5 -> x6, blocking collectives: 125 us -> 136 us  [exchange(): return lax.all_to_all(v, axes, 0, 0, tiled=True)]
    all_to_all x1 -> x0, waiting for transfers between devices: 5.88 us -> none  [exchange(): return lax.all_to_all(v, axes, 0, 0, tiled=True)]
    all_to_all x1 -> x0, starting transfers between devices: 5.38 us -> none  [exchange(): return lax.all_to_all(v, axes, 0, 0, tiled=True)]
    pallas_call x8 -> x7, Pallas kernels: 11.9 us -> 11.7 us  [call(): pl.pallas_call(kernel, out_shape=[jax.ShapeDtypeStruct(dims, F32) for dim...]
  transfers between devices with their start and end apart: 1 -> 0, of which waited for: 1 -> 0; matrix products, arithmetic and copies ran while one was open for 0% -> 0% of each run, Pallas kernels for 2% -> 0%
where the time goes in v7:
time: 148 us
  blocking collectives  136 us (92%)
  Pallas kernels  11.7 us (8%)
    all_to_all x6, blocking collectives, exchange(): return lax.all_to_all(v, axes, 0, 0, tiled=True)  136 us
    pallas_call x7, Pallas kernels, call(): pl.pallas_call(kernel, out_shape=[jax.ShapeDtypeStruct(dims, F32) for dim...  11.7 us

profile of v7, /device:TPU:1, one launch (start us, length us, event | category | flops | bytes accessed | tf_op | source)
XLA Modules:
  0.0 148.0 jit_solution(16194454706550363322)
XLA Ops:
  0.0 2.7 %shard_map.100 = f32[96,2,16,128]{3,2,1,0:T(8,128)S(1)} custom-call(f32[32,8,16,128]{3,2,1,0:T(8,128)} %field.1), custom_call_target="tpu_custom_call" | custom-call | tf_op jit(solution)/shard_map/pallas_call | solution.py:323
  2.7 0.0 copy-start
  2.7 0.0 copy-start.3
  2.7 0.0 copy-start.7
  2.7 0.0 copy-start.9
  2.7 30.0 %all_to_all.30 = f32[8,12,2,16,128]{4,3,2,1,0:T(8,128)S(1)} all-to-all(f32[8,12,2,16,128]{4,3,2,1,0:T(8,128)S(1)} %bitcast.17), channel_id=1, replica_groups=mesh['yl'=4,'zz'=8,'px'=4,'ph'=2,'core'=2] {'core','px'}, dimensions={0} | all-to-all | bytes 3145728 | tf_op jit(solution)/shard_map/all_to_all | solution.py:335
  32.8 0.0 copy-done.7
  32.8 0.0 copy-start.5
  32.8 0.8 shard_map.101
  33.6 0.0 copy-start.1
  33.6 0.0 copy-start.8
  33.6 0.0 copy-start.4
  33.6 29.1 %all_to_all.31 = f32[64,9,2,128]{3,2,1,0:T(2,128)S(1)} all-to-all(f32[64,9,2,128]{3,2,1,0:T(2,128)S(1)} %bitcast.24), channel_id=1, replica_groups=mesh['yl'=4,'zz'=8,'px'=4,'ph'=2,'core'=2] {'yl','zz','ph'}, dimensions={0} | all-to-all | bytes 1179648 | tf_op jit(solution)/shard_map/all_to_all | solution.py:335
  62.7 0.4 shard_map.102
  63.1 0.0 copy-start.2
  63.1 15.8 %all_to_all.32 = f32[32,8,128]{2,1,0:T(8,128)S(1)} all-to-all(f32[32,8,128]{2,1,0:T(8,128)S(1)} %bitcast.27), channel_id=1, replica_groups=mesh['yl'=4,'zz'=8,'px'=4,'ph'=2,'core'=2] {'zz','yl'}, dimensions={0} | all-to-all | bytes 262144 | tf_op jit(solution)/shard_map/all_to_all | solution.py:335
  78.9 1.2 shard_map.103
  80.1 12.8 %all_to_all.33 = f32[32,8,128]{2,1,0:T(8,128)S(1)} all-to-all(f32[32,8,128]{2,1,0:T(8,128)S(1)} %bitcast.26), channel_id=1, replica_groups=mesh['yl'=4,'zz'=8,'px'=4,'ph'=2,'core'=2] {'zz','yl'}, dimensions={0} | all-to-all | bytes 262144 | tf_op jit(solution)/shard_map/all_to_all | solution.py:335
  92.9 0.4 shard_map.104
  93.3 21.2 %all_to_all.34 = f32[64,9,2,128]{3,2,1,0:T(2,128)S(1)} all-to-all(f32[64,9,2,128]{3,2,1,0:T(2,128)S(1)} %bitcast.21), channel_id=1, replica_groups=mesh['yl'=4,'zz'=8,'px'=4,'ph'=2,'core'=2] {'yl','zz','ph'}, dimensions={0} | all-to-all | bytes 1179648 | tf_op jit(solution)/shard_map/all_to_all | solution.py:335
  114.5 3.6 %shard_map.105 = (f32[8,6,2,2,16,128]{5,4,3,2,1,0:T(8,128)S(1)}, f32[16,2,128,128]{3,2,1,0:T(8,128)S(1)}) custom-call(f32[1152,128]{1,0:T(8,128)S(1)} %bitcast.19, bf16[2,2,256,128]{3,2,1,0:T(8,128)(2,1)S(1)} %copy-done.2, f32[4096,128]{1,0:T(8,128)S(1)} %bitcast.15, f32[32,32]{1,0:T(8,128)S(1)} %copy-done.7, f32[32]{0:T(128)S(1)} %copy-done.9), custom_call_target="tpu_custom_call" | custom-call | tf_op jit(solution)/shard_map/pallas_call | solution.py:323
  118.1 0.0 copy-start.6
  118.1 27.0 %all_to_all.35 = f32[8,12,2,16,128]{4,3,2,1,0:T(8,128)S(1)} all-to-all(f32[8,12,2,16,128]{4,3,2,1,0:T(8,128)S(1)} %bitcast.22), channel_id=1, replica_groups=mesh['yl'=4,'zz'=8,'px'=4,'ph'=2,'core'=2] {'core','px'}, dimensions={0} | all-to-all | bytes 3145728 | tf_op jit(solution)/shard_map/all_to_all | solution.py:335
  145.1 2.7 %shard_map.106 = f32[32,8,16,128]{3,2,1,0:T(8,128)} custom-call(f32[96,2,16,128]{3,2,1,0:T(8,128)S(1)} %bitcast.18, f32[16,2,128,128]{3,2,1,0:T(8,128)S(1)} %get-tuple-element.11.linear_0, f32[16,2,128,128]{3,2,1,0:T(8,128)S(1)} %get-tuple-element.12.linear_1, bf16[192,256]{1,0:T(8,128)(2,1)S(1)} %copy-done.6), custom_call_target="tpu_custom_call" | custom-call | tf_op jit(solution)/shard_map/pallas_call | solution.py:323
  (9 shorter events, 0.0 us)
Async XLA Ops:
  2.7 30.1 %copy-start = (f32[32,8,16,128]{3,2,1,0:T(8,128)S(1)}, f32[32,8,16,128]{3,2,1,0:T(8,128)}, u32[]{:S(2)}) copy-start(f32[32,8,16,128]{3,2,1,0:T(8,128)} %field.1) | copy-start | bytes 6291460
  2.7 30.1 %copy-start.3 = (bf16[2,2,128,256]{3,2,1,0:T(8,128)(2,1)S(1)}, bf16[2,2,128,256]{3,2,1,0:T(8,128)(2,1)}, u32[]{:S(2)}) copy-start(bf16[2,2,128,256]{3,2,1,0:T(8,128)(2,1)} %constant.12.clone.table) | copy-start | bytes 786436
  2.7 30.1 %copy-start.7 = (f32[32,32]{1,0:T(8,128)S(1)}, f32[32,32]{1,0:T(8,128)}, u32[]{:S(2)}) copy-start(f32[32,32]{1,0:T(8,128)} %weight.3) | copy-start | bytes 12292
  2.7 30.1 %copy-start.9 = (f32[32]{0:T(128)S(1)}, f32[32]{0:T(128)}, u32[]{:S(2)}) copy-start(f32[32]{0:T(128)} %bias.3) | copy-start | bytes 388
  32.8 29.9 %copy-start.5 = (bf16[2,128,256]{2,1,0:T(8,128)(2,1)S(1)}, bf16[2,128,256]{2,1,0:T(8,128)(2,1)}, u32[]{:S(2)}) copy-start(bf16[2,128,256]{2,1,0:T(8,128)(2,1)} %constant.13.clone.table) | copy-start | bytes 393220
  33.6 45.3 %copy-start.1 = (bf16[2,72,3,1024]{3,1,2,0:T(8,128)(2,1)S(1)}, bf16[2,72,3,1024]{3,1,2,0:T(8,128)(2,1)}, u32[]{:S(2)}) copy-start(bf16[2,72,3,1024]{3,1,2,0:T(8,128)(2,1)} %param.11) | copy-start | bytes 2654212
  33.6 45.3 %copy-start.8 = (bf16[32,1024]{1,0:T(8,128)(2,1)S(1)}, bf16[32,1024]{1,0:T(8,128)(2,1)}, u32[]{:S(2)}) copy-start(bf16[32,1024]{1,0:T(8,128)(2,1)} %constant.14.clone.expand) | copy-start | bytes 196612
  33.6 59.2 %copy-start.4 = (bf16[2,256,128]{2,1,0:T(8,128)(2,1)S(1)}, bf16[2,256,128]{2,1,0:T(8,128)(2,1)}, u32[]{:S(2)}) copy-start(bf16[2,256,128]{2,1,0:T(8,128)(2,1)} %constant.15.clone.table) | copy-start | bytes 393220
  63.1 51.4 %copy-start.2 = (bf16[2,2,256,128]{3,2,1,0:T(8,128)(2,1)S(1)}, bf16[2,2,256,128]{3,2,1,0:T(8,128)(2,1)}, u32[]{:S(2)}) copy-start(bf16[2,2,256,128]{3,2,1,0:T(8,128)(2,1)} %constant.16.clone.table) | copy-start | bytes 786436
  118.1 27.0 %copy-start.6 = (bf16[192,256]{1,0:T(8,128)(2,1)S(1)}, bf16[192,256]{1,0:T(8,128)(2,1)}, u32[]{:S(2)}) copy-start(bf16[192,256]{1,0:T(8,128)(2,1)} %constant.17.clone.table) | copy-start | bytes 294916

commit v8 on v7

--- a/solution.py
+++ b/solution.py
@@ -70,7 +70,7 @@
 
 def x_tables():
     f = freq(x_rows().reshape(-1))
-    pos = (8 * np.arange(32)[None, :] + np.arange(8)[:, None]).reshape(-1)
+    pos = (8 * GX_OF[None, :] + np.arange(8)[:, None]).reshape(-1)
     th = angle(f[:, None], pos[None, :], NX)
     fwd = np.concatenate([np.cos(th), np.sin(th)])
     inv = np.concatenate([np.cos(th), np.sin(th)]).T
@@ -166,7 +166,7 @@
             v = jnp.concatenate([r[k][:48], r[2][16 * k : 16 * k + 16], r[k][64:112], r[2][64 + 16 * k : 80 + 16 * k]], axis=0)
             v = v.T
             for x in range(8):
-                out[pl.ds(h * 18 + k * 8 + x, 32, stride=36), :] = v[32 * x : 32 * x + 32]
+                out[pl.ds(h * 576 + k * 8 + x, 32, stride=18), :] = v[32 * x : 32 * x + 32]
         for xh in range(2):
             v = jnp.concatenate(
                 [
@@ -176,7 +176,7 @@
                 ],
                 axis=0,
             )
-            out[pl.ds(h * 18 + 16 + xh, 32, stride=36), :] = v.T
+            out[pl.ds(h * 576 + 16 + xh, 32, stride=18), :] = v.T
 
     @pl.when(lax.axis_index("core") == 0)
     def _():
@@ -191,7 +191,7 @@
 
 def x_kernel(rows, table, out):
     t = (table[0], table[1])
-    at = lambda r: rows[pl.ds(r, 32, stride=36), :] + rows[pl.ds(18 + r, 32, stride=36), :]
+    at = lambda r: rows[pl.ds(r, 32, stride=18), :] + rows[pl.ds(576 + r, 32, stride=18), :]
     last = [at(16), at(17)]
     for k in range(3):
         if k < 2:
@@ -201,16 +201,14 @@
         r = dot3(t, split(jnp.concatenate(s, axis=0)))
         m = r[:64] + turn(r[64:])
         for a in range(2):
-            out[pl.ds(2 * k + a, 32, stride=8), :] = m[32 * a : 32 * a + 32]
-    for a in range(6, 8):
-        out[pl.ds(a, 32, stride=8), :] = jnp.zeros((32, 128), F32)
+            out[pl.ds(2 * k + a, 32, stride=6), :] = m[32 * a : 32 * a + 32]
 
 
 def mix_kernel(modes, w, expand, out, in_re, in_im, mid_re, mid_im):
     start = pl.multiple_of(lax.axis_index("zz") % 2 * 24, 8)
     e = expand[...]
     for a in range(2):
-        v = [modes[pl.ds(2 * k + a, 32, stride=8), :].T for k in range(3)]
+        v = [modes[pl.ds(2 * k + a, 32, stride=6), :].T for k in range(3)]
         for ref, o in ((in_re, 0), (in_im, B)):
             for k in range(2):
                 ref[k, a * 48 : a * 48 + 48, :] = v[k][o : o + 48]
@@ -242,17 +240,14 @@
                 else:
                     v += [ref[2, a * 48 + 32 : a * 48 + 48, :], pad]
             v = jnp.concatenate(v, axis=0).T
-            for yl in range(4):
-                out[pl.ds(8 * yl + 2 * k + a, 8, stride=32), :] = v[8 * yl : 8 * yl + 8]
-    for a in range(6, 8):
-        out[pl.ds(a, 32, stride=8), :] = jnp.zeros((32, 128), F32)
+            out[pl.ds(2 * k + a, 32, stride=6), :] = v
 
 
 def x_back_kernel(modes, table, out):
     t = (table[0], table[1])
     lane = lax.broadcasted_iota(jnp.int32, (32, 128), 1) % B
     for k in range(3):
-        v = jnp.concatenate([modes[pl.ds(2 * k + a, 32, stride=8), :] for a in range(2)], axis=0)
+        v = jnp.concatenate([modes[pl.ds(2 * k + a, 32, stride=6), :] for a in range(2)], axis=0)
         r = dot3(t, split(jnp.concatenate([v, -turn(v)], axis=0)))
         s = [r[32 * x : 32 * x + 32] for x in range(8)]
         if k == 2:
@@ -265,7 +260,7 @@
             s = packed
         for x in range(len(s)):
             for h in range(2):
-                out[pl.ds(h * 18 + k * 8 + x, 32, stride=36), :] = s[x]
+                out[pl.ds(h * 576 + k * 8 + x, 32, stride=18), :] = s[x]
 
 
 def y_back_kernel(rows, table, field, weight, bias, out, linear):
@@ -273,7 +268,7 @@
     t = (table[0, half], table[1, half])
     lane = lax.broadcasted_iota(jnp.int32, (256, 128), 1) % B
     for h in range(2):
-        at = lambda r: rows[pl.ds(h * 18 + r, 32, stride=36), :]
+        at = lambda r: rows[pl.ds(h * 576 + r, 32, stride=18), :]
         v = [jnp.concatenate([at(8 * k + x) for x in range(8)], axis=0) for k in range(2)]
         last = [at(16), at(17)]
         v.append(
@@ -349,18 +344,18 @@
     mixed = (16, 2, 128, 128)
     v = v.reshape(8, 6, 2, 2, 16, 128)
     v, linear_0 = call(y_kernel, [(1152, 128), mixed], v, two(y_fwd), *mixing)
-    v = exchange(v.reshape(64, 9, 2, 128), GX + ("ph",))
-    v = call(x_kernel, (256, 128), v.reshape(1152, 128), two(x_fwd))
-
-    v = exchange(v.reshape(32, 8, 128), ("zz", "yl"))
-
-    expand = np.kron(np.eye(C)[GX_OF], np.ones((1, C))).astype(ml_dtypes.bfloat16)
+    v = exchange(v.reshape(64, 9, 2, 128), ("ph", "zz", "yl"))
+    v = call(x_kernel, (192, 128), v.reshape(1152, 128), two(x_fwd))
+
+    v = exchange(v.reshape(32, 3, 2, 128), ("zz", "yl"))
+
+    expand = np.kron(np.eye(C), np.ones((1, C))).astype(ml_dtypes.bfloat16)
     scratch = [pltpu.VMEM((3, 96, 32), F32) for _ in range(4)]
-    v = call(mix_kernel, (256, 128), v.reshape(256, 128), weight.transpose(0, 2, 1, 3), expand, scratch=scratch)
-
-    v = exchange(v.reshape(32, 8, 128), ("zz", "yl"))
-    v = call(x_back_kernel, (1152, 128), v.reshape(256, 128), two(x_inv))
-    v = exchange(v.reshape(64, 9, 2, 128), GX + ("ph",))
+    v = call(mix_kernel, (192, 128), v.reshape(192, 128), weight.transpose(0, 2, 1, 3), expand, scratch=scratch)
+
+    v = exchange(v.reshape(32, 3, 2, 128), ("zz", "yl"))
+    v = call(x_back_kernel, (1152, 128), v.reshape(192, 128), two(x_inv))
+    v = exchange(v.reshape(64, 9, 2, 128), ("ph", "zz", "yl"))
     v = v.reshape(1152, 128)
     v, linear_1 = call(y_back_kernel, [(8, 6, 2, 2, 16, 128), mixed], v, two(y_inv), *mixing)
     v = exchange(v.reshape(8, 12, 2, 16, 128), ("core", "px"))

time: 148 us -> 148 us (level)
  no operation moved by 1% of the time
where the time goes in v8:
time: 148 us
  blocking collectives  135 us (91%)
  Pallas kernels  11.7 us (8%)
    all_to_all x6, blocking collectives, exchange(): return lax.all_to_all(v, axes, 0, 0, tiled=True)  135 us
    pallas_call x7, Pallas kernels, call(): pl.pallas_call(kernel, out_shape=[jax.ShapeDtypeStruct(dims, F32) for dim...  11.7 us

profile of v8, /device:TPU:1, one launch (start us, length us, event | category | flops | bytes accessed | tf_op | source)
XLA Modules:
  0.0 147.5 jit_solution(9986358204627254345)
XLA Ops:
  0.0 2.7 %shard_map.100 = f32[96,2,16,128]{3,2,1,0:T(8,128)S(1)} custom-call(f32[32,8,16,128]{3,2,1,0:T(8,128)} %field.1), custom_call_target="tpu_custom_call" | custom-call | tf_op jit(solution)/shard_map/pallas_call | solution.py:318
  2.7 0.0 copy-start
  2.7 0.0 copy-start.3
  2.7 0.0 copy-start.7
  2.7 0.0 copy-start.9
  2.7 30.0 %all_to_all.30 = f32[8,12,2,16,128]{4,3,2,1,0:T(8,128)S(1)} all-to-all(f32[8,12,2,16,128]{4,3,2,1,0:T(8,128)S(1)} %bitcast.17), channel_id=1, replica_groups=mesh['yl'=4,'zz'=8,'px'=4,'ph'=2,'core'=2] {'core','px'}, dimensions={0} | all-to-all | bytes 3145728 | tf_op jit(solution)/shard_map/all_to_all | solution.py:330
  32.8 0.0 copy-done
  32.8 0.0 copy-start.5
  32.8 0.0 copy-start.1
  32.8 0.0 copy-start.8
  32.8 0.8 shard_map.101
  33.6 0.0 copy-start.4
  33.6 29.0 %all_to_all.31 = f32[64,9,2,128]{3,2,1,0:T(2,128)S(1)} all-to-all(f32[64,9,2,128]{3,2,1,0:T(2,128)S(1)} %bitcast.24), channel_id=1, replica_groups=mesh['yl'=4,'zz'=8,'px'=4,'ph'=2,'core'=2] {'ph','zz','yl'}, dimensions={0} | all-to-all | bytes 1179648 | tf_op jit(solution)/shard_map/all_to_all | solution.py:330
  62.6 0.4 shard_map.102
  63.0 15.9 %all_to_all.32 = f32[32,3,2,128]{3,2,1,0:T(2,128)S(1)} all-to-all(f32[32,3,2,128]{3,2,1,0:T(2,128)S(1)} %bitcast.25), channel_id=1, replica_groups=mesh['yl'=4,'zz'=8,'px'=4,'ph'=2,'core'=2] {'zz','yl'}, dimensions={0} | all-to-all | bytes 196608 | tf_op jit(solution)/shard_map/all_to_all | solution.py:330
  78.9 0.0 copy-done.8
  78.9 1.1 shard_map.103
  80.1 12.6 %all_to_all.33 = f32[32,3,2,128]{3,2,1,0:T(2,128)S(1)} all-to-all(f32[32,3,2,128]{3,2,1,0:T(2,128)S(1)} %bitcast.27), channel_id=1, replica_groups=mesh['yl'=4,'zz'=8,'px'=4,'ph'=2,'core'=2] {'zz','yl'}, dimensions={0} | all-to-all | bytes 196608 | tf_op jit(solution)/shard_map/all_to_all | solution.py:330
  92.6 0.4 shard_map.104
  93.1 20.5 %all_to_all.34 = f32[64,9,2,128]{3,2,1,0:T(2,128)S(1)} all-to-all(f32[64,9,2,128]{3,2,1,0:T(2,128)S(1)} %bitcast.21), channel_id=1, replica_groups=mesh['yl'=4,'zz'=8,'px'=4,'ph'=2,'core'=2] {'ph','zz','yl'}, dimensions={0} | all-to-all | bytes 1179648 | tf_op jit(solution)/shard_map/all_to_all | solution.py:330
  113.6 3.6 %shard_map.105 = (f32[8,6,2,2,16,128]{5,4,3,2,1,0:T(8,128)S(1)}, f32[16,2,128,128]{3,2,1,0:T(8,128)S(1)}) custom-call(f32[1152,128]{1,0:T(8,128)S(1)} %bitcast.19, bf16[2,2,256,128]{3,2,1,0:T(8,128)(2,1)S(1)} %copy-done.2, f32[4096,128]{1,0:T(8,128)S(1)} %bitcast.15, f32[32,32]{1,0:T(8,128)S(1)} %copy-done.7, f32[32]{0:T(128)S(1)} %copy-done.9), custom_call_target="tpu_custom_call" | custom-call | tf_op jit(solution)/shard_map/pallas_call | solution.py:318
  117.2 0.0 copy-start.6
  117.2 27.4 %all_to_all.35 = f32[8,12,2,16,128]{4,3,2,1,0:T(8,128)S(1)} all-to-all(f32[8,12,2,16,128]{4,3,2,1,0:T(8,128)S(1)} %bitcast.22), channel_id=1, replica_groups=mesh['yl'=4,'zz'=8,'px'=4,'ph'=2,'core'=2] {'core','px'}, dimensions={0} | all-to-all | bytes 3145728 | tf_op jit(solution)/shard_map/all_to_all | solution.py:330
  144.7 2.7 %shard_map.106 = f32[32,8,16,128]{3,2,1,0:T(8,128)} custom-call(f32[96,2,16,128]{3,2,1,0:T(8,128)S(1)} %bitcast.18, f32[16,2,128,128]{3,2,1,0:T(8,128)S(1)} %get-tuple-element.11.linear_0, f32[16,2,128,128]{3,2,1,0:T(8,128)S(1)} %get-tuple-element.12.linear_1, bf16[192,256]{1,0:T(8,128)(2,1)S(1)} %copy-done.6), custom_call_target="tpu_custom_call" | custom-call | tf_op jit(solution)/shard_map/pallas_call | solution.py:318
  (9 shorter events, 0.0 us)
Async XLA Ops:
  2.7 30.1 %copy-start = (f32[32,8,16,128]{3,2,1,0:T(8,128)S(1)}, f32[32,8,16,128]{3,2,1,0:T(8,128)}, u32[]{:S(2)}) copy-start(f32[32,8,16,128]{3,2,1,0:T(8,128)} %field.1) | copy-start | bytes 6291460
  2.7 30.1 %copy-start.3 = (bf16[2,2,128,256]{3,2,1,0:T(8,128)(2,1)S(1)}, bf16[2,2,128,256]{3,2,1,0:T(8,128)(2,1)}, u32[]{:S(2)}) copy-start(bf16[2,2,128,256]{3,2,1,0:T(8,128)(2,1)} %constant.12.clone.table) | copy-start | bytes 786436
  2.7 30.1 %copy-start.7 = (f32[32,32]{1,0:T(8,128)S(1)}, f32[32,32]{1,0:T(8,128)}, u32[]{:S(2)}) copy-start(f32[32,32]{1,0:T(8,128)} %weight.3) | copy-start | bytes 12292
  2.7 30.1 %copy-start.9 = (f32[32]{0:T(128)S(1)}, f32[32]{0:T(128)}, u32[]{:S(2)}) copy-start(f32[32]{0:T(128)} %bias.3) | copy-start | bytes 388
  32.8 29.8 %copy-start.5 = (bf16[2,128,256]{2,1,0:T(8,128)(2,1)S(1)}, bf16[2,128,256]{2,1,0:T(8,128)(2,1)}, u32[]{:S(2)}) copy-start(bf16[2,128,256]{2,1,0:T(8,128)(2,1)} %constant.13.clone.table) | copy-start | bytes 393220
  32.8 46.1 %copy-start.1 = (bf16[2,72,3,1024]{3,1,2,0:T(8,128)(2,1)S(1)}, bf16[2,72,3,1024]{3,1,2,0:T(8,128)(2,1)}, u32[]{:S(2)}) copy-start(bf16[2,72,3,1024]{3,1,2,0:T(8,128)(2,1)} %param.11) | copy-start | bytes 2654212
  32.8 46.1 %copy-start.8 = (bf16[32,1024]{1,0:T(8,128)(2,1)S(1)}, bf16[32,1024]{1,0:T(8,128)(2,1)}, u32[]{:S(2)}) copy-start(bf16[32,1024]{1,0:T(8,128)(2,1)} %constant.14.clone.expand) | copy-start | bytes 196612
  33.6 59.0 %copy-start.4 = (bf16[2,256,128]{2,1,0:T(8,128)(2,1)S(1)}, bf16[2,256,128]{2,1,0:T(8,128)(2,1)}, u32[]{:S(2)}) copy-start(bf16[2,256,128]{2,1,0:T(8,128)(2,1)} %constant.15.clone.table) | copy-start | bytes 393220
  62.6 51.0 %copy-start.2 = (bf16[2,2,256,128]{3,2,1,0:T(8,128)(2,1)S(1)}, bf16[2,2,256,128]{3,2,1,0:T(8,128)(2,1)}, u32[]{:S(2)}) copy-start(bf16[2,2,256,128]{3,2,1,0:T(8,128)(2,1)} %constant.16.clone.table) | copy-start | bytes 786436
  117.2 27.5 %copy-start.6 = (bf16[192,256]{1,0:T(8,128)(2,1)S(1)}, bf16[192,256]{1,0:T(8,128)(2,1)}, u32[]{:S(2)}) copy-start(bf16[192,256]{1,0:T(8,128)(2,1)} %constant.17.clone.table) | copy-start | bytes 294916

commit v9 on v8

--- a/solution.py
+++ b/solution.py
@@ -91,10 +91,6 @@
 
 
 NT = ((1,), (1,))
-
-
-def lines_at(ref, y):
-    return jnp.concatenate([ref[pl.ds(x * 16 + y, 32, stride=128), :] for x in range(8)], axis=0)
 
 
 CHUNKS = [(h, slice(4 * h, 4 * h + 4), slice(8 * i, 8 * i + 8)) for h in range(2) for i in range(2)]
@@ -143,8 +139,13 @@
     w = split(jnp.where(row == col, w, 0.0).T)
     b = jnp.broadcast_to(bias[...].reshape(1, 32), (NZ, 32)).T
     b = jnp.concatenate([b] * 8, axis=0)
-    for y in range(16):
-        linear[y] = (dot3(w, split(lines_at(field, y))) + b).reshape(2, 128, 128)
+    for i in range(2):
+        by_y = [jnp.swapaxes(field[:, x, 8 * i : 8 * i + 8, :], 0, 1) for x in range(8)]
+        for y in range(8):
+            hi, lo = split(jnp.concatenate([v[y] for v in by_y], axis=0))
+            r = dot(w[0], jnp.concatenate([hi, lo], axis=1))
+            r = r[:, :NZ] + r[:, NZ:] + dot(w[1], hi) + b
+            linear[8 * i + y] = r.reshape(2, 128, 128)
 
 
 def y_kernel(rows, table, field, weight, bias, out, linear):
@@ -339,8 +340,7 @@
     scratch = [block, pltpu.SemaphoreType.DMA((2,))]
     v = call(z_kernel, (96, 2, 16, 128), field, ins=ANY, scratch=scratch, limit=52)
     v = exchange(v.reshape(8, 12, 2, 16, 128), ("core", "px"))
-    lines = field.reshape(C * 8 * 16, NZ)
-    mixing = (lines, point_weight, point_bias)
+    mixing = (field, point_weight, point_bias)
     mixed = (16, 2, 128, 128)
     v = v.reshape(8, 6, 2, 2, 16, 128)
     v, linear_0 = call(y_kernel, [(1152, 128), mixed], v, two(y_fwd), *mixing)

time: 148 us -> 148 us (level)
  blocking collectives: 135 us -> 137 us
    all_to_all x6, blocking collectives: 135 us -> 137 us  [exchange(): return lax.all_to_all(v, axes, 0, 0, tiled=True)]
where the time goes in v9:
time: 148 us
  blocking collectives  137 us (93%)
  Pallas kernels  10.5 us (7%)
    all_to_all x6, blocking collectives, exchange(): return lax.all_to_all(v, axes, 0, 0, tiled=True)  137 us
    pallas_call x7, Pallas kernels, call(): pl.pallas_call(kernel, out_shape=[jax.ShapeDtypeStruct(dims, F32) for dim...  10.5 us

profile of v9, /device:TPU:1, one launch (start us, length us, event | category | flops | bytes accessed | tf_op | source)
XLA Modules:
  0.0 147.7 jit_solution(8833608848371594831)
XLA Ops:
  0.0 2.7 %shard_map.100 = f32[96,2,16,128]{3,2,1,0:T(8,128)S(1)} custom-call(f32[32,8,16,128]{3,2,1,0:T(8,128)} %field.5), custom_call_target="tpu_custom_call" | custom-call | tf_op jit(solution)/shard_map/pallas_call | solution.py:319
  2.7 0.0 copy-start
  2.7 0.0 copy-start.3
  2.7 0.0 copy-start.7
  2.7 0.0 copy-start.9
  2.7 30.0 %all_to_all.30 = f32[8,12,2,16,128]{4,3,2,1,0:T(8,128)S(1)} all-to-all(f32[8,12,2,16,128]{4,3,2,1,0:T(8,128)S(1)} %bitcast.14), channel_id=1, replica_groups=mesh['yl'=4,'zz'=8,'px'=4,'ph'=2,'core'=2] {'core','px'}, dimensions={0} | all-to-all | bytes 3145728 | tf_op jit(solution)/shard_map/all_to_all | solution.py:331
  32.8 0.0 copy-done.3
  32.8 0.0 copy-start.5
  32.8 0.0 copy-start.1
  32.8 0.0 copy-start.8
  32.8 0.8 shard_map.101
  33.6 0.0 copy-start.4
  33.6 30.3 %all_to_all.31 = f32[64,9,2,128]{3,2,1,0:T(2,128)S(1)} all-to-all(f32[64,9,2,128]{3,2,1,0:T(2,128)S(1)} %bitcast.21), channel_id=1, replica_groups=mesh['yl'=4,'zz'=8,'px'=4,'ph'=2,'core'=2] {'ph','zz','yl'}, dimensions={0} | all-to-all | bytes 1179648 | tf_op jit(solution)/shard_map/all_to_all | solution.py:331
  64.0 0.4 shard_map.102
  64.4 15.1 %all_to_all.32 = f32[32,3,2,128]{3,2,1,0:T(2,128)S(1)} all-to-all(f32[32,3,2,128]{3,2,1,0:T(2,128)S(1)} %bitcast.22), channel_id=1, replica_groups=mesh['yl'=4,'zz'=8,'px'=4,'ph'=2,'core'=2] {'zz','yl'}, dimensions={0} | all-to-all | bytes 196608 | tf_op jit(solution)/shard_map/all_to_all | solution.py:331
  79.4 1.1 shard_map.103
  80.6 12.6 %all_to_all.33 = f32[32,3,2,128]{3,2,1,0:T(2,128)S(1)} all-to-all(f32[32,3,2,128]{3,2,1,0:T(2,128)S(1)} %bitcast.24), channel_id=1, replica_groups=mesh['yl'=4,'zz'=8,'px'=4,'ph'=2,'core'=2] {'zz','yl'}, dimensions={0} | all-to-all | bytes 196608 | tf_op jit(solution)/shard_map/all_to_all | solution.py:331
  93.1 0.0 copy-done.4
  93.1 0.4 shard_map.104
  93.6 20.9 %all_to_all.34 = f32[64,9,2,128]{3,2,1,0:T(2,128)S(1)} all-to-all(f32[64,9,2,128]{3,2,1,0:T(2,128)S(1)} %bitcast.18), channel_id=1, replica_groups=mesh['yl'=4,'zz'=8,'px'=4,'ph'=2,'core'=2] {'ph','zz','yl'}, dimensions={0} | all-to-all | bytes 1179648 | tf_op jit(solution)/shard_map/all_to_all | solution.py:331
  114.4 2.4 %shard_map.105 = (f32[8,6,2,2,16,128]{5,4,3,2,1,0:T(8,128)S(1)}, f32[16,2,128,128]{3,2,1,0:T(8,128)S(1)}) custom-call(f32[1152,128]{1,0:T(8,128)S(1)} %bitcast.16, bf16[2,2,256,128]{3,2,1,0:T(8,128)(2,1)S(1)} %copy-done.2, f32[32,8,16,128]{3,2,1,0:T(8,128)S(1)} %copy-done, f32[32,32]{1,0:T(8,128)S(1)} %copy-done.7, f32[32]{0:T(128)S(1)} %copy-done.9), custom_call_target="tpu_custom_call" | custom-call | tf_op jit(solution)/shard_map/pallas_call | solution.py:319
  116.8 0.0 copy-start.6
  116.8 28.2 %all_to_all.35 = f32[8,12,2,16,128]{4,3,2,1,0:T(8,128)S(1)} all-to-all(f32[8,12,2,16,128]{4,3,2,1,0:T(8,128)S(1)} %bitcast.19), channel_id=1, replica_groups=mesh['yl'=4,'zz'=8,'px'=4,'ph'=2,'core'=2] {'core','px'}, dimensions={0} | all-to-all | bytes 3145728 | tf_op jit(solution)/shard_map/all_to_all | solution.py:331
  145.1 2.7 %shard_map.106 = f32[32,8,16,128]{3,2,1,0:T(8,128)} custom-call(f32[96,2,16,128]{3,2,1,0:T(8,128)S(1)} %bitcast.15, f32[16,2,128,128]{3,2,1,0:T(8,128)S(1)} %get-tuple-element.11.linear_0, f32[16,2,128,128]{3,2,1,0:T(8,128)S(1)} %get-tuple-element.12.linear_1, bf16[192,256]{1,0:T(8,128)(2,1)S(1)} %copy-done.6), custom_call_target="tpu_custom_call" | custom-call | tf_op jit(solution)/shard_map/pallas_call | solution.py:319
  (9 shorter events, 0.0 us)
Async XLA Ops:
  2.7 30.1 %copy-start = (f32[32,8,16,128]{3,2,1,0:T(8,128)S(1)}, f32[32,8,16,128]{3,2,1,0:T(8,128)}, u32[]{:S(2)}) copy-start(f32[32,8,16,128]{3,2,1,0:T(8,128)} %field.5) | copy-start | bytes 6291460
  2.7 30.1 %copy-start.3 = (bf16[2,2,128,256]{3,2,1,0:T(8,128)(2,1)S(1)}, bf16[2,2,128,256]{3,2,1,0:T(8,128)(2,1)}, u32[]{:S(2)}) copy-start(bf16[2,2,128,256]{3,2,1,0:T(8,128)(2,1)} %constant.12.clone.table) | copy-start | bytes 786436
  2.7 30.1 %copy-start.7 = (f32[32,32]{1,0:T(8,128)S(1)}, f32[32,32]{1,0:T(8,128)}, u32[]{:S(2)}) copy-start(f32[32,32]{1,0:T(8,128)} %weight.3) | copy-start | bytes 12292
  2.7 30.1 %copy-start.9 = (f32[32]{0:T(128)S(1)}, f32[32]{0:T(128)}, u32[]{:S(2)}) copy-start(f32[32]{0:T(128)} %bias.3) | copy-start | bytes 388
  32.8 31.2 %copy-start.5 = (bf16[2,128,256]{2,1,0:T(8,128)(2,1)S(1)}, bf16[2,128,256]{2,1,0:T(8,128)(2,1)}, u32[]{:S(2)}) copy-start(bf16[2,128,256]{2,1,0:T(8,128)(2,1)} %constant.13.clone.table) | copy-start | bytes 393220
  32.8 46.6 %copy-start.1 = (bf16[2,72,3,1024]{3,1,2,0:T(8,128)(2,1)S(1)}, bf16[2,72,3,1024]{3,1,2,0:T(8,128)(2,1)}, u32[]{:S(2)}) copy-start(bf16[2,72,3,1024]{3,1,2,0:T(8,128)(2,1)} %param.11) | copy-start | bytes 2654212
  32.8 46.6 %copy-start.8 = (bf16[32,1024]{1,0:T(8,128)(2,1)S(1)}, bf16[32,1024]{1,0:T(8,128)(2,1)}, u32[]{:S(2)}) copy-start(bf16[32,1024]{1,0:T(8,128)(2,1)} %constant.14.clone.expand) | copy-start | bytes 196612
  33.6 59.5 %copy-start.4 = (bf16[2,256,128]{2,1,0:T(8,128)(2,1)S(1)}, bf16[2,256,128]{2,1,0:T(8,128)(2,1)}, u32[]{:S(2)}) copy-start(bf16[2,256,128]{2,1,0:T(8,128)(2,1)} %constant.15.clone.table) | copy-start | bytes 393220
  64.0 50.4 %copy-start.2 = (bf16[2,2,256,128]{3,2,1,0:T(8,128)(2,1)S(1)}, bf16[2,2,256,128]{3,2,1,0:T(8,128)(2,1)}, u32[]{:S(2)}) copy-start(bf16[2,2,256,128]{3,2,1,0:T(8,128)(2,1)} %constant.16.clone.table) | copy-start | bytes 786436
  116.8 28.3 %copy-start.6 = (bf16[192,256]{1,0:T(8,128)(2,1)S(1)}, bf16[192,256]{1,0:T(8,128)(2,1)}, u32[]{:S(2)}) copy-start(bf16[192,256]{1,0:T(8,128)(2,1)} %constant.17.clone.table) | copy-start | bytes 294916

commit v10 on v8

--- a/solution.py
+++ b/solution.py
@@ -63,7 +63,7 @@
 
 
 def x_rows():
-    gx = GX_OF
+    gx = np.arange(32)
     first = 3 * (gx // 2) + gx % 2
     return np.stack([first, first + 1])
 
@@ -240,7 +240,8 @@
                 else:
                     v += [ref[2, a * 48 + 32 : a * 48 + 48, :], pad]
             v = jnp.concatenate(v, axis=0).T
-            out[pl.ds(2 * k + a, 32, stride=6), :] = v
+            for zz in range(8):
+                out[pl.ds(6 * zz + 2 * k + a, 4, stride=48), :] = v[4 * zz : 4 * zz + 4]
 
 
 def x_back_kernel(modes, table, out):
@@ -347,13 +348,13 @@
     v = exchange(v.reshape(64, 9, 2, 128), ("ph", "zz", "yl"))
     v = call(x_kernel, (192, 128), v.reshape(1152, 128), two(x_fwd))
 
-    v = exchange(v.reshape(32, 3, 2, 128), ("zz", "yl"))
-
-    expand = np.kron(np.eye(C), np.ones((1, C))).astype(ml_dtypes.bfloat16)
+    v = exchange(v.reshape(32, 3, 2, 128), GX)
+
+    expand = np.kron(np.eye(C)[np.argsort(GX_OF)], np.ones((1, C))).astype(ml_dtypes.bfloat16)
     scratch = [pltpu.VMEM((3, 96, 32), F32) for _ in range(4)]
     v = call(mix_kernel, (192, 128), v.reshape(192, 128), weight.transpose(0, 2, 1, 3), expand, scratch=scratch)
 
-    v = exchange(v.reshape(32, 3, 2, 128), ("zz", "yl"))
+    v = exchange(v.reshape(32, 3, 2, 128), GX)
     v = call(x_back_kernel, (1152, 128), v.reshape(192, 128), two(x_inv))
     v = exchange(v.reshape(64, 9, 2, 128), ("ph", "zz", "yl"))
     v = v.reshape(1152, 128)

time: 148 us -> 147 us (level)
  no operation moved by 1% of the time
where the time goes in v10:
time: 147 us
  blocking collectives  135 us (92%)
  Pallas kernels  11.7 us (8%)
    all_to_all x6, blocking collectives, exchange(): return lax.all_to_all(v, axes, 0, 0, tiled=True)  135 us
    pallas_call x7, Pallas kernels, call(): pl.pallas_call(kernel, out_shape=[jax.ShapeDtypeStruct(dims, F32) for dim...  11.7 us

profile of v10, /device:TPU:1, one launch (start us, length us, event | category | flops | bytes accessed | tf_op | source)
XLA Modules:
  0.0 147.1 jit_solution(6296670946498462647)
XLA Ops:
  0.0 2.7 %shard_map.100 = f32[96,2,16,128]{3,2,1,0:T(8,128)S(1)} custom-call(f32[32,8,16,128]{3,2,1,0:T(8,128)} %field.1), custom_call_target="tpu_custom_call" | custom-call | tf_op jit(solution)/shard_map/pallas_call | solution.py:319
  2.7 0.0 copy-start
  2.7 0.0 copy-start.3
  2.7 0.0 copy-start.7
  2.7 0.0 copy-start.9
  2.7 30.0 %all_to_all.30 = f32[8,12,2,16,128]{4,3,2,1,0:T(8,128)S(1)} all-to-all(f32[8,12,2,16,128]{4,3,2,1,0:T(8,128)S(1)} %bitcast.17), channel_id=1, replica_groups=mesh['yl'=4,'zz'=8,'px'=4,'ph'=2,'core'=2] {'core','px'}, dimensions={0} | all-to-all | bytes 3145728 | tf_op jit(solution)/shard_map/all_to_all | solution.py:331
  32.8 0.0 copy-done
  32.8 0.0 copy-done.7
  32.8 0.0 copy-start.5
  32.8 0.0 copy-start.1
  32.8 0.0 copy-start.8
  32.8 0.8 shard_map.101
  33.6 0.0 copy-start.4
  33.6 29.0 %all_to_all.31 = f32[64,9,2,128]{3,2,1,0:T(2,128)S(1)} all-to-all(f32[64,9,2,128]{3,2,1,0:T(2,128)S(1)} %bitcast.24), channel_id=1, replica_groups=mesh['yl'=4,'zz'=8,'px'=4,'ph'=2,'core'=2] {'ph','zz','yl'}, dimensions={0} | all-to-all | bytes 1179648 | tf_op jit(solution)/shard_map/all_to_all | solution.py:331
  62.6 0.4 shard_map.102
  63.0 15.7 %all_to_all.32 = f32[32,3,2,128]{3,2,1,0:T(2,128)S(1)} all-to-all(f32[32,3,2,128]{3,2,1,0:T(2,128)S(1)} %bitcast.25), channel_id=1, replica_groups=mesh['yl'=4,'zz'=8,'px'=4,'ph'=2,'core'=2] {'yl','zz'}, dimensions={0} | all-to-all | bytes 196608 | tf_op jit(solution)/shard_map/all_to_all | solution.py:331
  78.7 1.1 shard_map.103
  79.8 12.2 %all_to_all.33 = f32[32,3,2,128]{3,2,1,0:T(2,128)S(1)} all-to-all(f32[32,3,2,128]{3,2,1,0:T(2,128)S(1)} %bitcast.27), channel_id=1, replica_groups=mesh['yl'=4,'zz'=8,'px'=4,'ph'=2,'core'=2] {'yl','zz'}, dimensions={0} | all-to-all | bytes 196608 | tf_op jit(solution)/shard_map/all_to_all | solution.py:331
  92.0 0.4 shard_map.104
  92.5 20.7 %all_to_all.34 = f32[64,9,2,128]{3,2,1,0:T(2,128)S(1)} all-to-all(f32[64,9,2,128]{3,2,1,0:T(2,128)S(1)} %bitcast.21), channel_id=1, replica_groups=mesh['yl'=4,'zz'=8,'px'=4,'ph'=2,'core'=2] {'ph','zz','yl'}, dimensions={0} | all-to-all | bytes 1179648 | tf_op jit(solution)/shard_map/all_to_all | solution.py:331
  113.2 3.6 %shard_map.105 = (f32[8,6,2,2,16,128]{5,4,3,2,1,0:T(8,128)S(1)}, f32[16,2,128,128]{3,2,1,0:T(8,128)S(1)}) custom-call(f32[1152,128]{1,0:T(8,128)S(1)} %bitcast.19, bf16[2,2,256,128]{3,2,1,0:T(8,128)(2,1)S(1)} %copy-done.2, f32[4096,128]{1,0:T(8,128)S(1)} %bitcast.15, f32[32,32]{1,0:T(8,128)S(1)} %copy-done.7, f32[32]{0:T(128)S(1)} %copy-done.9), custom_call_target="tpu_custom_call" | custom-call | tf_op jit(solution)/shard_map/pallas_call | solution.py:319
  116.8 0.0 copy-start.6
  116.8 27.4 %all_to_all.35 = f32[8,12,2,16,128]{4,3,2,1,0:T(8,128)S(1)} all-to-all(f32[8,12,2,16,128]{4,3,2,1,0:T(8,128)S(1)} %bitcast.22), channel_id=1, replica_groups=mesh['yl'=4,'zz'=8,'px'=4,'ph'=2,'core'=2] {'core','px'}, dimensions={0} | all-to-all | bytes 3145728 | tf_op jit(solution)/shard_map/all_to_all | solution.py:331
  144.3 2.7 %shard_map.106 = f32[32,8,16,128]{3,2,1,0:T(8,128)} custom-call(f32[96,2,16,128]{3,2,1,0:T(8,128)S(1)} %bitcast.18, f32[16,2,128,128]{3,2,1,0:T(8,128)S(1)} %get-tuple-element.11.linear_0, f32[16,2,128,128]{3,2,1,0:T(8,128)S(1)} %get-tuple-element.12.linear_1, bf16[192,256]{1,0:T(8,128)(2,1)S(1)} %copy-done.6), custom_call_target="tpu_custom_call" | custom-call | tf_op jit(solution)/shard_map/pallas_call | solution.py:319
  (9 shorter events, 0.0 us)
Async XLA Ops:
  2.7 30.1 %copy-start = (f32[32,8,16,128]{3,2,1,0:T(8,128)S(1)}, f32[32,8,16,128]{3,2,1,0:T(8,128)}, u32[]{:S(2)}) copy-start(f32[32,8,16,128]{3,2,1,0:T(8,128)} %field.1) | copy-start | bytes 6291460
  2.7 30.1 %copy-start.3 = (bf16[2,2,128,256]{3,2,1,0:T(8,128)(2,1)S(1)}, bf16[2,2,128,256]{3,2,1,0:T(8,128)(2,1)}, u32[]{:S(2)}) copy-start(bf16[2,2,128,256]{3,2,1,0:T(8,128)(2,1)} %constant.12.clone.table) | copy-start | bytes 786436
  2.7 30.1 %copy-start.7 = (f32[32,32]{1,0:T(8,128)S(1)}, f32[32,32]{1,0:T(8,128)}, u32[]{:S(2)}) copy-start(f32[32,32]{1,0:T(8,128)} %weight.3) | copy-start | bytes 12292
  2.7 30.1 %copy-start.9 = (f32[32]{0:T(128)S(1)}, f32[32]{0:T(128)}, u32[]{:S(2)}) copy-start(f32[32]{0:T(128)} %bias.3) | copy-start | bytes 388
  32.8 29.8 %copy-start.5 = (bf16[2,128,256]{2,1,0:T(8,128)(2,1)S(1)}, bf16[2,128,256]{2,1,0:T(8,128)(2,1)}, u32[]{:S(2)}) copy-start(bf16[2,128,256]{2,1,0:T(8,128)(2,1)} %constant.13.clone.table) | copy-start | bytes 393220
  32.8 45.9 %copy-start.1 = (bf16[2,72,3,1024]{3,1,2,0:T(8,128)(2,1)S(1)}, bf16[2,72,3,1024]{3,1,2,0:T(8,128)(2,1)}, u32[]{:S(2)}) copy-start(bf16[2,72,3,1024]{3,1,2,0:T(8,128)(2,1)} %param.11) | copy-start | bytes 2654212
  32.8 45.9 %copy-start.8 = (bf16[32,1024]{1,0:T(8,128)(2,1)S(1)}, bf16[32,1024]{1,0:T(8,128)(2,1)}, u32[]{:S(2)}) copy-start(bf16[32,1024]{1,0:T(8,128)(2,1)} %constant.14.clone.expand) | copy-start | bytes 196612
  33.6 58.4 %copy-start.4 = (bf16[2,256,128]{2,1,0:T(8,128)(2,1)S(1)}, bf16[2,256,128]{2,1,0:T(8,128)(2,1)}, u32[]{:S(2)}) copy-start(bf16[2,256,128]{2,1,0:T(8,128)(2,1)} %constant.15.clone.table) | copy-start | bytes 393220
  62.6 50.6 %copy-start.2 = (bf16[2,2,256,128]{3,2,1,0:T(8,128)(2,1)S(1)}, bf16[2,2,256,128]{3,2,1,0:T(8,128)(2,1)}, u32[]{:S(2)}) copy-start(bf16[2,2,256,128]{3,2,1,0:T(8,128)(2,1)} %constant.16.clone.table) | copy-start | bytes 786436
  116.8 27.5 %copy-start.6 = (bf16[192,256]{1,0:T(8,128)(2,1)S(1)}, bf16[192,256]{1,0:T(8,128)(2,1)}, u32[]{:S(2)}) copy-start(bf16[192,256]{1,0:T(8,128)(2,1)} %constant.17.clone.table) | copy-start | bytes 294916

commit v11 on v9

--- a/solution.py
+++ b/solution.py
@@ -63,7 +63,7 @@
 
 
 def x_rows():
-    gx = GX_OF
+    gx = np.arange(32)
     first = 3 * (gx // 2) + gx % 2
     return np.stack([first, first + 1])
 
@@ -241,7 +241,8 @@
                 else:
                     v += [ref[2, a * 48 + 32 : a * 48 + 48, :], pad]
             v = jnp.concatenate(v, axis=0).T
-            out[pl.ds(2 * k + a, 32, stride=6), :] = v
+            for zz in range(8):
+                out[pl.ds(6 * zz + 2 * k + a, 4, stride=48), :] = v[4 * zz : 4 * zz + 4]
 
 
 def x_back_kernel(modes, table, out):
@@ -347,13 +348,13 @@
     v = exchange(v.reshape(64, 9, 2, 128), ("ph", "zz", "yl"))
     v = call(x_kernel, (192, 128), v.reshape(1152, 128), two(x_fwd))
 
-    v = exchange(v.reshape(32, 3, 2, 128), ("zz", "yl"))
-
-    expand = np.kron(np.eye(C), np.ones((1, C))).astype(ml_dtypes.bfloat16)
+    v = exchange(v.reshape(32, 3, 2, 128), GX)
+
+    expand = np.kron(np.eye(C)[np.argsort(GX_OF)], np.ones((1, C))).astype(ml_dtypes.bfloat16)
     scratch = [pltpu.VMEM((3, 96, 32), F32) for _ in range(4)]
     v = call(mix_kernel, (192, 128), v.reshape(192, 128), weight.transpose(0, 2, 1, 3), expand, scratch=scratch)
 
-    v = exchange(v.reshape(32, 3, 2, 128), ("zz", "yl"))
+    v = exchange(v.reshape(32, 3, 2, 128), GX)
     v = call(x_back_kernel, (1152, 128), v.reshape(192, 128), two(x_inv))
     v = exchange(v.reshape(64, 9, 2, 128), ("ph", "zz", "yl"))
     v = v.reshape(1152, 128)

time: 148 us -> 148 us (level)
  no operation moved by 1% of the time
where the time goes in v11:
time: 148 us
  blocking collectives  137 us (93%)
  Pallas kernels  10.5 us (7%)
    all_to_all x6, blocking collectives, exchange(): return lax.all_to_all(v, axes, 0, 0, tiled=True)  137 us
    pallas_call x7, Pallas kernels, call(): pl.pallas_call(kernel, out_shape=[jax.ShapeDtypeStruct(dims, F32) for dim...  10.5 us

profile of v11, /device:TPU:1, one launch (start us, length us, event | category | flops | bytes accessed | tf_op | source)
XLA Modules:
  0.0 147.6 jit_solution(8413790154028012307)
XLA Ops:
  0.0 2.7 %shard_map.100 = f32[96,2,16,128]{3,2,1,0:T(8,128)S(1)} custom-call(f32[32,8,16,128]{3,2,1,0:T(8,128)} %field.5), custom_call_target="tpu_custom_call" | custom-call | tf_op jit(solution)/shard_map/pallas_call | solution.py:320
  2.7 0.0 copy-start
  2.7 0.0 copy-start.3
  2.7 0.0 copy-start.7
  2.7 0.0 copy-start.9
  2.7 30.0 %all_to_all.30 = f32[8,12,2,16,128]{4,3,2,1,0:T(8,128)S(1)} all-to-all(f32[8,12,2,16,128]{4,3,2,1,0:T(8,128)S(1)} %bitcast.14), channel_id=1, replica_groups=mesh['yl'=4,'zz'=8,'px'=4,'ph'=2,'core'=2] {'core','px'}, dimensions={0} | all-to-all | bytes 3145728 | tf_op jit(solution)/shard_map/all_to_all | solution.py:332
  32.8 0.0 copy-done
  32.8 0.0 copy-start.5
  32.8 0.0 copy-start.1
  32.8 0.0 copy-start.8
  32.8 0.8 shard_map.101
  33.6 0.0 copy-start.4
  33.6 30.3 %all_to_all.31 = f32[64,9,2,128]{3,2,1,0:T(2,128)S(1)} all-to-all(f32[64,9,2,128]{3,2,1,0:T(2,128)S(1)} %bitcast.21), channel_id=1, replica_groups=mesh['yl'=4,'zz'=8,'px'=4,'ph'=2,'core'=2] {'ph','zz','yl'}, dimensions={0} | all-to-all | bytes 1179648 | tf_op jit(solution)/shard_map/all_to_all | solution.py:332
  64.0 0.0 copy-done.5
  64.0 0.4 shard_map.102
  64.4 14.7 %all_to_all.32 = f32[32,3,2,128]{3,2,1,0:T(2,128)S(1)} all-to-all(f32[32,3,2,128]{3,2,1,0:T(2,128)S(1)} %bitcast.22), channel_id=1, replica_groups=mesh['yl'=4,'zz'=8,'px'=4,'ph'=2,'core'=2] {'yl','zz'}, dimensions={0} | all-to-all | bytes 196608 | tf_op jit(solution)/shard_map/all_to_all | solution.py:332
  79.1 1.2 shard_map.103
  80.2 12.2 %all_to_all.33 = f32[32,3,2,128]{3,2,1,0:T(2,128)S(1)} all-to-all(f32[32,3,2,128]{3,2,1,0:T(2,128)S(1)} %bitcast.24), channel_id=1, replica_groups=mesh['yl'=4,'zz'=8,'px'=4,'ph'=2,'core'=2] {'yl','zz'}, dimensions={0} | all-to-all | bytes 196608 | tf_op jit(solution)/shard_map/all_to_all | solution.py:332
  92.5 0.4 shard_map.104
  92.9 21.4 %all_to_all.34 = f32[64,9,2,128]{3,2,1,0:T(2,128)S(1)} all-to-all(f32[64,9,2,128]{3,2,1,0:T(2,128)S(1)} %bitcast.18), channel_id=1, replica_groups=mesh['yl'=4,'zz'=8,'px'=4,'ph'=2,'core'=2] {'ph','zz','yl'}, dimensions={0} | all-to-all | bytes 1179648 | tf_op jit(solution)/shard_map/all_to_all | solution.py:332
  114.3 2.4 %shard_map.105 = (f32[8,6,2,2,16,128]{5,4,3,2,1,0:T(8,128)S(1)}, f32[16,2,128,128]{3,2,1,0:T(8,128)S(1)}) custom-call(f32[1152,128]{1,0:T(8,128)S(1)} %bitcast.16, bf16[2,2,256,128]{3,2,1,0:T(8,128)(2,1)S(1)} %copy-done.2, f32[32,8,16,128]{3,2,1,0:T(8,128)S(1)} %copy-done, f32[32,32]{1,0:T(8,128)S(1)} %copy-done.7, f32[32]{0:T(128)S(1)} %copy-done.9), custom_call_target="tpu_custom_call" | custom-call | tf_op jit(solution)/shard_map/pallas_call | solution.py:320
  116.6 0.0 copy-start.6
  116.7 28.2 %all_to_all.35 = f32[8,12,2,16,128]{4,3,2,1,0:T(8,128)S(1)} all-to-all(f32[8,12,2,16,128]{4,3,2,1,0:T(8,128)S(1)} %bitcast.19), channel_id=1, replica_groups=mesh['yl'=4,'zz'=8,'px'=4,'ph'=2,'core'=2] {'core','px'}, dimensions={0} | all-to-all | bytes 3145728 | tf_op jit(solution)/shard_map/all_to_all | solution.py:332
  144.9 2.7 %shard_map.106 = f32[32,8,16,128]{3,2,1,0:T(8,128)} custom-call(f32[96,2,16,128]{3,2,1,0:T(8,128)S(1)} %bitcast.15, f32[16,2,128,128]{3,2,1,0:T(8,128)S(1)} %get-tuple-element.11.linear_0, f32[16,2,128,128]{3,2,1,0:T(8,128)S(1)} %get-tuple-element.12.linear_1, bf16[192,256]{1,0:T(8,128)(2,1)S(1)} %copy-done.6), custom_call_target="tpu_custom_call" | custom-call | tf_op jit(solution)/shard_map/pallas_call | solution.py:320
  (9 shorter events, 0.0 us)
Async XLA Ops:
  2.7 30.1 %copy-start = (f32[32,8,16,128]{3,2,1,0:T(8,128)S(1)}, f32[32,8,16,128]{3,2,1,0:T(8,128)}, u32[]{:S(2)}) copy-start(f32[32,8,16,128]{3,2,1,0:T(8,128)} %field.5) | copy-start | bytes 6291460
  2.7 30.1 %copy-start.3 = (bf16[2,2,128,256]{3,2,1,0:T(8,128)(2,1)S(1)}, bf16[2,2,128,256]{3,2,1,0:T(8,128)(2,1)}, u32[]{:S(2)}) copy-start(bf16[2,2,128,256]{3,2,1,0:T(8,128)(2,1)} %constant.12.clone.table) | copy-start | bytes 786436
  2.7 30.1 %copy-start.7 = (f32[32,32]{1,0:T(8,128)S(1)}, f32[32,32]{1,0:T(8,128)}, u32[]{:S(2)}) copy-start(f32[32,32]{1,0:T(8,128)} %weight.3) | copy-start | bytes 12292
  2.7 30.1 %copy-start.9 = (f32[32]{0:T(128)S(1)}, f32[32]{0:T(128)}, u32[]{:S(2)}) copy-start(f32[32]{0:T(128)} %bias.3) | copy-start | bytes 388
  32.8 31.2 %copy-start.5 = (bf16[2,128,256]{2,1,0:T(8,128)(2,1)S(1)}, bf16[2,128,256]{2,1,0:T(8,128)(2,1)}, u32[]{:S(2)}) copy-start(bf16[2,128,256]{2,1,0:T(8,128)(2,1)} %constant.13.clone.table) | copy-start | bytes 393220
  32.8 46.3 %copy-start.1 = (bf16[2,72,3,1024]{3,1,2,0:T(8,128)(2,1)S(1)}, bf16[2,72,3,1024]{3,1,2,0:T(8,128)(2,1)}, u32[]{:S(2)}) copy-start(bf16[2,72,3,1024]{3,1,2,0:T(8,128)(2,1)} %param.11) | copy-start | bytes 2654212
  32.8 46.3 %copy-start.8 = (bf16[32,1024]{1,0:T(8,128)(2,1)S(1)}, bf16[32,1024]{1,0:T(8,128)(2,1)}, u32[]{:S(2)}) copy-start(bf16[32,1024]{1,0:T(8,128)(2,1)} %constant.14.clone.expand) | copy-start | bytes 196612
  33.6 58.8 %copy-start.4 = (bf16[2,256,128]{2,1,0:T(8,128)(2,1)S(1)}, bf16[2,256,128]{2,1,0:T(8,128)(2,1)}, u32[]{:S(2)}) copy-start(bf16[2,256,128]{2,1,0:T(8,128)(2,1)} %constant.15.clone.table) | copy-start | bytes 393220
  64.0 50.3 %copy-start.2 = (bf16[2,2,256,128]{3,2,1,0:T(8,128)(2,1)S(1)}, bf16[2,2,256,128]{3,2,1,0:T(8,128)(2,1)}, u32[]{:S(2)}) copy-start(bf16[2,2,256,128]{3,2,1,0:T(8,128)(2,1)} %constant.16.clone.table) | copy-start | bytes 786436
  116.6 28.2 %copy-start.6 = (bf16[192,256]{1,0:T(8,128)(2,1)S(1)}, bf16[192,256]{1,0:T(8,128)(2,1)}, u32[]{:S(2)}) copy-start(bf16[192,256]{1,0:T(8,128)(2,1)} %constant.17.clone.table) | copy-start | bytes 294916
